TPU v7x, 512 devices: a whole 4x4x16 slice. The times are simulated.
512 devices in a mesh: fsdp: 32 (over y, x, core), expert: 16 (over z).
Axes of the slice: x: 4, y: 4, z: 16, core: 2. Of those that a mesh axis runs over, the one named last changes fastest.
Arguments:
- grad: bfloat16 [16, 7168, 384], P('expert', 'fsdp')
- momentum: float32 [16, 7168, 384], P('expert', 'fsdp'), may hold values from -6 to 6
Outputs:
- new_momentum: float32 [16, 7168, 384], P('expert', 'fsdp')
- update: bfloat16 [16, 7168, 384], P('expert', 'fsdp')
All inputs are finite; a program needn't handle non-finite values.
Results may differ from a plain program's by a relative error of at most 0.012.
Values may be sent and summed in bfloat16 or wider, within the bound.
No kernel may reach another device: no remote copies, remote signals or barrier semaphores. Data moves between devices by JAX's collectives and lax.ppermute only.
A program may use at most 64 MiB of HBM per device.

v0:
```python
import math

import jax
import jax.numpy as jnp
from jax import lax
from jax.sharding import PartitionSpec as P

ITERS = 3


BETA = 0.95
COEF_A = 3.4445
COEF_B = -4.775
COEF_C = 2.0315


def orthogonal_factor(gram_matrix):
    order = gram_matrix.shape[0]
    identity = jnp.eye(order, dtype=jnp.float32)
    norm_inv = 1.0 / (jnp.sqrt(jnp.trace(gram_matrix)) + 1e-07)
    moment = gram_matrix * (norm_inv * norm_inv)
    factor = identity * norm_inv
    for iteration in range(ITERS):
        square = jnp.dot(moment, moment, precision=lax.Precision.HIGHEST)
        poly = COEF_A * identity + COEF_B * moment + COEF_C * square
        factor = jnp.dot(poly, factor, precision=lax.Precision.HIGHEST)
        moment = jnp.dot(
            jnp.dot(poly, moment, precision=lax.Precision.HIGHEST),
            poly,
            precision=lax.Precision.HIGHEST,
        )
    return factor.astype(jnp.bfloat16)


def per_device(grad, momentum):
    grad_full = grad.astype(jnp.float32)
    fsdp_count = lax.axis_size("fsdp")
    group_count = lax.axis_size("expert")
    total = lax.psum(jnp.sum(grad_full * grad_full), ("fsdp", "expert"))
    mean_square = total / (grad.size * fsdp_count * group_count)
    clip_factor = 1.0 / jnp.sqrt(mean_square + 1e-06)
    new_momentum = BETA * momentum + clip_factor * grad_full
    direction = (clip_factor * grad_full + BETA * new_momentum).astype(jnp.bfloat16)
    mat_count, width, row_count = direction.shape
    step_scale = 0.2 * math.sqrt(max(row_count, width * fsdp_count))
    owners = 0 // mat_count
    targets = jnp.arange(fsdp_count)
    send_buffer = jnp.zeros((fsdp_count, width, row_count), jnp.bfloat16)
    chosen = (targets == owners)[:, None, None]
    send_buffer = jnp.where(chosen, direction[0][None, :, :], send_buffer)
    whole = lax.all_to_all(
        send_buffer.reshape(fsdp_count * width, row_count),
        "fsdp",
        split_axis=0,
        concat_axis=0,
        tiled=True,
    )
    gram_matrix = jnp.einsum("cn,cm->nm", whole, whole, preferred_element_type=jnp.float32)
    factor = orthogonal_factor(gram_matrix)
    finished = (step_scale * jnp.dot(whole, factor.T, preferred_element_type=jnp.float32)).astype(
        jnp.bfloat16
    )
    returned = lax.all_to_all(finished, "fsdp", split_axis=0, concat_axis=0, tiled=True).reshape(
        fsdp_count, width, row_count
    )
    update = jnp.stack([returned[owners]])
    return (new_momentum, update)


def solution(mesh):
    placed = (P("expert", "fsdp", None), P("expert", "fsdp", None))
    return jax.shard_map(
        per_device,
        mesh=mesh,
        in_specs=placed,
        out_specs=(P("expert", "fsdp", None), P("expert", "fsdp", None)),
        check_vma=False,
    )
```

profile of v0, /device:TPU:1, one launch (start us, length us, event | category | flops | bytes accessed | tf_op | source)
XLA Modules:
  0.0 276.4 jit_solution(16115869292102485166)
XLA Ops:
  0.6 1.6 fusion.11
  2.2 111.0 %psum.7 = f32[]{:T(128)} all-reduce(f32[]{:T(128)} %fusion.11), channel_id=1, replica_groups=mesh['fsdp'=32,'expert'=16] {'fsdp','expert'}, use_global_device_ids=true, to_apply=%region_1.0 | all-reduce | flops 1 | bytes 8 | tf_op jit(solution)/shard_map/psum | solution.py:39
  114.0 1.9 fusion.16
  115.8 0.6 broadcast_select_fusion
  116.4 69.1 %all_to_all.18 = bf16[32,224,384]{2,1,0:T(8,128)(2,1)S(1)} all-to-all(bf16[32,224,384]{2,1,0:T(8,128)(2,1)S(1)} %broadcast_select_fusion), channel_id=1, replica_groups=mesh['fsdp'=32,'expert'=16] {'fsdp'}, dimensions={0} | all-to-all | bytes 11010048 | tf_op jit(solution)/shard_map/all_to_all | solution.py:51
  185.5 0.0 copy-start
  185.5 3.6 %select_reduce_fusion = (f32[]{:T(128)}, f32[384,384]{1,0:T(8,128)S(1)}) fusion(bf16[32,224,384]{2,1,0:T(8,128)(2,1)S(1)} %all_to_all.18), kind=kOutput, calls=%fused_computation.15 | convolution fusion | flops 2114371584 | bytes 6094852 | tf_op jit(solution)/shard_map/cn,cm->nm/dot_general | solution.py:58
  189.1 0.0 copy-done
  189.9 1.3 fusion
  191.2 0.0 slice-start
  191.2 1.3 fusion.6
  192.4 1.1 fusion.3
  193.5 1.3 fusion.19
  194.8 1.3 fusion.1
  196.1 0.0 slice-start.1
  196.1 1.3 fusion.20
  197.4 1.3 fusion.22
  198.6 1.4 fusion.21
  200.1 1.3 fusion.2
  201.4 1.3 convolution_convert_fusion
  202.7 0.0 slice-done
  202.7 0.0 slice-done.1
  202.7 3.8 %multiply_convert_fusion = bf16[7168,384]{1,0:T(8,128)(2,1)S(1)} fusion(bf16[7168,384]{1,0:T(8,128)(2,1)S(1)} %bitcast.28, bf16[384,384]{1,0:T(8,128)(2,1)S(1)} %convolution_convert_fusion), kind=kOutput, calls=%fused_computation | convolution fusion | flops 2119434240 | bytes 11304960 | tf_op jit(solution)/shard_map/dot_general | solution.py:60
  206.5 69.3 %all_to_all.19 = bf16[32,224,384]{2,1,0:T(8,128)(2,1)S(1)} all-to-all(bf16[32,224,384]{2,1,0:T(8,128)(2,1)S(1)} %bitcast.29), channel_id=1, replica_groups=mesh['fsdp'=32,'expert'=16] {'fsdp'}, dimensions={0} | all-to-all | bytes 11010048 | tf_op jit(solution)/shard_map/all_to_all | solution.py:63
  275.7 0.7 slice.6
  (2 shorter events, 0.0 us)
Async XLA Ops:
  185.5 3.6 %copy-start = (bf16[32,224,384]{2,1,0:T(8,128)(2,1)}, bf16[32,224,384]{2,1,0:T(8,128)(2,1)S(1)}, u32[]{:S(2)}) copy-start(bf16[32,224,384]{2,1,0:T(8,128)(2,1)S(1)} %all_to_all.18) | copy-start | bytes 16515076
  191.2 11.5 %slice-start = ((s8[5505024]{0:T(1024)(128)(4,1)}), s8[4194304]{0:T(1024)(128)(4,1)S(1)}, s32[]{:S(2)}) async-start(s8[5505024]{0:T(1024)(128)(4,1)} %bitcast.26), calls=%async_computation.2 | async-start | bytes 8388608
  196.1 6.6 %slice-start.1 = ((s8[5505024]{0:T(1024)(128)(4,1)}), s8[1310720]{0:T(1024)(128)(4,1)S(1)}, s32[]{:S(2)}) async-start(s8[5505024]{0:T(1024)(128)(4,1)} %bitcast.26), calls=%async_computation.3 | async-start | bytes 2621440
where the time goes:
time: 277 us; the launch traced here: 276 us
  blocking collectives  249 us (90%)
  matrix products  20.1 us (7%)
  other arithmetic  4.06 us (1%)
    psum x1, blocking collectives, per_device(): total = lax.psum(jnp.sum(grad_full * grad_full), ('fsdp', 'expert'))  111 us
    all_to_all x1, blocking collectives, per_device(): lax.all_to_all(finished, 'fsdp', split_axis=0, concat_axis=0, tiled=True)  69.3 us
    all_to_all x1, blocking collectives, per_device(): lax.all_to_all(send_buffer.reshape(fsdp_count * width, row_count), 'fsdp'...  69.1 us

commit v1 on v0

v1 whole, which is shorter than its diff:
```python
import math

import jax
import jax.numpy as jnp
from jax import lax
from jax.sharding import PartitionSpec as P

ITERS = 3

BETA = 0.95
COEF_A = 3.4445
COEF_B = -4.775
COEF_C = 2.0315


def orthogonal_factor(gram_matrix):
    order = gram_matrix.shape[0]
    identity = jnp.eye(order, dtype=jnp.float32)
    norm_inv = 1.0 / (jnp.sqrt(jnp.trace(gram_matrix)) + 1e-07)
    moment = gram_matrix * (norm_inv * norm_inv)
    factor = None
    for iteration in range(ITERS):
        square = jnp.dot(moment, moment, precision=lax.Precision.HIGHEST)
        poly = COEF_A * identity + COEF_B * moment + COEF_C * square
        if factor is None:
            factor = poly * norm_inv
        else:
            factor = jnp.dot(poly, factor, precision=lax.Precision.HIGHEST)
        if iteration + 1 < ITERS:
            moment = jnp.dot(
                jnp.dot(poly, moment, precision=lax.Precision.HIGHEST),
                poly,
                precision=lax.Precision.HIGHEST,
            )
    return factor.astype(jnp.bfloat16)


def exchange(blocks, axis):
    return lax.all_to_all(blocks, axis, split_axis=0, concat_axis=0, tiled=True)


def scalar_sum(value, axis):
    size = lax.axis_size(axis)
    rows = exchange(jnp.full((size, 128), value, jnp.float32), axis)
    return jnp.sum(rows[:, 0])


def per_device(grad, momentum):
    grad_full = grad[0].astype(jnp.float32)
    fsdp_count = lax.axis_size("fsdp")
    group_count = lax.axis_size("expert")
    total = scalar_sum(jnp.sum(grad_full * grad_full), "expert")
    total = scalar_sum(total, "fsdp")
    mean_square = total / (grad.size * fsdp_count * group_count)
    clip_factor = 1.0 / jnp.sqrt(mean_square + 1e-06)
    new_momentum = BETA * momentum[0] + clip_factor * grad_full
    direction = (clip_factor * grad_full + BETA * new_momentum).astype(jnp.bfloat16)
    width, row_count = direction.shape
    step_scale = 0.2 * math.sqrt(max(row_count, width * fsdp_count))
    part = jnp.einsum("cn,cm->nm", direction, direction, preferred_element_type=jnp.float32)
    share = row_count // fsdp_count
    mine = jnp.sum(exchange(part.reshape(fsdp_count, share, row_count), "fsdp"), axis=0)
    spread = jnp.broadcast_to(mine[None], (fsdp_count, share, row_count))
    gram_matrix = exchange(spread, "fsdp").reshape(row_count, row_count)
    factor = orthogonal_factor(gram_matrix)
    product = jnp.dot(direction, factor.T, preferred_element_type=jnp.float32)
    update = (step_scale * product).astype(jnp.bfloat16)
    return (new_momentum[None], update[None])


def solution(mesh):
    placed = P("expert", "fsdp", None)
    return jax.shard_map(
        per_device,
        mesh=mesh,
        in_specs=(placed, placed),
        out_specs=(placed, placed),
        check_vma=False,
    )
```

time: 277 us -> 103 us (0.37)
  blocking collectives: 249 us -> 60.7 us
  waiting for transfers between devices: 0 us -> 14.3 us
  matrix products: 20.1 us -> 12.7 us
  starting transfers between devices: 0 us -> 4.13 us
    psum x1 -> x0, blocking collectives: 111 us -> none  [per_device(): total = lax.psum(jnp.sum(grad_full * grad_full), ('fsdp', 'expert'))]
    all_to_all x2 -> x3, blocking collectives: 138 us -> 60.7 us  [exchange(): return lax.all_to_all(blocks, axis, split_axis=0, concat_axis=0, tiled=True)]
    all_to_all x0 -> x1, waiting for transfers between devices: none -> 14.3 us  [exchange(): return lax.all_to_all(blocks, axis, split_axis=0, concat_axis=0, tiled=True)]
    dot_general x2, matrix products: 7.43 us -> 1.25 us  [the longest x1 0.95 us: per_device(): product = jnp.dot(direction, factor.T, preferred_element_type=jnp.float32)]
    all_to_all x0 -> x1, starting transfers between devices: none -> 4.13 us  [exchange(): return lax.all_to_all(blocks, axis, split_axis=0, concat_axis=0, tiled=True)]
  transfers between devices with their start and end apart: 0 -> 1, of which waited for: 0 -> 1; matrix products, arithmetic and copies ran while one was open for 0% -> 0% of each run, Pallas kernels for 0% -> 0%
where the time goes in v1:
time: 103 us
  blocking collectives  60.7 us (59%)
  waiting for transfers between devices  14.3 us (14%)
  matrix products  12.7 us (12%)
  other arithmetic  5.09 us (5%)
  starting transfers between devices  4.13 us (4%)
  local copies, waits for them, and re-layouts  3.38 us (3%)
  between operations  2.25 us (2%)
    all_to_all x3, blocking collectives, exchange(): return lax.all_to_all(blocks, axis, split_axis=0, concat_axis=0, tiled=True)  60.7 us
    all_to_all x1, waiting for transfers between devices, exchange(): return lax.all_to_all(blocks, axis, split_axis=0, concat_axis=0, tiled=True)  14.3 us
    all_to_all x1, starting transfers between devices, exchange(): return lax.all_to_all(blocks, axis, split_axis=0, concat_axis=0, tiled=True)  4.13 us
    dot_general x3, matrix products, orthogonal_factor(): square = jnp.dot(moment, moment, precision=lax.Precision.HIGHEST)  3.83 us
    dot_general x2, matrix products, orthogonal_factor(): jnp.dot(poly, moment, precision=lax.Precision.HIGHEST)  2.53 us
    dot_general x2, matrix products, orthogonal_factor(): factor = jnp.dot(poly, factor, precision=lax.Precision.HIGHEST)  2.53 us
    dot_general x2, matrix products, orthogonal_factor(): jnp.dot(jnp.dot(poly, moment, precision=lax.Precision.HIGHEST), poly, pre...  2.53 us
  transfers between devices with their start and end apart: 1, of which 1 were waited for; matrix products, arithmetic and copies ran while one was open for 0% of the time, Pallas kernels for 0%

profile of v1, /device:TPU:1, one launch (start us, length us, event | category | flops | bytes accessed | tf_op | source)
XLA Modules:
  0.0 102.5 jit_solution(1586092935588370652)
XLA Ops:
  0.6 0.0 copy-start
  0.6 1.7 %fusion.15 = f32[]{:T(128)} fusion(bf16[1,224,384]{2,1,0:T(8,128)(2,1)} %param.2), kind=kLoop, calls=%fused_computation.29 | loop fusion | flops 258047 | bytes 172036 | tf_op jit(solution)/shard_map/reduce_sum | solution.py:52
  2.3 0.6 broadcast_in_dim.20
  3.0 26.8 %all_to_all.28 = f32[16,1,128]{2,1,0:T(1,128)S(1)} all-to-all(f32[16,1,128]{2,1,0:T(1,128)S(1)} %broadcast_in_dim.20), channel_id=1, replica_groups=mesh['fsdp'=32,'expert'=16] {'expert'}, dimensions={0} | all-to-all | bytes 16384 | tf_op jit(solution)/shard_map/all_to_all | solution.py:39
  29.8 0.6 slice_reduce_fusion.1
  30.4 0.7 broadcast_in_dim.21
  31.1 15.9 %all_to_all.29 = f32[32,1,128]{2,1,0:T(1,128)S(1)} all-to-all(f32[32,1,128]{2,1,0:T(1,128)S(1)} %broadcast_in_dim.21), channel_id=1, replica_groups=mesh['fsdp'=32,'expert'=16] {'fsdp'}, dimensions={0} | all-to-all | bytes 32768 | tf_op jit(solution)/shard_map/all_to_all | solution.py:39
  47.0 0.6 slice_reduce_fusion
  48.3 0.0 copy-done
  48.3 0.0 copy-start.1
  48.3 1.1 %fusion.13 = bf16[224,384]{1,0:T(8,128)(2,1)S(1)} fusion(bf16[1,224,384]{2,1,0:T(8,128)(2,1)S(1)} %copy-done, f32[1,224,384]{2,1,0:T(8,128)} %param.3, f32[]{:T(128)S(6)} %sqrt.6), kind=kLoop, calls=%fused_computation.27 | loop fusion | flops 602112 | bytes 688132 | tf_op jit(solution)/shard_map/convert_element_type | solution.py:57
  49.4 0.0 copy-done.1
  49.4 0.1 fusion.9
  49.5 0.0 copy-start.2
  49.5 0.1 copy.15
  49.7 0.1 dot_general.38
  49.7 0.5 copy-done.2
  50.2 0.3 fusion.17
  50.5 0.4 copy.17
  50.9 17.9 %all_to_all.30 = f32[32,12,384]{2,1,0:T(8,128)S(1)} all-to-all(f32[32,12,384]{2,1,0:T(8,128)S(1)} %copy.17), channel_id=1, replica_groups=mesh['fsdp'=32,'expert'=16] {'fsdp'}, dimensions={0} | all-to-all | bytes 1179648 | tf_op jit(solution)/shard_map/all_to_all | solution.py:39
  68.9 0.1 reduce_sum.49
  68.9 0.9 broadcast_in_dim.22
  69.9 4.1 %all-to-all-start.3 = ((f32[32,12,384]{2,1,0:T(8,128)}), f32[32,12,384]{2,1,0:T(8,128)S(1)}, u32[]{:S(2)}, u32[]{:S(2)}) async-start(f32[32,12,384]{2,1,0:T(8,128)} %broadcast_in_dim.22), calls=%async_computation.3 | async-start | bytes 1572864 | tf_op jit(solution)/shard_map/all_to_all | solution.py:39
  74.0 14.3 %all-to-all-done.3 = f32[32,12,384]{2,1,0:T(8,128)S(1)} async-done(((f32[32,12,384]{2,1,0:T(8,128)}), f32[32,12,384]{2,1,0:T(8,128)S(1)}, u32[]{:S(2)}, u32[]{:S(2)}) %all-to-all-start.3) | async-done | bytes 589856 | tf_op jit(solution)/shard_map/all_to_all | solution.py:39
  88.3 0.9 select_reduce_fusion
  90.0 0.1 broadcast_multiply_fusion
  90.0 0.1 mul.96
  90.1 1.3 %fusion = f32[384,384]{1,0:T(8,128)S(1)} fusion(f32[384,384]{1,0:T(8,128)S(1)} %mul.96), kind=kOutput, calls=%fused_computation.3 | convolution fusion | flops 680361984 | bytes 1179648 | tf_op jit(solution)/shard_map/dot_general | solution.py:23
  91.4 1.3 %fusion.24 = f32[384,384]{1,0:T(8,128)S(1)} fusion(f32[384,384]{1,0:T(8,128)S(1)} %fusion, f32[384,384]{1,0:T(8,128)S(1)} %mul.96), kind=kOutput, calls=%fused_computation.40 | convolution fusion | flops 679477248 | bytes 1769472 | tf_op jit(solution)/shard_map/dot_general | solution.py:31
  92.7 1.3 %fusion.25 = f32[384,384]{1,0:T(8,128)S(1)} fusion(f32[384,384]{1,0:T(8,128)S(1)} %fusion.24, f32[384,384]{1,0:T(8,128)S(1)} %fusion), kind=kOutput, calls=%fused_computation.41 | convolution fusion | flops 679477248 | bytes 1769472 | tf_op jit(solution)/shard_map/dot_general | solution.py:30
  93.9 1.3 %fusion.1 = f32[384,384]{1,0:T(8,128)S(1)} fusion(f32[384,384]{1,0:T(8,128)S(1)} %fusion.25), kind=kOutput, calls=%fused_computation.4 | convolution fusion | flops 680361984 | bytes 1179648 | tf_op jit(solution)/shard_map/dot_general | solution.py:23
  95.2 1.3 %fusion.5 = f32[384,384]{1,0:T(8,128)S(1)} fusion(f32[384,384]{1,0:T(8,128)S(1)} %fusion.1, f32[384,384]{1,0:T(8,128)S(1)} %fusion, f32[]{:T(128)S(6)} %div.8), kind=kOutput, calls=%fused_computation.15 | convolution fusion | flops 679624704 | bytes 1769476 | tf_op jit(solution)/shard_map/dot_general | solution.py:28
  96.5 1.3 %fusion.26 = f32[384,384]{1,0:T(8,128)S(1)} fusion(f32[384,384]{1,0:T(8,128)S(1)} %fusion.1, f32[384,384]{1,0:T(8,128)S(1)} %fusion.25), kind=kOutput, calls=%fused_computation.42 | convolution fusion | flops 679477248 | bytes 1769472 | tf_op jit(solution)/shard_map/dot_general | solution.py:31
  97.8 1.3 %fusion.27 = f32[384,384]{1,0:T(8,128)S(1)} fusion(f32[384,384]{1,0:T(8,128)S(1)} %fusion.26, f32[384,384]{1,0:T(8,128)S(1)} %fusion.1), kind=kOutput, calls=%fused_computation.43 | convolution fusion | flops 679477248 | bytes 1769472 | tf_op jit(solution)/shard_map/dot_general | solution.py:30
  99.0 1.3 %fusion.2 = f32[384,384]{1,0:T(8,128)S(1)} fusion(f32[384,384]{1,0:T(8,128)S(1)} %fusion.27), kind=kOutput, calls=%fused_computation.5 | convolution fusion | flops 680361984 | bytes 1179648 | tf_op jit(solution)/shard_map/dot_general | solution.py:23
  100.3 1.3 %convolution_convert_fusion = bf16[384,384]{1,0:T(8,128)(2,1)S(1)} fusion(f32[384,384]{1,0:T(8,128)S(1)} %fusion.2, f32[384,384]{1,0:T(8,128)S(1)} %fusion.5), kind=kOutput, calls=%fused_computation.6 | convolution fusion | flops 679624704 | bytes 1474560 | tf_op jit(solution)/shard_map/dot_general | solution.py:28
  101.6 0.9 fusion.4
  (1 shorter events, 0.0 us)
Async XLA Ops:
  0.6 47.7 %copy-start = (bf16[1,224,384]{2,1,0:T(8,128)(2,1)S(1)}, bf16[1,224,384]{2,1,0:T(8,128)(2,1)}, u32[]{:S(2)}) copy-start(bf16[1,224,384]{2,1,0:T(8,128)(2,1)} %param.2) | copy-start | bytes 516100
  48.3 1.1 %copy-start.1 = (f32[1,224,384]{2,1,0:T(8,128)S(1)}, f32[1,224,384]{2,1,0:T(8,128)}, u32[]{:S(2)}) copy-start(f32[1,224,384]{2,1,0:T(8,128)} %param.3) | copy-start | bytes 1032196
  49.5 0.7 copy-start.2
  69.9 18.5 %all-to-all-start.3 = ((f32[32,12,384]{2,1,0:T(8,128)}), f32[32,12,384]{2,1,0:T(8,128)S(1)}, u32[]{:S(2)}, u32[]{:S(2)}) async-start(f32[32,12,384]{2,1,0:T(8,128)} %broadcast_in_dim.22), calls=%async_computation.3 | async-start | bytes 1572864 | tf_op jit(solution)/shard_map/all_to_all | solution.py:39

commit v2 on v1

v2 whole, which is shorter than its diff:
```python
import functools
import math

import jax
import jax.numpy as jnp
from jax import lax
from jax.experimental import pallas as pl
from jax.experimental.pallas import tpu as pltpu
from jax.sharding import PartitionSpec as P

ITERS = 3

BETA = 0.95
COEF_A = 3.4445
COEF_B = -4.775
COEF_C = 2.0315

LANE = 128
SUB = 8
CORES = 2


def dot(a, b):
    return jnp.dot(a, b, preferred_element_type=jnp.float32)


def split(x):
    high = x.astype(jnp.bfloat16)
    return high, (x - high.astype(jnp.float32)).astype(jnp.bfloat16)


def blocks_of(order):
    side = order // LANE
    return [(i, j) for i in range(side) for j in range(i, side)]


def gram_kernel(grad_ref, momentum_ref, keep_ref, send_ref, square_ref):
    core = lax.rem(lax.axis_index("fsdp"), CORES)
    grad = grad_ref[0]
    full = grad.astype(jnp.float32)
    squares = jnp.sum(full * full, axis=0, keepdims=True)
    square_ref[...] = jnp.broadcast_to(jnp.sum(squares, axis=1, keepdims=True), square_ref.shape)
    high, low = split(momentum_ref[0])
    grad_t, high_t, low_t = grad.T, high.T, low.T
    grams = (
        dot(grad_t, grad),
        (dot(grad_t, high) + dot(high_t, grad)) + (dot(grad_t, low) + dot(low_t, grad)),
        dot(high_t, high) + (dot(high_t, low) + dot(low_t, high)),
    )
    chips, rows, _ = keep_ref.shape
    per_gram = rows // len(grams)
    pieces = per_gram // SUB
    blocks = blocks_of(grad.shape[1])
    for which, gram in enumerate(grams):

        def piece(q):
            i, j = blocks[q // (LANE // SUB)]
            top = i * LANE + q % (LANE // SUB) * SUB
            return gram[top : top + SUB, j * LANE : (j + 1) * LANE]

        for chip in range(chips):
            for p in range(pieces):
                first = piece((chip * CORES) * pieces + p)
                second = piece((chip * CORES + 1) * pieces + p)
                at = pl.ds(which * per_gram + p * SUB, SUB)
                keep_ref[chip, at, :] = jnp.where(core == 0, first, second)
                send_ref[chip, at, :] = jnp.where(core == 0, second, first)


def middle_kernel(parts_ref, squares_ref, spread_ref):
    chips, rows, _ = parts_ref.shape
    total = jnp.sum(parts_ref[...], axis=0)
    squares = jnp.sum(squares_ref[...], axis=0, keepdims=True)
    for chip in range(chips):
        spread_ref[chip, :rows, :] = total
        spread_ref[chip, rows:, :] = jnp.broadcast_to(squares, (SUB, LANE))


def product(a, b):
    return dot(a[0], b[0]) + (dot(a[0], b[1]) + dot(a[1], b[0]))


def final_kernel(step_scale, count, mine_ref, other_ref, grad_ref, momentum_ref, new_ref, update_ref, gram_ref):
    core = lax.rem(lax.axis_index("fsdp"), CORES)
    order = grad_ref.shape[2]
    chips, rows, _ = mine_ref.shape
    per_gram = (rows - SUB) // 3
    pieces = per_gram // SUB
    squares = jnp.sum(mine_ref[:, rows - SUB :, :], axis=0) + jnp.sum(other_ref[:, rows - SUB :, :], axis=0)
    clip = 1.0 / jnp.sqrt(squares / count + 1e-06)
    alpha = (1.0 + BETA) * clip
    some = alpha > 0.0
    gain_gg, gain_gm, gain_mm = alpha * alpha, alpha * (BETA * BETA), BETA**4
    blocks = blocks_of(order)
    trace = jnp.zeros((SUB, LANE), jnp.float32)
    for chip in range(chips):
        for p in range(pieces):
            at = [pl.ds(which * per_gram + p * SUB, SUB) for which in range(3)]
            held = [mine_ref[chip, a, :] for a in at]
            came = [other_ref[chip, a, :] for a in at]

            def joined(gg, gm, mm):
                return jnp.where(some, gain_gg * gg + gain_gm * gm, 0.0) + gain_mm * mm

            held, came = joined(*held), joined(*came)
            for c, piece in ((0, jnp.where(core == 0, held, came)), (1, jnp.where(core == 0, came, held))):
                q = (chip * CORES + c) * pieces + p
                i, j = blocks[q // (LANE // SUB)]
                down = q % (LANE // SUB) * SUB
                gram_ref[i * LANE + down : i * LANE + down + SUB, j * LANE : (j + 1) * LANE] = piece
                if i == j:
                    row = lax.broadcasted_iota(jnp.int32, (SUB, LANE), 0) + down
                    col = lax.broadcasted_iota(jnp.int32, (SUB, LANE), 1)
                    trace = trace + jnp.where(row == col, piece, 0.0)
    for i, j in blocks:
        if i < j:
            gram_ref[j * LANE : (j + 1) * LANE, i * LANE : (i + 1) * LANE] = gram_ref[
                i * LANE : (i + 1) * LANE, j * LANE : (j + 1) * LANE
            ].T

    clip = clip[:1, :1]
    grad_full = grad_ref[0].astype(jnp.float32)
    new_momentum = BETA * momentum_ref[0] + clip * grad_full
    new_ref[0] = new_momentum
    direction = (clip * grad_full + BETA * new_momentum).astype(jnp.bfloat16)

    trace = jnp.sum(jnp.sum(trace, axis=0, keepdims=True), axis=1, keepdims=True)
    norm_inv = 1.0 / (jnp.sqrt(trace) + 1e-07)
    moment = gram_ref[...] * (norm_inv * norm_inv)
    row = lax.broadcasted_iota(jnp.int32, (order, order), 0)
    col = lax.broadcasted_iota(jnp.int32, (order, order), 1)
    diagonal = jnp.where(row == col, COEF_A, 0.0)
    factor = None
    for iteration in range(ITERS):
        moment_parts = split(moment)
        poly = diagonal + COEF_B * moment + COEF_C * product(moment_parts, moment_parts)
        poly_parts = split(poly)
        if factor is None:
            factor = poly * norm_inv
        else:
            factor = product(poly_parts, split(factor))
        if iteration + 1 < ITERS:
            moment = product(split(product(poly_parts, moment_parts)), poly_parts)
    update = dot(direction, factor.astype(jnp.bfloat16).T)
    update_ref[0] = (step_scale * update).astype(jnp.bfloat16)


def call(kernel, shapes, scratch=()):
    return pl.pallas_call(
        kernel,
        out_shape=shapes,
        scratch_shapes=scratch,
        compiler_params=pltpu.CompilerParams(vmem_limit_bytes=24 * 2**20),
    )


def per_device(grad, momentum):
    fsdp_count = lax.axis_size("fsdp")
    group_count = lax.axis_size("expert")
    _, width, order = grad.shape
    step_scale = 0.2 * math.sqrt(max(order, width * fsdp_count))
    count = grad.size * fsdp_count * group_count
    chips = fsdp_count // CORES
    share = len(blocks_of(order)) * LANE // fsdp_count
    f32 = jnp.float32
    half = jax.ShapeDtypeStruct((chips, 3 * share, LANE), f32)
    keep, send, square = call(
        gram_kernel, (half, half, jax.ShapeDtypeStruct((group_count, LANE), f32))
    )(grad, momentum)
    squares = lax.all_to_all(square, "expert", split_axis=0, concat_axis=0, tiled=True)
    pairs = [(i, i ^ 1) for i in range(fsdp_count)]
    groups = [[CORES * i + c for i in range(chips)] for c in range(CORES)]
    both = keep + lax.ppermute(send, "fsdp", pairs)

    def exchange(x):
        return lax.all_to_all(x, "fsdp", split_axis=0, concat_axis=0, tiled=True, axis_index_groups=groups)

    spread = call(
        middle_kernel, jax.ShapeDtypeStruct((chips, 3 * share + SUB, LANE), f32)
    )(exchange(both), squares)
    mine = exchange(spread)
    other = lax.ppermute(mine, "fsdp", pairs)
    return call(
        functools.partial(final_kernel, step_scale, count),
        (
            jax.ShapeDtypeStruct(grad.shape, f32),
            jax.ShapeDtypeStruct(grad.shape, jnp.bfloat16),
        ),
        (pltpu.VMEM((order, order), f32),),
    )(mine, other, grad, momentum)


def solution(mesh):
    placed = P("expert", "fsdp", None)
    return jax.shard_map(
        per_device,
        mesh=mesh,
        in_specs=(placed, placed),
        out_specs=(placed, placed),
        check_vma=False,
    )
```

time: 103 us -> 79.2 us (0.77)
  blocking collectives: 60.7 us -> 30.3 us
  starting transfers between devices: 4.13 us -> 23.9 us
  matrix products: 12.7 us -> 0 us
  Pallas kernels: 0 us -> 9.09 us
  other arithmetic: 5.09 us -> 0.08 us
  between operations: 2.25 us -> 0.7 us
  waiting for transfers between devices: 14.3 us -> 12.8 us
  local copies, waits for them, and re-layouts: 3.38 us -> 1.9 us
    all_to_all x3 -> x2, blocking collectives: 60.7 us -> 30.3 us  [exchange(): lax.all_to_all(x, 'fsdp', split_axis=0, concat_axis=0, tiled=True, axis_i...]
    ppermute x0 -> x2, starting transfers between devices: none -> 14.4 us  [the longest x1 8.78 us: per_device(): both = keep + lax.ppermute(send, 'fsdp', pairs)]
    dot_general x11 -> x0, matrix products: 12.7 us -> none  [the longest x3 3.83 us: orthogonal_factor(): square = jnp.dot(moment, moment, precision=lax.Precision.HIGHEST)]
    pallas_call x0 -> x3, Pallas kernels: none -> 9.09 us  [the longest x1 7.49 us: per_device(): call(functools.partial(final_kernel, step_scale, count), (jax.ShapeDtypeS...]
    all_to_all x1, starting transfers between devices: 4.13 us -> 9.55 us  [per_device(): lax.all_to_all(square, 'expert', split_axis=0, concat_axis=0, tiled=True)]
    reduce_sum x5 -> x0, other arithmetic: 3.85 us -> none  [the longest x1 1.68 us: per_device(): total = scalar_sum(jnp.sum(grad_full * grad_full), 'expert')]
    all_to_all x1, waiting for transfers between devices: 14.3 us -> 11.1 us  [per_device(): lax.all_to_all(square, 'expert', split_axis=0, concat_axis=0, tiled=True)]
    broadcast_in_dim x3 -> x0, local copies, waits for them, and re-layouts: 2.23 us -> none  [the longest x2 1.3 us: scalar_sum(): rows = exchange(jnp.full((size, 128), value, jnp.float32), axis)]
  transfers between devices with their start and end apart: 1 -> 3, of which waited for: 1 -> 2; matrix products, arithmetic and copies ran while one was open for 0% -> 0% of each run, Pallas kernels for 0% -> 0%
where the time goes in v2:
time: 79.2 us; the launch traced here: 78.9 us
  blocking collectives  30.3 us (38%)
  starting transfers between devices  23.9 us (30%)
  waiting for transfers between devices  12.8 us (16%)
  Pallas kernels  9.09 us (11%)
  local copies, waits for them, and re-layouts  1.9 us (2%)
    all_to_all x2, blocking collectives, exchange(): lax.all_to_all(x, 'fsdp', split_axis=0, concat_axis=0, tiled=True, axis_i...  30.3 us
    all_to_all x1, waiting for transfers between devices, per_device(): lax.all_to_all(square, 'expert', split_axis=0, concat_axis=0, tiled=True)  11.1 us
    all_to_all x1, starting transfers between devices, per_device(): lax.all_to_all(square, 'expert', split_axis=0, concat_axis=0, tiled=True)  9.55 us
    ppermute x1, starting transfers between devices, per_device(): both = keep + lax.ppermute(send, 'fsdp', pairs)  8.78 us
    pallas_call x1, Pallas kernels, per_device(): call(functools.partial(final_kernel, step_scale, count), (jax.ShapeDtypeS...  7.49 us
    ppermute x1, starting transfers between devices, per_device(): other = lax.ppermute(mine, 'fsdp', pairs)  5.61 us
    unnamed x8, local copies, waits for them, and re-layouts  1.9 us
    ppermute x1, waiting for transfers between devices, per_device(): other = lax.ppermute(mine, 'fsdp', pairs)  1.7 us
  transfers between devices with their start and end apart: 3, of which 2 were waited for; matrix products, arithmetic and copies ran while one was open for 0% of the time, Pallas kernels for 0%

profile of v2, /device:TPU:1, one launch (start us, length us, event | category | flops | bytes accessed | tf_op | source)
XLA Modules:
  0.0 78.9 jit_solution(15103195648645038929)
XLA Ops:
  0.6 0.0 copy-start
  0.6 1.0 %copy-done = f32[1,224,384]{2,1,0:T(8,128)S(1)} copy-done((f32[1,224,384]{2,1,0:T(8,128)S(1)}, f32[1,224,384]{2,1,0:T(8,128)}, u32[]{:S(2)}) %copy-start) | copy-done | bytes 344088
  1.6 0.0 copy-start.2
  1.6 0.9 %copy-done.2 = bf16[1,224,384]{2,1,0:T(8,128)(2,1)S(1)} copy-done((bf16[1,224,384]{2,1,0:T(8,128)(2,1)S(1)}, bf16[1,224,384]{2,1,0:T(8,128)(2,1)}, u32[]{:S(2)}) %copy-start.2) | copy-done | bytes 172056
  2.5 1.5 %shard_map.41 = (f32[16,72,128]{2,1,0:T(8,128)S(1)}, f32[16,72,128]{2,1,0:T(8,128)S(1)}, f32[16,128]{1,0:T(8,128)}) custom-call(bf16[1,224,384]{2,1,0:T(8,128)(2,1)S(1)} %copy-done.2, f32[1,224,384]{2,1,0:T(8,128)S(1)} %copy-done), custom_call_target="tpu_custom_call" | custom-call | tf_op jit(solution)/shard_map/pallas_call | solution.py:167
  4.1 8.8 %collective-permute-start = (f32[16,72,128]{2,1,0:T(8,128)S(1)}, f32[16,72,128]{2,1,0:T(8,128)S(1)}, u32[]{:S(2)}, u32[]{:S(2)}) collective-permute-start(f32[16,72,128]{2,1,0:T(8,128)S(1)} %get-tuple-element.6), channel_id=1, source_target_pairs={{0,16},{16,0},{32,48},{48,32},{64,80},{80,64},{96,112},{112,96},{1... | collective-permute-start | bytes 1769480 | tf_op jit(solution)/shard_map/ppermute | solution.py:173
  12.9 9.6 %all-to-all-start.1 = ((f32[16,1,128]{2,1,0:T(1,128)}), f32[16,1,128]{2,1,0:T(1,128)S(1)}, u32[]{:S(2)}, u32[]{:S(2)}) async-start(f32[16,1,128]{2,1,0:T(1,128)} %bitcast.1), calls=%async_computation.1 | async-start | bytes 16384 | tf_op jit(solution)/shard_map/all_to_all | solution.py:170
  22.4 0.0 collective-permute-done
  22.4 0.1 add.3
  22.5 11.1 %all-to-all-done.1 = f32[16,1,128]{2,1,0:T(1,128)S(1)} async-done(((f32[16,1,128]{2,1,0:T(1,128)}), f32[16,1,128]{2,1,0:T(1,128)S(1)}, u32[]{:S(2)}, u32[]{:S(2)}) %all-to-all-start.1) | async-done | bytes 8224 | tf_op jit(solution)/shard_map/all_to_all | solution.py:170
  33.6 17.0 %all_to_all.21.parts_ref = f32[16,72,128]{2,1,0:T(8,128)S(1)} all-to-all(f32[16,72,128]{2,1,0:T(8,128)S(1)} %add.3), channel_id=1, replica_groups={{0,32,64,96,128,160,192,224,256,288,320,352,384,416,448,480},{16,48,80,..., dimensions={0} | all-to-all | bytes 1179648 | tf_op jit(solution)/shard_map/all_to_all | solution.py:176
  50.7 0.1 shard_map.42
  50.7 0.0 copy-start.1
  50.7 0.0 copy-start.3
  50.8 13.3 %all_to_all.22.mine_ref = f32[16,80,128]{2,1,0:T(8,128)S(1)} all-to-all(f32[16,80,128]{2,1,0:T(8,128)S(1)} %shard_map.42), channel_id=1, replica_groups={{0,32,64,96,128,160,192,224,256,288,320,352,384,416,448,480},{16,48,80,..., dimensions={0} | all-to-all | bytes 1310720 | tf_op jit(solution)/shard_map/all_to_all | solution.py:176
  64.0 5.6 %collective-permute-start.1 = (f32[16,80,128]{2,1,0:T(8,128)S(1)}, f32[16,80,128]{2,1,0:T(8,128)S(1)}, u32[]{:S(2)}, u32[]{:S(2)}) collective-permute-start(f32[16,80,128]{2,1,0:T(8,128)S(1)} %all_to_all.22.mine_ref), channel_id=1, source_target_pairs={{0,16},{16,0},{32,48},{48,32},{64,80},{80,64},{96,112},{112,96},{1... | collective-permute-start | bytes 1966088 | tf_op jit(solution)/shard_map/ppermute | solution.py:182
  69.7 1.7 %collective-permute-done.1.other_ref = f32[16,80,128]{2,1,0:T(8,128)S(1)} collective-permute-done((f32[16,80,128]{2,1,0:T(8,128)S(1)}, f32[16,80,128]{2,1,0:T(8,128)S(1)}, u32[]{:S(2)}, u32[]{:S(2)}) %collective-permute-start.1) | collective-permute-done | bytes 655392 | tf_op jit(solution)/shard_map/ppermute | solution.py:182
  71.4 0.0 copy-done.1
  71.4 0.0 copy-done.3
  71.4 7.5 %shard_map.43 = (f32[1,224,384]{2,1,0:T(8,128)}, bf16[1,224,384]{2,1,0:T(8,128)(2,1)}) custom-call(f32[16,80,128]{2,1,0:T(8,128)S(1)} %all_to_all.22.mine_ref, f32[16,80,128]{2,1,0:T(8,128)S(1)} %collective-permute-done.1.other_ref, bf16[1,224,384]{2,1,0:T(8,128)(2,1)S(1)} %copy-done.3, f32[1,224,384]{2,1,0:T(8,128)S(1)} %copy-done.1), custom_call_target="tpu_custom_call" | custom-call | tf_op jit(solution)/shard_map/pallas_call | solution.py:183
Async XLA Ops:
  0.6 1.0 %copy-start = (f32[1,224,384]{2,1,0:T(8,128)S(1)}, f32[1,224,384]{2,1,0:T(8,128)}, u32[]{:S(2)}) copy-start(f32[1,224,384]{2,1,0:T(8,128)} %momentum_ref.3) | copy-start | bytes 1032196
  1.6 0.9 %copy-start.2 = (bf16[1,224,384]{2,1,0:T(8,128)(2,1)S(1)}, bf16[1,224,384]{2,1,0:T(8,128)(2,1)}, u32[]{:S(2)}) copy-start(bf16[1,224,384]{2,1,0:T(8,128)(2,1)} %grad_ref.3) | copy-start | bytes 516100
  4.1 18.4 %collective-permute-start = (f32[16,72,128]{2,1,0:T(8,128)S(1)}, f32[16,72,128]{2,1,0:T(8,128)S(1)}, u32[]{:S(2)}, u32[]{:S(2)}) collective-permute-start(f32[16,72,128]{2,1,0:T(8,128)S(1)} %get-tuple-element.6), channel_id=1, source_target_pairs={{0,16},{16,0},{32,48},{48,32},{64,80},{80,64},{96,112},{112,96},{1... | collective-permute-start | bytes 1769480 | tf_op jit(solution)/shard_map/ppermute | solution.py:173
  12.9 20.8 %all-to-all-start.1 = ((f32[16,1,128]{2,1,0:T(1,128)}), f32[16,1,128]{2,1,0:T(1,128)S(1)}, u32[]{:S(2)}, u32[]{:S(2)}) async-start(f32[16,1,128]{2,1,0:T(1,128)} %bitcast.1), calls=%async_computation.1 | async-start | bytes 16384 | tf_op jit(solution)/shard_map/all_to_all | solution.py:170
  50.7 20.6 %copy-start.1 = (f32[1,224,384]{2,1,0:T(8,128)S(1)}, f32[1,224,384]{2,1,0:T(8,128)}, u32[]{:S(2)}) copy-start(f32[1,224,384]{2,1,0:T(8,128)} %momentum_ref.3) | copy-start | bytes 1032196
  50.7 20.6 %copy-start.3 = (bf16[1,224,384]{2,1,0:T(8,128)(2,1)S(1)}, bf16[1,224,384]{2,1,0:T(8,128)(2,1)}, u32[]{:S(2)}) copy-start(bf16[1,224,384]{2,1,0:T(8,128)(2,1)} %grad_ref.3) | copy-start | bytes 516100
  64.0 7.3 %collective-permute-start.1 = (f32[16,80,128]{2,1,0:T(8,128)S(1)}, f32[16,80,128]{2,1,0:T(8,128)S(1)}, u32[]{:S(2)}, u32[]{:S(2)}) collective-permute-start(f32[16,80,128]{2,1,0:T(8,128)S(1)} %all_to_all.22.mine_ref), channel_id=1, source_target_pairs={{0,16},{16,0},{32,48},{48,32},{64,80},{80,64},{96,112},{112,96},{1... | collective-permute-start | bytes 1966088 | tf_op jit(solution)/shard_map/ppermute | solution.py:182

commit v3 on v2

--- a/solution.py
+++ b/solution.py
@@ -34,8 +34,7 @@
     return [(i, j) for i in range(side) for j in range(i, side)]
 
 
-def gram_kernel(grad_ref, momentum_ref, keep_ref, send_ref, square_ref):
-    core = lax.rem(lax.axis_index("fsdp"), CORES)
+def gram_kernel(grad_ref, momentum_ref, parts_ref, square_ref):
     grad = grad_ref[0]
     full = grad.astype(jnp.float32)
     squares = jnp.sum(full * full, axis=0, keepdims=True)
@@ -47,28 +46,23 @@
         (dot(grad_t, high) + dot(high_t, grad)) + (dot(grad_t, low) + dot(low_t, grad)),
         dot(high_t, high) + (dot(high_t, low) + dot(low_t, high)),
     )
-    chips, rows, _ = keep_ref.shape
+    devices, rows, _ = parts_ref.shape
     per_gram = rows // len(grams)
     pieces = per_gram // SUB
     blocks = blocks_of(grad.shape[1])
     for which, gram in enumerate(grams):
-
-        def piece(q):
-            i, j = blocks[q // (LANE // SUB)]
-            top = i * LANE + q % (LANE // SUB) * SUB
-            return gram[top : top + SUB, j * LANE : (j + 1) * LANE]
-
-        for chip in range(chips):
+        for device in range(devices):
             for p in range(pieces):
-                first = piece((chip * CORES) * pieces + p)
-                second = piece((chip * CORES + 1) * pieces + p)
+                q = device * pieces + p
+                i, j = blocks[q // (LANE // SUB)]
+                top = i * LANE + q % (LANE // SUB) * SUB
                 at = pl.ds(which * per_gram + p * SUB, SUB)
-                keep_ref[chip, at, :] = jnp.where(core == 0, first, second)
-                send_ref[chip, at, :] = jnp.where(core == 0, second, first)
+                parts_ref[device, at, :] = gram[top : top + SUB, j * LANE : (j + 1) * LANE]
 
 
 def middle_kernel(parts_ref, squares_ref, spread_ref):
-    chips, rows, _ = parts_ref.shape
+    _, rows, _ = parts_ref.shape
+    chips = spread_ref.shape[0]
     total = jnp.sum(parts_ref[...], axis=0)
     squares = jnp.sum(squares_ref[...], axis=0, keepdims=True)
     for chip in range(chips):
@@ -163,22 +157,23 @@
     chips = fsdp_count // CORES
     share = len(blocks_of(order)) * LANE // fsdp_count
     f32 = jnp.float32
-    half = jax.ShapeDtypeStruct((chips, 3 * share, LANE), f32)
-    keep, send, square = call(
-        gram_kernel, (half, half, jax.ShapeDtypeStruct((group_count, LANE), f32))
+    parts, square = call(
+        gram_kernel,
+        (
+            jax.ShapeDtypeStruct((fsdp_count, 3 * share, LANE), f32),
+            jax.ShapeDtypeStruct((SUB, LANE), f32),
+        ),
     )(grad, momentum)
-    squares = lax.all_to_all(square, "expert", split_axis=0, concat_axis=0, tiled=True)
+    squares = lax.all_gather(square[0], "expert")
+    parts = lax.all_to_all(parts, "fsdp", split_axis=0, concat_axis=0, tiled=True)
     pairs = [(i, i ^ 1) for i in range(fsdp_count)]
     groups = [[CORES * i + c for i in range(chips)] for c in range(CORES)]
-    both = keep + lax.ppermute(send, "fsdp", pairs)
-
-    def exchange(x):
-        return lax.all_to_all(x, "fsdp", split_axis=0, concat_axis=0, tiled=True, axis_index_groups=groups)
-
     spread = call(
         middle_kernel, jax.ShapeDtypeStruct((chips, 3 * share + SUB, LANE), f32)
-    )(exchange(both), squares)
-    mine = exchange(spread)
+    )(parts, squares)
+    mine = lax.all_to_all(
+        spread, "fsdp", split_axis=0, concat_axis=0, tiled=True, axis_index_groups=groups
+    )
     other = lax.ppermute(mine, "fsdp", pairs)
     return call(
         functools.partial(final_kernel, step_scale, count),

time: 79.2 us -> 78 us (0.985)
  blocking collectives: 30.3 us -> 43.3 us
  waiting for transfers between devices: 12.8 us -> 1.7 us
  starting transfers between devices: 23.9 us -> 20.5 us
    all_gather x0 -> x1, blocking collectives: none -> 27.4 us  [per_device(): squares = lax.all_gather(square[0], 'expert')]
    all_to_all x2 -> x1, blocking collectives: 30.3 us -> 15.9 us  [per_device(): lax.all_to_all(spread, 'fsdp', split_axis=0, concat_axis=0, tiled=True, a...]
    all_to_all x1, waiting for transfers between devices: 11.1 us -> 0.01 us  [per_device(): lax.all_to_all(parts, 'fsdp', split_axis=0, concat_axis=0, tiled=True)]
    ppermute x1 -> x0, starting transfers between devices: 8.78 us -> none  [per_device(): both = keep + lax.ppermute(send, 'fsdp', pairs)]
    ppermute x1, starting transfers between devices: 5.61 us -> 10 us  [per_device(): other = lax.ppermute(mine, 'fsdp', pairs)]
    all_to_all x1, starting transfers between devices: 9.55 us -> 10.5 us  [per_device(): lax.all_to_all(parts, 'fsdp', split_axis=0, concat_axis=0, tiled=True)]
    unnamed x8 -> x9, local copies, waits for them, and re-layouts: 1.9 us -> 1.9 us
  transfers between devices with their start and end apart: 3 -> 2, of which waited for: 2 -> 1; matrix products, arithmetic and copies ran while one was open for 0% -> 0% of each run, Pallas kernels for 0% -> 0%
where the time goes in v3:
time: 78 us; the launch traced here: 77.7 us
  blocking collectives  43.3 us (56%)
  starting transfers between devices  20.5 us (26%)
  Pallas kernels  9.6 us (12%)
  local copies, waits for them, and re-layouts  1.9 us (2%)
  waiting for transfers between devices  1.7 us (2%)
    all_gather x1, blocking collectives, per_device(): squares = lax.all_gather(square[0], 'expert')  27.4 us
    all_to_all x1, blocking collectives, per_device(): lax.all_to_all(spread, 'fsdp', split_axis=0, concat_axis=0, tiled=True, a...  15.9 us
    all_to_all x1, starting transfers between devices, per_device(): lax.all_to_all(parts, 'fsdp', split_axis=0, concat_axis=0, tiled=True)  10.5 us
    ppermute x1, starting transfers between devices, per_device(): other = lax.ppermute(mine, 'fsdp', pairs)  10 us
    pallas_call x1, Pallas kernels, per_device(): call(functools.partial(final_kernel, step_scale, count), (jax.ShapeDtypeS...  7.48 us
    pallas_call x1, Pallas kernels, per_device(): call(gram_kernel, (jax.ShapeDtypeStruct((fsdp_count, 3 * share, LANE), f3...  2.03 us
    unnamed x9, local copies, waits for them, and re-layouts  1.9 us
    ppermute x1, waiting for transfers between devices, per_device(): other = lax.ppermute(mine, 'fsdp', pairs)  1.7 us
  transfers between devices with their start and end apart: 2, of which 1 were waited for; matrix products, arithmetic and copies ran while one was open for 0% of the time, Pallas kernels for 0%

profile of v3, /device:TPU:1, one launch (start us, length us, event | category | flops | bytes accessed | tf_op | source)
XLA Modules:
  0.0 77.7 jit_solution(16088486525832359591)
XLA Ops:
  0.6 0.0 copy-start
  0.6 1.0 %copy-done = f32[1,224,384]{2,1,0:T(8,128)S(1)} copy-done((f32[1,224,384]{2,1,0:T(8,128)S(1)}, f32[1,224,384]{2,1,0:T(8,128)}, u32[]{:S(2)}) %copy-start) | copy-done | bytes 344088
  1.6 0.0 copy-start.2
  1.6 0.9 %copy-done.2 = bf16[1,224,384]{2,1,0:T(8,128)(2,1)S(1)} copy-done((bf16[1,224,384]{2,1,0:T(8,128)(2,1)S(1)}, bf16[1,224,384]{2,1,0:T(8,128)(2,1)}, u32[]{:S(2)}) %copy-start.2) | copy-done | bytes 172056
  2.5 2.0 %shard_map.41 = (f32[32,72,128]{2,1,0:T(8,128)}, f32[8,128]{1,0:T(8,128)S(1)}) custom-call(bf16[1,224,384]{2,1,0:T(8,128)(2,1)S(1)} %copy-done.2, f32[1,224,384]{2,1,0:T(8,128)S(1)} %copy-done), custom_call_target="tpu_custom_call" | custom-call | tf_op jit(solution)/shard_map/pallas_call | solution.py:160
  4.6 10.5 %all-to-all-start = ((f32[32,72,128]{2,1,0:T(8,128)}), f32[32,72,128]{2,1,0:T(8,128)S(1)}, u32[]{:S(2)}, u32[]{:S(2)}) async-start(f32[32,72,128]{2,1,0:T(8,128)} %get-tuple-element.4), calls=%async_computation | async-start | bytes 2359296 | tf_op jit(solution)/shard_map/all_to_all | solution.py:168
  15.1 27.4 %all-gather = f32[16,1,128]{2,1,0:T(1,128)S(1)} all-gather(f32[1,1,128]{2,1,0:T(1,128)S(1)} %slice_bitcast_fusion), channel_id=1, replica_groups=mesh['fsdp'=32,'expert'=16] {'expert'}, dimensions={0}, use_global_device_ids=true | all-gather | bytes 8704 | tf_op jit(solution)/shard_map/all_gather | solution.py:167
  42.5 0.0 all-to-all-done.parts_ref
  42.5 0.0 copy-start.1
  42.5 0.0 copy-start.3
  42.5 0.1 shard_map.42
  42.5 15.9 %all_to_all.10.mine_ref = f32[16,80,128]{2,1,0:T(8,128)S(1)} all-to-all(f32[16,80,128]{2,1,0:T(8,128)S(1)} %shard_map.42), channel_id=1, replica_groups={{0,32,64,96,128,160,192,224,256,288,320,352,384,416,448,480},{16,48,80,..., dimensions={0} | all-to-all | bytes 1310720 | tf_op jit(solution)/shard_map/all_to_all | solution.py:174
  58.5 10.0 %collective-permute-start = (f32[16,80,128]{2,1,0:T(8,128)S(1)}, f32[16,80,128]{2,1,0:T(8,128)S(1)}, u32[]{:S(2)}, u32[]{:S(2)}) collective-permute-start(f32[16,80,128]{2,1,0:T(8,128)S(1)} %all_to_all.10.mine_ref), channel_id=1, source_target_pairs={{0,16},{16,0},{32,48},{48,32},{64,80},{80,64},{96,112},{112,96},{1... | collective-permute-start | bytes 1966088 | tf_op jit(solution)/shard_map/ppermute | solution.py:177
  68.5 1.7 %collective-permute-done.other_ref = f32[16,80,128]{2,1,0:T(8,128)S(1)} collective-permute-done((f32[16,80,128]{2,1,0:T(8,128)S(1)}, f32[16,80,128]{2,1,0:T(8,128)S(1)}, u32[]{:S(2)}, u32[]{:S(2)}) %collective-permute-start) | collective-permute-done | bytes 655392 | tf_op jit(solution)/shard_map/ppermute | solution.py:177
  70.2 0.0 copy-done.1
  70.2 0.0 copy-done.3
  70.2 7.5 %shard_map.43 = (f32[1,224,384]{2,1,0:T(8,128)}, bf16[1,224,384]{2,1,0:T(8,128)(2,1)}) custom-call(f32[16,80,128]{2,1,0:T(8,128)S(1)} %all_to_all.10.mine_ref, f32[16,80,128]{2,1,0:T(8,128)S(1)} %collective-permute-done.other_ref, bf16[1,224,384]{2,1,0:T(8,128)(2,1)S(1)} %copy-done.3, f32[1,224,384]{2,1,0:T(8,128)S(1)} %copy-done.1), custom_call_target="tpu_custom_call" | custom-call | tf_op jit(solution)/shard_map/pallas_call | solution.py:178
  (1 shorter events, 0.0 us)
Async XLA Ops:
  0.6 1.0 %copy-start = (f32[1,224,384]{2,1,0:T(8,128)S(1)}, f32[1,224,384]{2,1,0:T(8,128)}, u32[]{:S(2)}) copy-start(f32[1,224,384]{2,1,0:T(8,128)} %momentum_ref.3) | copy-start | bytes 1032196
  1.6 0.9 %copy-start.2 = (bf16[1,224,384]{2,1,0:T(8,128)(2,1)S(1)}, bf16[1,224,384]{2,1,0:T(8,128)(2,1)}, u32[]{:S(2)}) copy-start(bf16[1,224,384]{2,1,0:T(8,128)(2,1)} %grad_ref.3) | copy-start | bytes 516100
  4.6 37.9 %all-to-all-start = ((f32[32,72,128]{2,1,0:T(8,128)}), f32[32,72,128]{2,1,0:T(8,128)S(1)}, u32[]{:S(2)}, u32[]{:S(2)}) async-start(f32[32,72,128]{2,1,0:T(8,128)} %get-tuple-element.4), calls=%async_computation | async-start | bytes 2359296 | tf_op jit(solution)/shard_map/all_to_all | solution.py:168
  42.5 27.7 %copy-start.1 = (f32[1,224,384]{2,1,0:T(8,128)S(1)}, f32[1,224,384]{2,1,0:T(8,128)}, u32[]{:S(2)}) copy-start(f32[1,224,384]{2,1,0:T(8,128)} %momentum_ref.3) | copy-start | bytes 1032196
  42.5 27.7 %copy-start.3 = (bf16[1,224,384]{2,1,0:T(8,128)(2,1)S(1)}, bf16[1,224,384]{2,1,0:T(8,128)(2,1)}, u32[]{:S(2)}) copy-start(bf16[1,224,384]{2,1,0:T(8,128)(2,1)} %grad_ref.3) | copy-start | bytes 516100
  58.5 11.7 %collective-permute-start = (f32[16,80,128]{2,1,0:T(8,128)S(1)}, f32[16,80,128]{2,1,0:T(8,128)S(1)}, u32[]{:S(2)}, u32[]{:S(2)}) collective-permute-start(f32[16,80,128]{2,1,0:T(8,128)S(1)} %all_to_all.10.mine_ref), channel_id=1, source_target_pairs={{0,16},{16,0},{32,48},{48,32},{64,80},{80,64},{96,112},{112,96},{1... | collective-permute-start | bytes 1966088 | tf_op jit(solution)/shard_map/ppermute | solution.py:177

commit v4 on v2

--- a/solution.py
+++ b/solution.py
@@ -34,12 +34,15 @@
     return [(i, j) for i in range(side) for j in range(i, side)]
 
 
-def gram_kernel(grad_ref, momentum_ref, keep_ref, send_ref, square_ref):
+def square_kernel(grad_ref, square_ref):
+    full = grad_ref[0].astype(jnp.float32)
+    squares = jnp.sum(full * full, axis=0, keepdims=True)
+    square_ref[...] = jnp.broadcast_to(jnp.sum(squares, axis=1, keepdims=True), square_ref.shape)
+
+
+def gram_kernel(grad_ref, momentum_ref, keep_ref, send_ref):
     core = lax.rem(lax.axis_index("fsdp"), CORES)
     grad = grad_ref[0]
-    full = grad.astype(jnp.float32)
-    squares = jnp.sum(full * full, axis=0, keepdims=True)
-    square_ref[...] = jnp.broadcast_to(jnp.sum(squares, axis=1, keepdims=True), square_ref.shape)
     high, low = split(momentum_ref[0])
     grad_t, high_t, low_t = grad.T, high.T, low.T
     grams = (
@@ -70,10 +73,10 @@
 def middle_kernel(parts_ref, squares_ref, spread_ref):
     chips, rows, _ = parts_ref.shape
     total = jnp.sum(parts_ref[...], axis=0)
-    squares = jnp.sum(squares_ref[...], axis=0, keepdims=True)
+    squares = jnp.broadcast_to(squares_ref[...], (SUB, LANE))
     for chip in range(chips):
         spread_ref[chip, :rows, :] = total
-        spread_ref[chip, rows:, :] = jnp.broadcast_to(squares, (SUB, LANE))
+        spread_ref[chip, rows:, :] = squares
 
 
 def product(a, b):
@@ -164,20 +167,25 @@
     share = len(blocks_of(order)) * LANE // fsdp_count
     f32 = jnp.float32
     half = jax.ShapeDtypeStruct((chips, 3 * share, LANE), f32)
-    keep, send, square = call(
-        gram_kernel, (half, half, jax.ShapeDtypeStruct((group_count, LANE), f32))
-    )(grad, momentum)
-    squares = lax.all_to_all(square, "expert", split_axis=0, concat_axis=0, tiled=True)
-    pairs = [(i, i ^ 1) for i in range(fsdp_count)]
     groups = [[CORES * i + c for i in range(chips)] for c in range(CORES)]
-    both = keep + lax.ppermute(send, "fsdp", pairs)
 
     def exchange(x):
         return lax.all_to_all(x, "fsdp", split_axis=0, concat_axis=0, tiled=True, axis_index_groups=groups)
 
+    square = call(square_kernel, jax.ShapeDtypeStruct((chips, LANE), f32))(grad)
+    plane = jnp.sum(exchange(square), axis=0, keepdims=True)
+    turns = [
+        (f * group_count + z, f * group_count + (z + f // CORES) % group_count)
+        for f in range(fsdp_count)
+        for z in range(group_count)
+    ]
+    planes = lax.ppermute(plane, ("fsdp", "expert"), turns)
+    keep, send = call(gram_kernel, (half, half))(grad, momentum)
+    pairs = [(i, i ^ 1) for i in range(fsdp_count)]
+    both = keep + lax.ppermute(send, "fsdp", pairs)
     spread = call(
         middle_kernel, jax.ShapeDtypeStruct((chips, 3 * share + SUB, LANE), f32)
-    )(exchange(both), squares)
+    )(exchange(both), planes)
     mine = exchange(spread)
     other = lax.ppermute(mine, "fsdp", pairs)
     return call(

time: 79.2 us -> 71.7 us (0.905)
  blocking collectives: 30.3 us -> 18.9 us
  waiting for transfers between devices: 12.8 us -> 17.4 us
  starting transfers between devices: 23.9 us -> 22.1 us
  other arithmetic: 0.08 us -> 0.91 us
    all_to_all x2 -> x1, blocking collectives: 30.3 us -> 18.9 us  [exchange(): lax.all_to_all(x, 'fsdp', split_axis=0, concat_axis=0, tiled=True, axis_i...]
    all_to_all x1 -> x2, waiting for transfers between devices: 11.1 us -> 15.7 us  [exchange(): lax.all_to_all(x, 'fsdp', split_axis=0, concat_axis=0, tiled=True, axis_i...]
    all_to_all x1 -> x2, starting transfers between devices: 9.55 us -> 7.05 us  [exchange(): lax.all_to_all(x, 'fsdp', split_axis=0, concat_axis=0, tiled=True, axis_i...]
    add x1, other arithmetic: 0.08 us -> 0.88 us  [per_device(): both = keep + lax.ppermute(send, 'fsdp', pairs)]
    pallas_call x1 -> x2, Pallas kernels: 1.54 us -> 1.73 us  [the longest x1 1.01 us: per_device(): keep, send = call(gram_kernel, (half, half))(grad, momentum)]
  transfers between devices with their start and end apart: 3 -> 5, of which waited for: 2 -> 3; matrix products, arithmetic and copies ran while one was open for 0% -> 1% of each run, Pallas kernels for 0% -> 1%
where the time goes in v4:
time: 71.7 us; the launch traced here: 71.3 us
  starting transfers between devices  22.1 us (31%)
  blocking collectives  18.9 us (26%)
  waiting for transfers between devices  17.4 us (24%)
  Pallas kernels  9.27 us (13%)
  local copies, waits for them, and re-layouts  1.9 us (3%)
  other arithmetic  0.91 us (1%)
  between operations  0.73 us (1%)
    all_to_all x1, blocking collectives, exchange(): lax.all_to_all(x, 'fsdp', split_axis=0, concat_axis=0, tiled=True, axis_i...  18.9 us
    all_to_all x2, waiting for transfers between devices, exchange(): lax.all_to_all(x, 'fsdp', split_axis=0, concat_axis=0, tiled=True, axis_i...  15.7 us
    ppermute x1, starting transfers between devices, per_device(): both = keep + lax.ppermute(send, 'fsdp', pairs)  8.79 us
    pallas_call x1, Pallas kernels, per_device(): call(functools.partial(final_kernel, step_scale, count), (jax.ShapeDtypeS...  7.48 us
    all_to_all x2, starting transfers between devices, exchange(): lax.all_to_all(x, 'fsdp', split_axis=0, concat_axis=0, tiled=True, axis_i...  7.05 us
    ppermute x1, starting transfers between devices, per_device(): other = lax.ppermute(mine, 'fsdp', pairs)  5.62 us
    unnamed x8, local copies, waits for them, and re-layouts  1.9 us
    ppermute x1, waiting for transfers between devices, per_device(): other = lax.ppermute(mine, 'fsdp', pairs)  1.7 us
  transfers between devices with their start and end apart: 5, of which 3 were waited for; matrix products, arithmetic and copies ran while one was open for 1% of the time, Pallas kernels for 1%

profile of v4, /device:TPU:1, one launch (start us, length us, event | category | flops | bytes accessed | tf_op | source)
XLA Modules:
  0.0 71.3 jit_solution(4277305629021757852)
XLA Ops:
  0.6 0.0 copy-start
  0.6 0.9 %copy-done = bf16[1,224,384]{2,1,0:T(8,128)(2,1)S(1)} copy-done((bf16[1,224,384]{2,1,0:T(8,128)(2,1)S(1)}, bf16[1,224,384]{2,1,0:T(8,128)(2,1)}, u32[]{:S(2)}) %copy-start) | copy-done | bytes 172056
  1.6 0.0 copy-start.2
  1.6 1.0 %copy-done.2 = f32[1,224,384]{2,1,0:T(8,128)S(1)} copy-done((f32[1,224,384]{2,1,0:T(8,128)S(1)}, f32[1,224,384]{2,1,0:T(8,128)}, u32[]{:S(2)}) %copy-start.2) | copy-done | bytes 344088
  2.5 1.0 %shard_map.41 = (f32[16,72,128]{2,1,0:T(8,128)S(1)}, f32[16,72,128]{2,1,0:T(8,128)S(1)}) custom-call(bf16[1,224,384]{2,1,0:T(8,128)(2,1)S(1)} %copy-done, f32[1,224,384]{2,1,0:T(8,128)S(1)} %copy-done.2), custom_call_target="tpu_custom_call" | custom-call | tf_op jit(solution)/shard_map/pallas_call | solution.py:183
  3.5 8.8 %collective-permute-start = (f32[16,72,128]{2,1,0:T(8,128)S(1)}, f32[16,72,128]{2,1,0:T(8,128)S(1)}, u32[]{:S(2)}, u32[]{:S(2)}) collective-permute-start(f32[16,72,128]{2,1,0:T(8,128)S(1)} %get-tuple-element.5), channel_id=1, source_target_pairs={{0,16},{16,0},{32,48},{48,32},{64,80},{80,64},{96,112},{112,96},{1... | collective-permute-start | bytes 1769480 | tf_op jit(solution)/shard_map/ppermute | solution.py:185
  12.3 0.7 %shard_map.42 = f32[16,128]{1,0:T(8,128)} custom-call(bf16[1,224,384]{2,1,0:T(8,128)(2,1)S(1)} %copy-done), custom_call_target="tpu_custom_call" | custom-call | tf_op jit(solution)/shard_map/pallas_call | solution.py:175
  13.1 3.5 %all-to-all-start.1 = ((f32[16,1,128]{2,1,0:T(1,128)}), f32[16,1,128]{2,1,0:T(1,128)S(1)}, u32[]{:S(2)}, u32[]{:S(2)}) async-start(f32[16,1,128]{2,1,0:T(1,128)} %bitcast.1), calls=%async_computation.1 | async-start | bytes 16384 | tf_op jit(solution)/shard_map/all_to_all | solution.py:173
  16.5 0.0 collective-permute-done
  16.6 0.9 %add.3 = f32[16,72,128]{2,1,0:T(8,128)} add(f32[16,72,128]{2,1,0:T(8,128)S(1)} %get-tuple-element.4, f32[16,72,128]{2,1,0:T(8,128)S(1)} %collective-permute-done) | non-fusion elementwise | flops 147456 | bytes 1769472 | tf_op jit(solution)/shard_map/add | solution.py:185
  17.4 5.4 %all-to-all-done.1 = f32[16,1,128]{2,1,0:T(1,128)S(1)} async-done(((f32[16,1,128]{2,1,0:T(1,128)}), f32[16,1,128]{2,1,0:T(1,128)S(1)}, u32[]{:S(2)}, u32[]{:S(2)}) %all-to-all-start.1) | async-done | bytes 8224 | tf_op jit(solution)/shard_map/all_to_all | solution.py:173
  22.8 3.6 %all-to-all-start = ((f32[16,72,128]{2,1,0:T(8,128)}), f32[16,72,128]{2,1,0:T(8,128)S(1)}, u32[]{:S(2)}, u32[]{:S(2)}) async-start(f32[16,72,128]{2,1,0:T(8,128)} %add.3), calls=%async_computation | async-start | bytes 1179648 | tf_op jit(solution)/shard_map/all_to_all | solution.py:173
  26.4 0.7 collective-permute-start.1
  27.1 0.0 collective-permute-done.1.squares_ref
  27.1 10.3 %all-to-all-done.parts_ref = f32[16,72,128]{2,1,0:T(8,128)S(1)} async-done(((f32[16,72,128]{2,1,0:T(8,128)}), f32[16,72,128]{2,1,0:T(8,128)S(1)}, u32[]{:S(2)}, u32[]{:S(2)}) %all-to-all-start) | async-done | bytes 589856 | tf_op jit(solution)/shard_map/all_to_all | solution.py:173
  37.5 0.1 shard_map.43
  37.5 0.0 copy-start.1
  37.5 0.0 copy-start.3
  37.5 18.9 %all_to_all.19.mine_ref = f32[16,80,128]{2,1,0:T(8,128)S(1)} all-to-all(f32[16,80,128]{2,1,0:T(8,128)S(1)} %shard_map.43), channel_id=1, replica_groups={{0,32,64,96,128,160,192,224,256,288,320,352,384,416,448,480},{16,48,80,..., dimensions={0} | all-to-all | bytes 1310720 | tf_op jit(solution)/shard_map/all_to_all | solution.py:173
  56.4 5.6 %collective-permute-start.2 = (f32[16,80,128]{2,1,0:T(8,128)S(1)}, f32[16,80,128]{2,1,0:T(8,128)S(1)}, u32[]{:S(2)}, u32[]{:S(2)}) collective-permute-start(f32[16,80,128]{2,1,0:T(8,128)S(1)} %all_to_all.19.mine_ref), channel_id=1, source_target_pairs={{0,16},{16,0},{32,48},{48,32},{64,80},{80,64},{96,112},{112,96},{1... | collective-permute-start | bytes 1966088 | tf_op jit(solution)/shard_map/ppermute | solution.py:190
  62.1 1.7 %collective-permute-done.2.other_ref = f32[16,80,128]{2,1,0:T(8,128)S(1)} collective-permute-done((f32[16,80,128]{2,1,0:T(8,128)S(1)}, f32[16,80,128]{2,1,0:T(8,128)S(1)}, u32[]{:S(2)}, u32[]{:S(2)}) %collective-permute-start.2) | collective-permute-done | bytes 655392 | tf_op jit(solution)/shard_map/ppermute | solution.py:190
  63.8 0.0 copy-done.1
  63.8 0.0 copy-done.3
  63.8 7.5 %shard_map.44 = (f32[1,224,384]{2,1,0:T(8,128)}, bf16[1,224,384]{2,1,0:T(8,128)(2,1)}) custom-call(f32[16,80,128]{2,1,0:T(8,128)S(1)} %all_to_all.19.mine_ref, f32[16,80,128]{2,1,0:T(8,128)S(1)} %collective-permute-done.2.other_ref, bf16[1,224,384]{2,1,0:T(8,128)(2,1)S(1)} %copy-done.1, f32[1,224,384]{2,1,0:T(8,128)S(1)} %copy-done.3), custom_call_target="tpu_custom_call" | custom-call | tf_op jit(solution)/shard_map/pallas_call | solution.py:191
  (1 shorter events, 0.0 us)
Async XLA Ops:
  0.6 0.9 %copy-start = (bf16[1,224,384]{2,1,0:T(8,128)(2,1)S(1)}, bf16[1,224,384]{2,1,0:T(8,128)(2,1)}, u32[]{:S(2)}) copy-start(bf16[1,224,384]{2,1,0:T(8,128)(2,1)} %grad_ref.5) | copy-start | bytes 516100
  1.6 1.0 %copy-start.2 = (f32[1,224,384]{2,1,0:T(8,128)S(1)}, f32[1,224,384]{2,1,0:T(8,128)}, u32[]{:S(2)}) copy-start(f32[1,224,384]{2,1,0:T(8,128)} %momentum_ref.3) | copy-start | bytes 1032196
  3.5 13.0 %collective-permute-start = (f32[16,72,128]{2,1,0:T(8,128)S(1)}, f32[16,72,128]{2,1,0:T(8,128)S(1)}, u32[]{:S(2)}, u32[]{:S(2)}) collective-permute-start(f32[16,72,128]{2,1,0:T(8,128)S(1)} %get-tuple-element.5), channel_id=1, source_target_pairs={{0,16},{16,0},{32,48},{48,32},{64,80},{80,64},{96,112},{112,96},{1... | collective-permute-start | bytes 1769480 | tf_op jit(solution)/shard_map/ppermute | solution.py:185
  13.1 9.7 %all-to-all-start.1 = ((f32[16,1,128]{2,1,0:T(1,128)}), f32[16,1,128]{2,1,0:T(1,128)S(1)}, u32[]{:S(2)}, u32[]{:S(2)}) async-start(f32[16,1,128]{2,1,0:T(1,128)} %bitcast.1), calls=%async_computation.1 | async-start | bytes 16384 | tf_op jit(solution)/shard_map/all_to_all | solution.py:173
  22.8 14.6 %all-to-all-start = ((f32[16,72,128]{2,1,0:T(8,128)}), f32[16,72,128]{2,1,0:T(8,128)S(1)}, u32[]{:S(2)}, u32[]{:S(2)}) async-start(f32[16,72,128]{2,1,0:T(8,128)} %add.3), calls=%async_computation | async-start | bytes 1179648 | tf_op jit(solution)/shard_map/all_to_all | solution.py:173
  26.4 0.7 collective-permute-start.1
  37.5 26.3 %copy-start.1 = (bf16[1,224,384]{2,1,0:T(8,128)(2,1)S(1)}, bf16[1,224,384]{2,1,0:T(8,128)(2,1)}, u32[]{:S(2)}) copy-start(bf16[1,224,384]{2,1,0:T(8,128)(2,1)} %grad_ref.5) | copy-start | bytes 516100
  37.5 26.2 %copy-start.3 = (f32[1,224,384]{2,1,0:T(8,128)S(1)}, f32[1,224,384]{2,1,0:T(8,128)}, u32[]{:S(2)}) copy-start(f32[1,224,384]{2,1,0:T(8,128)} %momentum_ref.3) | copy-start | bytes 1032196
  56.4 7.3 %collective-permute-start.2 = (f32[16,80,128]{2,1,0:T(8,128)S(1)}, f32[16,80,128]{2,1,0:T(8,128)S(1)}, u32[]{:S(2)}, u32[]{:S(2)}) collective-permute-start(f32[16,80,128]{2,1,0:T(8,128)S(1)} %all_to_all.19.mine_ref), channel_id=1, source_target_pairs={{0,16},{16,0},{32,48},{48,32},{64,80},{80,64},{96,112},{112,96},{1... | collective-permute-start | bytes 1966088 | tf_op jit(solution)/shard_map/ppermute | solution.py:190

commit v5 on v4

--- a/solution.py
+++ b/solution.py
@@ -34,16 +34,21 @@
     return [(i, j) for i in range(side) for j in range(i, side)]
 
 
-def square_kernel(grad_ref, square_ref):
-    full = grad_ref[0].astype(jnp.float32)
+def gram_kernel(grad_ref, momentum_ref, keep_ref, send_ref, square_ref, grad_in, momentum_in, sems):
+    core = lax.rem(lax.axis_index("fsdp"), CORES)
+    copies = [
+        pltpu.make_async_copy(grad_ref.at[0], grad_in, sems.at[0]),
+        pltpu.make_async_copy(momentum_ref.at[0], momentum_in, sems.at[1]),
+    ]
+    for copy in copies:
+        copy.start()
+    copies[0].wait()
+    grad = grad_in[...]
+    full = grad.astype(jnp.float32)
     squares = jnp.sum(full * full, axis=0, keepdims=True)
     square_ref[...] = jnp.broadcast_to(jnp.sum(squares, axis=1, keepdims=True), square_ref.shape)
-
-
-def gram_kernel(grad_ref, momentum_ref, keep_ref, send_ref):
-    core = lax.rem(lax.axis_index("fsdp"), CORES)
-    grad = grad_ref[0]
-    high, low = split(momentum_ref[0])
+    copies[1].wait()
+    high, low = split(momentum_in[...])
     grad_t, high_t, low_t = grad.T, high.T, low.T
     grams = (
         dot(grad_t, grad),
@@ -73,17 +78,22 @@
 def middle_kernel(parts_ref, squares_ref, spread_ref):
     chips, rows, _ = parts_ref.shape
     total = jnp.sum(parts_ref[...], axis=0)
-    squares = jnp.broadcast_to(squares_ref[...], (SUB, LANE))
+    squares = jnp.broadcast_to(jnp.sum(squares_ref[...], axis=0, keepdims=True), (SUB, LANE))
     for chip in range(chips):
         spread_ref[chip, :rows, :] = total
         spread_ref[chip, rows:, :] = squares
 
 
 def product(a, b):
-    return dot(a[0], b[0]) + (dot(a[0], b[1]) + dot(a[1], b[0]))
-
-
-def final_kernel(step_scale, count, mine_ref, other_ref, grad_ref, momentum_ref, new_ref, update_ref, gram_ref):
+    order = b[0].shape[1]
+    cut = order - order % 256
+    left = jnp.concatenate([a[0], a[1][:, cut:]], axis=1)
+    rest = jnp.concatenate([b[0][cut:], jnp.zeros((order - cut, order), jnp.bfloat16)], axis=1)
+    wide = dot(left, jnp.concatenate([jnp.concatenate(b, axis=1), rest], axis=0))
+    return wide[:, :order] + (wide[:, order:] + dot(a[1][:, :cut], b[0][:cut]))
+
+
+def final_kernel(step_scale, count, mine_ref, other_ref, grad_ref, momentum_ref, new_ref, update_ref, gram_ref, new_out, sem):
     core = lax.rem(lax.axis_index("fsdp"), CORES)
     order = grad_ref.shape[2]
     chips, rows, _ = mine_ref.shape
@@ -124,7 +134,9 @@
     clip = clip[:1, :1]
     grad_full = grad_ref[0].astype(jnp.float32)
     new_momentum = BETA * momentum_ref[0] + clip * grad_full
-    new_ref[0] = new_momentum
+    new_out[...] = new_momentum
+    copy = pltpu.make_async_copy(new_out, new_ref.at[0], sem)
+    copy.start()
     direction = (clip * grad_full + BETA * new_momentum).astype(jnp.bfloat16)
 
     trace = jnp.sum(jnp.sum(trace, axis=0, keepdims=True), axis=1, keepdims=True)
@@ -146,14 +158,18 @@
             moment = product(split(product(poly_parts, moment_parts)), poly_parts)
     update = dot(direction, factor.astype(jnp.bfloat16).T)
     update_ref[0] = (step_scale * update).astype(jnp.bfloat16)
-
-
-def call(kernel, shapes, scratch=()):
+    copy.wait()
+
+
+HBM = pl.BlockSpec(memory_space=pltpu.HBM)
+
+
+def call(kernel, shapes, **specs):
     return pl.pallas_call(
         kernel,
         out_shape=shapes,
-        scratch_shapes=scratch,
         compiler_params=pltpu.CompilerParams(vmem_limit_bytes=24 * 2**20),
+        **specs,
     )
 
 
@@ -172,15 +188,24 @@
     def exchange(x):
         return lax.all_to_all(x, "fsdp", split_axis=0, concat_axis=0, tiled=True, axis_index_groups=groups)
 
-    square = call(square_kernel, jax.ShapeDtypeStruct((chips, LANE), f32))(grad)
-    plane = jnp.sum(exchange(square), axis=0, keepdims=True)
+    keep, send, square = pl.pallas_call(
+        gram_kernel,
+        out_shape=(half, half, jax.ShapeDtypeStruct((chips, LANE), f32)),
+        compiler_params=pltpu.CompilerParams(vmem_limit_bytes=60 * 2**20),
+        in_specs=[HBM, HBM],
+        scratch_shapes=[
+            pltpu.VMEM((width, order), grad.dtype),
+            pltpu.VMEM((width, order), f32),
+            pltpu.SemaphoreType.DMA((2,)),
+        ],
+    )(grad, momentum)
+    plane = exchange(square)
     turns = [
         (f * group_count + z, f * group_count + (z + f // CORES) % group_count)
         for f in range(fsdp_count)
         for z in range(group_count)
     ]
     planes = lax.ppermute(plane, ("fsdp", "expert"), turns)
-    keep, send = call(gram_kernel, (half, half))(grad, momentum)
     pairs = [(i, i ^ 1) for i in range(fsdp_count)]
     both = keep + lax.ppermute(send, "fsdp", pairs)
     spread = call(
@@ -194,7 +219,12 @@
             jax.ShapeDtypeStruct(grad.shape, f32),
             jax.ShapeDtypeStruct(grad.shape, jnp.bfloat16),
         ),
-        (pltpu.VMEM((order, order), f32),),
+        out_specs=(HBM, pl.BlockSpec(memory_space=pltpu.VMEM)),
+        scratch_shapes=[
+            pltpu.VMEM((order, order), f32),
+            pltpu.VMEM((width, order), f32),
+            pltpu.SemaphoreType.DMA,
+        ],
     )(mine, other, grad, momentum)
 
 

time: 71.7 us -> 69.7 us (0.972)
  local copies, waits for them, and re-layouts: 1.9 us -> 0.01 us
  other arithmetic: 0.91 us -> 1.97 us
  waiting for transfers between devices: 17.4 us -> 16.4 us
    unnamed x8 -> x4, local copies, waits for them, and re-layouts: 1.9 us -> 0.01 us
    pallas_call x1, Pallas kernels: 7.48 us -> 5.99 us  [per_device(): call(functools.partial(final_kernel, step_scale, count), (jax.ShapeDtypeS...]
    pallas_call x2 -> x1, Pallas kernels: 1.73 us -> 3.14 us  [per_device(): pl.pallas_call(gram_kernel, out_shape=(half, half, jax.ShapeDtypeStruct((...]
    add x1, other arithmetic: 0.88 us -> 1.97 us  [per_device(): both = keep + lax.ppermute(send, 'fsdp', pairs)]
    all_to_all x2, waiting for transfers between devices: 15.7 us -> 14.7 us  [exchange(): lax.all_to_all(x, 'fsdp', split_axis=0, concat_axis=0, tiled=True, axis_i...]
  transfers between devices with their start and end apart: 5 -> 5, of which waited for: 3 -> 3; matrix products, arithmetic and copies ran while one was open for 1% -> 3% of each run, Pallas kernels for 1% -> 0%
where the time goes in v5:
time: 69.7 us; the launch traced here: 69.3 us
  starting transfers between devices  22.1 us (32%)
  blocking collectives  18.9 us (27%)
  waiting for transfers between devices  16.4 us (24%)
  Pallas kernels  9.19 us (13%)
  other arithmetic  1.97 us (3%)
  between operations  0.72 us (1%)
    all_to_all x1, blocking collectives, exchange(): lax.all_to_all(x, 'fsdp', split_axis=0, concat_axis=0, tiled=True, axis_i...  18.9 us
    all_to_all x2, waiting for transfers between devices, exchange(): lax.all_to_all(x, 'fsdp', split_axis=0, concat_axis=0, tiled=True, axis_i...  14.7 us
    ppermute x1, starting transfers between devices, per_device(): both = keep + lax.ppermute(send, 'fsdp', pairs)  8.79 us
    all_to_all x2, starting transfers between devices, exchange(): lax.all_to_all(x, 'fsdp', split_axis=0, concat_axis=0, tiled=True, axis_i...  7.07 us
    pallas_call x1, Pallas kernels, per_device(): call(functools.partial(final_kernel, step_scale, count), (jax.ShapeDtypeS...  5.99 us
    ppermute x1, starting transfers between devices, per_device(): other = lax.ppermute(mine, 'fsdp', pairs)  5.62 us
    pallas_call x1, Pallas kernels, per_device(): pl.pallas_call(gram_kernel, out_shape=(half, half, jax.ShapeDtypeStruct((...  3.14 us
    add x1, other arithmetic, per_device(): both = keep + lax.ppermute(send, 'fsdp', pairs)  1.97 us
  transfers between devices with their start and end apart: 5, of which 3 were waited for; matrix products, arithmetic and copies ran while one was open for 3% of the time, Pallas kernels for 0%

profile of v5, /device:TPU:1, one launch (start us, length us, event | category | flops | bytes accessed | tf_op | source)
XLA Modules:
  0.0 69.3 jit_solution(17202270484370710093)
XLA Ops:
  0.6 3.1 %shard_map.41 = (f32[16,72,128]{2,1,0:T(8,128)}, f32[16,72,128]{2,1,0:T(8,128)}, f32[16,128]{1,0:T(8,128)}) custom-call(bf16[1,224,384]{2,1,0:T(8,128)(2,1)} %grad_ref.3, f32[1,224,384]{2,1,0:T(8,128)} %momentum_ref.3), custom_call_target="tpu_custom_call" | custom-call | tf_op jit(solution)/shard_map/pallas_call | solution.py:191
  3.8 8.8 %collective-permute-start = (f32[16,72,128]{2,1,0:T(8,128)}, f32[16,72,128]{2,1,0:T(8,128)S(1)}, u32[]{:S(2)}, u32[]{:S(2)}) collective-permute-start(f32[16,72,128]{2,1,0:T(8,128)} %get-tuple-element.6), channel_id=1, source_target_pairs={{0,16},{16,0},{32,48},{48,32},{64,80},{80,64},{96,112},{112,96},{1... | collective-permute-start | bytes 1769480 | tf_op jit(solution)/shard_map/ppermute | solution.py:210
  12.6 3.5 %all-to-all-start.1 = ((f32[16,1,128]{2,1,0:T(1,128)}), f32[16,1,128]{2,1,0:T(1,128)S(1)}, u32[]{:S(2)}, u32[]{:S(2)}) async-start(f32[16,1,128]{2,1,0:T(1,128)} %bitcast.5), calls=%async_computation.1 | async-start | bytes 16384 | tf_op jit(solution)/shard_map/all_to_all | solution.py:189
  16.1 0.0 collective-permute-done
  16.1 2.0 %add.3 = f32[16,72,128]{2,1,0:T(8,128)} add(f32[16,72,128]{2,1,0:T(8,128)} %get-tuple-element.5, f32[16,72,128]{2,1,0:T(8,128)S(1)} %collective-permute-done) | non-fusion elementwise | flops 147456 | bytes 1769472 | tf_op jit(solution)/shard_map/add | solution.py:210
  18.0 4.3 %all-to-all-done.1 = f32[16,1,128]{2,1,0:T(1,128)S(1)} async-done(((f32[16,1,128]{2,1,0:T(1,128)}), f32[16,1,128]{2,1,0:T(1,128)S(1)}, u32[]{:S(2)}, u32[]{:S(2)}) %all-to-all-start.1) | async-done | bytes 8224 | tf_op jit(solution)/shard_map/all_to_all | solution.py:189
  22.3 3.6 %all-to-all-start = ((f32[16,72,128]{2,1,0:T(8,128)}), f32[16,72,128]{2,1,0:T(8,128)S(1)}, u32[]{:S(2)}, u32[]{:S(2)}) async-start(f32[16,72,128]{2,1,0:T(8,128)} %add.3), calls=%async_computation | async-start | bytes 1179648 | tf_op jit(solution)/shard_map/all_to_all | solution.py:189
  25.9 0.7 collective-permute-start.1
  26.6 0.0 collective-permute-done.1.squares_ref
  26.6 10.4 %all-to-all-done.parts_ref = f32[16,72,128]{2,1,0:T(8,128)S(1)} async-done(((f32[16,72,128]{2,1,0:T(8,128)}), f32[16,72,128]{2,1,0:T(8,128)S(1)}, u32[]{:S(2)}, u32[]{:S(2)}) %all-to-all-start) | async-done | bytes 589856 | tf_op jit(solution)/shard_map/all_to_all | solution.py:189
  37.0 0.1 shard_map.42
  37.0 0.0 copy-start
  37.1 0.0 copy-start.1
  37.1 18.9 %all_to_all.22.mine_ref = f32[16,80,128]{2,1,0:T(8,128)S(1)} all-to-all(f32[16,80,128]{2,1,0:T(8,128)S(1)} %shard_map.42), channel_id=1, replica_groups={{0,32,64,96,128,160,192,224,256,288,320,352,384,416,448,480},{16,48,80,..., dimensions={0} | all-to-all | bytes 1310720 | tf_op jit(solution)/shard_map/all_to_all | solution.py:189
  56.0 5.6 %collective-permute-start.2 = (f32[16,80,128]{2,1,0:T(8,128)S(1)}, f32[16,80,128]{2,1,0:T(8,128)S(1)}, u32[]{:S(2)}, u32[]{:S(2)}) collective-permute-start(f32[16,80,128]{2,1,0:T(8,128)S(1)} %all_to_all.22.mine_ref), channel_id=1, source_target_pairs={{0,16},{16,0},{32,48},{48,32},{64,80},{80,64},{96,112},{112,96},{1... | collective-permute-start | bytes 1966088 | tf_op jit(solution)/shard_map/ppermute | solution.py:215
  61.6 1.7 %collective-permute-done.2.other_ref = f32[16,80,128]{2,1,0:T(8,128)S(1)} collective-permute-done((f32[16,80,128]{2,1,0:T(8,128)S(1)}, f32[16,80,128]{2,1,0:T(8,128)S(1)}, u32[]{:S(2)}, u32[]{:S(2)}) %collective-permute-start.2) | collective-permute-done | bytes 655392 | tf_op jit(solution)/shard_map/ppermute | solution.py:215
  63.3 0.0 copy-done
  63.3 0.0 copy-done.1
  63.3 6.0 %shard_map.43 = (f32[1,224,384]{2,1,0:T(8,128)}, bf16[1,224,384]{2,1,0:T(8,128)(2,1)}) custom-call(f32[16,80,128]{2,1,0:T(8,128)S(1)} %all_to_all.22.mine_ref, f32[16,80,128]{2,1,0:T(8,128)S(1)} %collective-permute-done.2.other_ref, bf16[1,224,384]{2,1,0:T(8,128)(2,1)S(1)} %copy-done.1, f32[1,224,384]{2,1,0:T(8,128)S(1)} %copy-done), custom_call_target="tpu_custom_call" | custom-call | tf_op jit(solution)/shard_map/pallas_call | solution.py:216
Async XLA Ops:
  3.8 12.3 %collective-permute-start = (f32[16,72,128]{2,1,0:T(8,128)}, f32[16,72,128]{2,1,0:T(8,128)S(1)}, u32[]{:S(2)}, u32[]{:S(2)}) collective-permute-start(f32[16,72,128]{2,1,0:T(8,128)} %get-tuple-element.6), channel_id=1, source_target_pairs={{0,16},{16,0},{32,48},{48,32},{64,80},{80,64},{96,112},{112,96},{1... | collective-permute-start | bytes 1769480 | tf_op jit(solution)/shard_map/ppermute | solution.py:210
  12.6 9.8 %all-to-all-start.1 = ((f32[16,1,128]{2,1,0:T(1,128)}), f32[16,1,128]{2,1,0:T(1,128)S(1)}, u32[]{:S(2)}, u32[]{:S(2)}) async-start(f32[16,1,128]{2,1,0:T(1,128)} %bitcast.5), calls=%async_computation.1 | async-start | bytes 16384 | tf_op jit(solution)/shard_map/all_to_all | solution.py:189
  22.3 14.6 %all-to-all-start = ((f32[16,72,128]{2,1,0:T(8,128)}), f32[16,72,128]{2,1,0:T(8,128)S(1)}, u32[]{:S(2)}, u32[]{:S(2)}) async-start(f32[16,72,128]{2,1,0:T(8,128)} %add.3), calls=%async_computation | async-start | bytes 1179648 | tf_op jit(solution)/shard_map/all_to_all | solution.py:189
  25.9 0.7 collective-permute-start.1
  37.0 26.3 %copy-start = (f32[1,224,384]{2,1,0:T(8,128)S(1)}, f32[1,224,384]{2,1,0:T(8,128)}, u32[]{:S(2)}) copy-start(f32[1,224,384]{2,1,0:T(8,128)} %momentum_ref.3) | copy-start | bytes 1032196
  37.1 26.3 %copy-start.1 = (bf16[1,224,384]{2,1,0:T(8,128)(2,1)S(1)}, bf16[1,224,384]{2,1,0:T(8,128)(2,1)}, u32[]{:S(2)}) copy-start(bf16[1,224,384]{2,1,0:T(8,128)(2,1)} %grad_ref.3) | copy-start | bytes 516100
  56.0 7.3 %collective-permute-start.2 = (f32[16,80,128]{2,1,0:T(8,128)S(1)}, f32[16,80,128]{2,1,0:T(8,128)S(1)}, u32[]{:S(2)}, u32[]{:S(2)}) collective-permute-start(f32[16,80,128]{2,1,0:T(8,128)S(1)} %all_to_all.22.mine_ref), channel_id=1, source_target_pairs={{0,16},{16,0},{32,48},{48,32},{64,80},{80,64},{96,112},{112,96},{1... | collective-permute-start | bytes 1966088 | tf_op jit(solution)/shard_map/ppermute | solution.py:215

commit v6 on v5

--- a/solution.py
+++ b/solution.py
@@ -18,6 +18,7 @@
 LANE = 128
 SUB = 8
 CORES = 2
+SPARE = 4
 
 
 def dot(a, b):
@@ -29,9 +30,21 @@
     return high, (x - high.astype(jnp.float32)).astype(jnp.bfloat16)
 
 
-def blocks_of(order):
-    side = order // LANE
-    return [(i, j) for i in range(side) for j in range(i, side)]
+def pairs_of(side):
+    return [(i, j) for i in range(side) for j in range(i + 1, side)]
+
+
+def places(shape):
+    return lax.broadcasted_iota(jnp.int32, shape, 0), lax.broadcasted_iota(jnp.int32, shape, 1)
+
+
+def block_of(gram, i, j):
+    return gram[i * LANE : (i + 1) * LANE, j * LANE : (j + 1) * LANE]
+
+
+def diagonal_of(block):
+    row, col = places(block.shape)
+    return jnp.sum(jnp.where(row == col, block, 0.0), axis=0, keepdims=True)
 
 
 def gram_kernel(grad_ref, momentum_ref, keep_ref, send_ref, square_ref, grad_in, momentum_in, sems):
@@ -55,33 +68,40 @@
         (dot(grad_t, high) + dot(high_t, grad)) + (dot(grad_t, low) + dot(low_t, grad)),
         dot(high_t, high) + (dot(high_t, low) + dot(low_t, high)),
     )
+    side = grad.shape[1] // LANE
+    row, col = places((LANE, LANE))
+    gg, gm, mm = [[block_of(gram, k, k) for k in range(side)] for gram in grams]
+    packed = [jnp.where(row <= col, gg[k], gm[k]) for k in range(side)]
+    packed += [jnp.where(row <= col, mm[0], mm[1]), mm[2]]
+    packed += [block_of(gram, i, j) for gram in grams for i, j in pairs_of(side)]
+    last = [diagonal_of(block) for block in gm + [mm[1]]]
+    last = jnp.concatenate(last + [jnp.zeros((SUB - len(last), LANE), jnp.float32)], axis=0)
     chips, rows, _ = keep_ref.shape
-    per_gram = rows // len(grams)
-    pieces = per_gram // SUB
-    blocks = blocks_of(grad.shape[1])
-    for which, gram in enumerate(grams):
-
-        def piece(q):
-            i, j = blocks[q // (LANE // SUB)]
-            top = i * LANE + q % (LANE // SUB) * SUB
-            return gram[top : top + SUB, j * LANE : (j + 1) * LANE]
-
-        for chip in range(chips):
-            for p in range(pieces):
-                first = piece((chip * CORES) * pieces + p)
-                second = piece((chip * CORES + 1) * pieces + p)
-                at = pl.ds(which * per_gram + p * SUB, SUB)
-                keep_ref[chip, at, :] = jnp.where(core == 0, first, second)
-                send_ref[chip, at, :] = jnp.where(core == 0, second, first)
+    pieces = rows // SUB - 1
+
+    def piece(q):
+        top = q % (LANE // SUB) * SUB
+        return packed[q // (LANE // SUB)][top : top + SUB]
+
+    for chip in range(chips):
+        for p in range(pieces):
+            first = piece((chip * CORES) * pieces + p)
+            second = piece((chip * CORES + 1) * pieces + p)
+            keep_ref[chip, p * SUB : (p + 1) * SUB, :] = jnp.where(core == 0, first, second)
+            send_ref[chip, p * SUB : (p + 1) * SUB, :] = jnp.where(core == 0, second, first)
+        keep_ref[chip, pieces * SUB :, :] = last
+        send_ref[chip, pieces * SUB :, :] = last
 
 
 def middle_kernel(parts_ref, squares_ref, spread_ref):
     chips, rows, _ = parts_ref.shape
     total = jnp.sum(parts_ref[...], axis=0)
-    squares = jnp.broadcast_to(jnp.sum(squares_ref[...], axis=0, keepdims=True), (SUB, LANE))
+    squares = jnp.sum(squares_ref[...], axis=0, keepdims=True)
+    row, _ = places((SUB, LANE))
+    last = jnp.where(row == SPARE, squares, total[rows - SUB :])
     for chip in range(chips):
-        spread_ref[chip, :rows, :] = total
-        spread_ref[chip, rows:, :] = squares
+        spread_ref[chip, : rows - SUB, :] = total[: rows - SUB]
+        spread_ref[chip, rows - SUB :, :] = last
 
 
 def product(a, b):
@@ -93,43 +113,55 @@
     return wide[:, :order] + (wide[:, order:] + dot(a[1][:, :cut], b[0][:cut]))
 
 
-def final_kernel(step_scale, count, mine_ref, other_ref, grad_ref, momentum_ref, new_ref, update_ref, gram_ref, new_out, sem):
+def final_kernel(step_scale, count, mine_ref, other_ref, grad_ref, momentum_ref, new_ref, update_ref, packed_ref, gram_ref, new_out, sem):
     core = lax.rem(lax.axis_index("fsdp"), CORES)
     order = grad_ref.shape[2]
+    side = order // LANE
     chips, rows, _ = mine_ref.shape
-    per_gram = (rows - SUB) // 3
-    pieces = per_gram // SUB
-    squares = jnp.sum(mine_ref[:, rows - SUB :, :], axis=0) + jnp.sum(other_ref[:, rows - SUB :, :], axis=0)
+    pieces = rows // SUB - 1
+    squares = jnp.zeros((1, LANE), jnp.float32)
+    for ref in (mine_ref, other_ref):
+        squares = squares + jnp.sum(ref[:, rows - SUB :, :], axis=0)[SPARE : SPARE + 1]
     clip = 1.0 / jnp.sqrt(squares / count + 1e-06)
     alpha = (1.0 + BETA) * clip
     some = alpha > 0.0
     gain_gg, gain_gm, gain_mm = alpha * alpha, alpha * (BETA * BETA), BETA**4
-    blocks = blocks_of(order)
-    trace = jnp.zeros((SUB, LANE), jnp.float32)
+
+    def grown(gain, block):
+        return jnp.where(some, gain * block, 0.0)
+
     for chip in range(chips):
         for p in range(pieces):
-            at = [pl.ds(which * per_gram + p * SUB, SUB) for which in range(3)]
-            held = [mine_ref[chip, a, :] for a in at]
-            came = [other_ref[chip, a, :] for a in at]
-
-            def joined(gg, gm, mm):
-                return jnp.where(some, gain_gg * gg + gain_gm * gm, 0.0) + gain_mm * mm
-
-            held, came = joined(*held), joined(*came)
-            for c, piece in ((0, jnp.where(core == 0, held, came)), (1, jnp.where(core == 0, came, held))):
+            held = mine_ref[chip, p * SUB : (p + 1) * SUB, :]
+            came = other_ref[chip, p * SUB : (p + 1) * SUB, :]
+            for c, value in ((0, jnp.where(core == 0, held, came)), (1, jnp.where(core == 0, came, held))):
                 q = (chip * CORES + c) * pieces + p
-                i, j = blocks[q // (LANE // SUB)]
-                down = q % (LANE // SUB) * SUB
-                gram_ref[i * LANE + down : i * LANE + down + SUB, j * LANE : (j + 1) * LANE] = piece
-                if i == j:
-                    row = lax.broadcasted_iota(jnp.int32, (SUB, LANE), 0) + down
-                    col = lax.broadcasted_iota(jnp.int32, (SUB, LANE), 1)
-                    trace = trace + jnp.where(row == col, piece, 0.0)
-    for i, j in blocks:
-        if i < j:
-            gram_ref[j * LANE : (j + 1) * LANE, i * LANE : (i + 1) * LANE] = gram_ref[
-                i * LANE : (i + 1) * LANE, j * LANE : (j + 1) * LANE
-            ].T
+                packed_ref[q * SUB : (q + 1) * SUB, :] = value
+    blocks = [packed_ref[k * LANE : (k + 1) * LANE, :] for k in range(packed_ref.shape[0] // LANE)]
+    last = mine_ref[0, rows - SUB :, :]
+    row, col = places((LANE, LANE))
+    upper = jnp.where(row == col, 0.5, jnp.where(row < col, 1.0, 0.0))
+    lower = jnp.where(row > col, 1.0, 0.0)
+    half = jnp.where(row == col, 0.5, 0.0)
+    trace = jnp.zeros((1, LANE), jnp.float32)
+    for k in range(side):
+        both = jnp.where(row > col, grown(gain_gm, blocks[k]), grown(gain_gg, blocks[k]) * jnp.where(row == col, 0.5, 1.0))
+        both = both + half * grown(gain_gm, last[k : k + 1])
+        if k == 0:
+            both = both + gain_mm * (upper * blocks[side])
+        elif k == 1:
+            both = both + gain_mm * (lower * blocks[side] + half * last[side : side + 1])
+        else:
+            both = both + (0.5 * gain_mm) * blocks[side + 1]
+        both = both + both.T
+        trace = trace + diagonal_of(both)
+        gram_ref[k * LANE : (k + 1) * LANE, k * LANE : (k + 1) * LANE] = both
+    pairs = pairs_of(side)
+    for n, (i, j) in enumerate(pairs):
+        gg, gm, mm = [blocks[side + 2 + which * len(pairs) + n] for which in range(3)]
+        block = grown(gain_gg, gg) + grown(gain_gm, gm) + gain_mm * mm
+        gram_ref[i * LANE : (i + 1) * LANE, j * LANE : (j + 1) * LANE] = block
+        gram_ref[j * LANE : (j + 1) * LANE, i * LANE : (i + 1) * LANE] = block.T
 
     clip = clip[:1, :1]
     grad_full = grad_ref[0].astype(jnp.float32)
@@ -139,7 +171,7 @@
     copy.start()
     direction = (clip * grad_full + BETA * new_momentum).astype(jnp.bfloat16)
 
-    trace = jnp.sum(jnp.sum(trace, axis=0, keepdims=True), axis=1, keepdims=True)
+    trace = jnp.sum(trace, axis=1, keepdims=True)
     norm_inv = 1.0 / (jnp.sqrt(trace) + 1e-07)
     moment = gram_ref[...] * (norm_inv * norm_inv)
     row = lax.broadcasted_iota(jnp.int32, (order, order), 0)
@@ -180,9 +212,11 @@
     step_scale = 0.2 * math.sqrt(max(order, width * fsdp_count))
     count = grad.size * fsdp_count * group_count
     chips = fsdp_count // CORES
-    share = len(blocks_of(order)) * LANE // fsdp_count
+    side = order // LANE
+    packed = (side + 2 + 3 * len(pairs_of(side))) * LANE
+    share = packed // fsdp_count + SUB
     f32 = jnp.float32
-    half = jax.ShapeDtypeStruct((chips, 3 * share, LANE), f32)
+    half = jax.ShapeDtypeStruct((chips, share, LANE), f32)
     groups = [[CORES * i + c for i in range(chips)] for c in range(CORES)]
 
     def exchange(x):
@@ -209,7 +243,7 @@
     pairs = [(i, i ^ 1) for i in range(fsdp_count)]
     both = keep + lax.ppermute(send, "fsdp", pairs)
     spread = call(
-        middle_kernel, jax.ShapeDtypeStruct((chips, 3 * share + SUB, LANE), f32)
+        middle_kernel, half
     )(exchange(both), planes)
     mine = exchange(spread)
     other = lax.ppermute(mine, "fsdp", pairs)
@@ -221,6 +255,7 @@
         ),
         out_specs=(HBM, pl.BlockSpec(memory_space=pltpu.VMEM)),
         scratch_shapes=[
+            pltpu.VMEM((packed, LANE), f32),
             pltpu.VMEM((order, order), f32),
             pltpu.VMEM((width, order), f32),
             pltpu.SemaphoreType.DMA,

time: 69.7 us -> 68.6 us (0.984)
  waiting for transfers between devices: 16.4 us -> 15.6 us
where the time goes in v6:
time: 68.6 us; the launch traced here: 68.2 us
  starting transfers between devices  22.4 us (33%)
  blocking collectives  18.4 us (27%)
  waiting for transfers between devices  15.6 us (23%)
  Pallas kernels  9.16 us (13%)
  other arithmetic  1.9 us (3%)
  between operations  0.72 us (1%)
    all_to_all x1, blocking collectives, exchange(): lax.all_to_all(x, 'fsdp', split_axis=0, concat_axis=0, tiled=True, axis_i...  18.4 us
    all_to_all x2, waiting for transfers between devices, exchange(): lax.all_to_all(x, 'fsdp', split_axis=0, concat_axis=0, tiled=True, axis_i...  14.1 us
    ppermute x1, starting transfers between devices, per_device(): both = keep + lax.ppermute(send, 'fsdp', pairs)  8.79 us
    all_to_all x2, starting transfers between devices, exchange(): lax.all_to_all(x, 'fsdp', split_axis=0, concat_axis=0, tiled=True, axis_i...  7.05 us
    pallas_call x1, Pallas kernels, per_device(): call(functools.partial(final_kernel, step_scale, count), (jax.ShapeDtypeS...  6.03 us
    ppermute x1, starting transfers between devices, per_device(): other = lax.ppermute(mine, 'fsdp', pairs)  5.9 us
    pallas_call x1, Pallas kernels, per_device(): pl.pallas_call(gram_kernel, out_shape=(half, half, jax.ShapeDtypeStruct((...  3.07 us
    add x1, other arithmetic, per_device(): both = keep + lax.ppermute(send, 'fsdp', pairs)  1.9 us
  transfers between devices with their start and end apart: 5, of which 3 were waited for; matrix products, arithmetic and copies ran while one was open for 3% of the time, Pallas kernels for 0%

profile of v6, /device:TPU:1, one launch (start us, length us, event | category | flops | bytes accessed | tf_op | source)
XLA Modules:
  0.0 68.2 jit_solution(17441301607511788930)
XLA Ops:
  0.6 3.1 %shard_map.41 = (f32[16,64,128]{2,1,0:T(8,128)}, f32[16,64,128]{2,1,0:T(8,128)}, f32[16,128]{1,0:T(8,128)}) custom-call(bf16[1,224,384]{2,1,0:T(8,128)(2,1)} %grad_ref.3, f32[1,224,384]{2,1,0:T(8,128)} %momentum_ref.3), custom_call_target="tpu_custom_call" | custom-call | tf_op jit(solution)/shard_map/pallas_call | solution.py:225
  3.7 8.8 %collective-permute-start = (f32[16,64,128]{2,1,0:T(8,128)}, f32[16,64,128]{2,1,0:T(8,128)S(1)}, u32[]{:S(2)}, u32[]{:S(2)}) collective-permute-start(f32[16,64,128]{2,1,0:T(8,128)} %get-tuple-element.6), channel_id=1, source_target_pairs={{0,16},{16,0},{32,48},{48,32},{64,80},{80,64},{96,112},{112,96},{1... | collective-permute-start | bytes 1572872 | tf_op jit(solution)/shard_map/ppermute | solution.py:244
  12.5 3.5 %all-to-all-start.1 = ((f32[16,1,128]{2,1,0:T(1,128)}), f32[16,1,128]{2,1,0:T(1,128)S(1)}, u32[]{:S(2)}, u32[]{:S(2)}) async-start(f32[16,1,128]{2,1,0:T(1,128)} %bitcast.5), calls=%async_computation.1 | async-start | bytes 16384 | tf_op jit(solution)/shard_map/all_to_all | solution.py:223
  16.0 0.0 collective-permute-done
  16.0 1.9 %add.3 = f32[16,64,128]{2,1,0:T(8,128)} add(f32[16,64,128]{2,1,0:T(8,128)} %get-tuple-element.5, f32[16,64,128]{2,1,0:T(8,128)S(1)} %collective-permute-done) | non-fusion elementwise | flops 131072 | bytes 1572864 | tf_op jit(solution)/shard_map/add | solution.py:244
  17.9 4.4 %all-to-all-done.1 = f32[16,1,128]{2,1,0:T(1,128)S(1)} async-done(((f32[16,1,128]{2,1,0:T(1,128)}), f32[16,1,128]{2,1,0:T(1,128)S(1)}, u32[]{:S(2)}, u32[]{:S(2)}) %all-to-all-start.1) | async-done | bytes 8224 | tf_op jit(solution)/shard_map/all_to_all | solution.py:223
  22.3 3.6 %all-to-all-start = ((f32[16,64,128]{2,1,0:T(8,128)}), f32[16,64,128]{2,1,0:T(8,128)S(1)}, u32[]{:S(2)}, u32[]{:S(2)}) async-start(f32[16,64,128]{2,1,0:T(8,128)} %add.3), calls=%async_computation | async-start | bytes 1048576 | tf_op jit(solution)/shard_map/all_to_all | solution.py:223
  25.8 0.7 collective-permute-start.1
  26.5 0.0 collective-permute-done.1.squares_ref
  26.5 9.7 %all-to-all-done.parts_ref = f32[16,64,128]{2,1,0:T(8,128)S(1)} async-done(((f32[16,64,128]{2,1,0:T(8,128)}), f32[16,64,128]{2,1,0:T(8,128)S(1)}, u32[]{:S(2)}, u32[]{:S(2)}) %all-to-all-start) | async-done | bytes 524320 | tf_op jit(solution)/shard_map/all_to_all | solution.py:223
  36.3 0.1 shard_map.42
  36.3 0.0 copy-start
  36.3 0.0 copy-start.1
  36.3 18.4 %all_to_all.22.mine_ref = f32[16,64,128]{2,1,0:T(8,128)S(1)} all-to-all(f32[16,64,128]{2,1,0:T(8,128)S(1)} %shard_map.42), channel_id=1, replica_groups={{0,32,64,96,128,160,192,224,256,288,320,352,384,416,448,480},{16,48,80,..., dimensions={0} | all-to-all | bytes 1048576 | tf_op jit(solution)/shard_map/all_to_all | solution.py:223
  54.8 5.9 %collective-permute-start.2 = (f32[16,64,128]{2,1,0:T(8,128)S(1)}, f32[16,64,128]{2,1,0:T(8,128)S(1)}, u32[]{:S(2)}, u32[]{:S(2)}) collective-permute-start(f32[16,64,128]{2,1,0:T(8,128)S(1)} %all_to_all.22.mine_ref), channel_id=1, source_target_pairs={{0,16},{16,0},{32,48},{48,32},{64,80},{80,64},{96,112},{112,96},{1... | collective-permute-start | bytes 1572872 | tf_op jit(solution)/shard_map/ppermute | solution.py:249
  60.7 1.5 %collective-permute-done.2.other_ref = f32[16,64,128]{2,1,0:T(8,128)S(1)} collective-permute-done((f32[16,64,128]{2,1,0:T(8,128)S(1)}, f32[16,64,128]{2,1,0:T(8,128)S(1)}, u32[]{:S(2)}, u32[]{:S(2)}) %collective-permute-start.2) | collective-permute-done | bytes 524320 | tf_op jit(solution)/shard_map/ppermute | solution.py:249
  62.2 0.0 copy-done
  62.2 0.0 copy-done.1
  62.2 6.0 %shard_map.43 = (f32[1,224,384]{2,1,0:T(8,128)}, bf16[1,224,384]{2,1,0:T(8,128)(2,1)}) custom-call(f32[16,64,128]{2,1,0:T(8,128)S(1)} %all_to_all.22.mine_ref, f32[16,64,128]{2,1,0:T(8,128)S(1)} %collective-permute-done.2.other_ref, bf16[1,224,384]{2,1,0:T(8,128)(2,1)S(1)} %copy-done.1, f32[1,224,384]{2,1,0:T(8,128)S(1)} %copy-done), custom_call_target="tpu_custom_call" | custom-call | tf_op jit(solution)/shard_map/pallas_call | solution.py:250
Async XLA Ops:
  3.7 12.3 %collective-permute-start = (f32[16,64,128]{2,1,0:T(8,128)}, f32[16,64,128]{2,1,0:T(8,128)S(1)}, u32[]{:S(2)}, u32[]{:S(2)}) collective-permute-start(f32[16,64,128]{2,1,0:T(8,128)} %get-tuple-element.6), channel_id=1, source_target_pairs={{0,16},{16,0},{32,48},{48,32},{64,80},{80,64},{96,112},{112,96},{1... | collective-permute-start | bytes 1572872 | tf_op jit(solution)/shard_map/ppermute | solution.py:244
  12.5 9.8 %all-to-all-start.1 = ((f32[16,1,128]{2,1,0:T(1,128)}), f32[16,1,128]{2,1,0:T(1,128)S(1)}, u32[]{:S(2)}, u32[]{:S(2)}) async-start(f32[16,1,128]{2,1,0:T(1,128)} %bitcast.5), calls=%async_computation.1 | async-start | bytes 16384 | tf_op jit(solution)/shard_map/all_to_all | solution.py:223
  22.3 14.0 %all-to-all-start = ((f32[16,64,128]{2,1,0:T(8,128)}), f32[16,64,128]{2,1,0:T(8,128)S(1)}, u32[]{:S(2)}, u32[]{:S(2)}) async-start(f32[16,64,128]{2,1,0:T(8,128)} %add.3), calls=%async_computation | async-start | bytes 1048576 | tf_op jit(solution)/shard_map/all_to_all | solution.py:223
  25.8 0.7 collective-permute-start.1
  36.3 25.9 %copy-start = (f32[1,224,384]{2,1,0:T(8,128)S(1)}, f32[1,224,384]{2,1,0:T(8,128)}, u32[]{:S(2)}) copy-start(f32[1,224,384]{2,1,0:T(8,128)} %momentum_ref.3) | copy-start | bytes 1032196
  36.3 25.8 %copy-start.1 = (bf16[1,224,384]{2,1,0:T(8,128)(2,1)S(1)}, bf16[1,224,384]{2,1,0:T(8,128)(2,1)}, u32[]{:S(2)}) copy-start(bf16[1,224,384]{2,1,0:T(8,128)(2,1)} %grad_ref.3) | copy-start | bytes 516100
  54.8 7.4 %collective-permute-start.2 = (f32[16,64,128]{2,1,0:T(8,128)S(1)}, f32[16,64,128]{2,1,0:T(8,128)S(1)}, u32[]{:S(2)}, u32[]{:S(2)}) collective-permute-start(f32[16,64,128]{2,1,0:T(8,128)S(1)} %all_to_all.22.mine_ref), channel_id=1, source_target_pairs={{0,16},{16,0},{32,48},{48,32},{64,80},{80,64},{96,112},{112,96},{1... | collective-permute-start | bytes 1572872 | tf_op jit(solution)/shard_map/ppermute | solution.py:249

commit v7 on v6

--- a/solution.py
+++ b/solution.py
@@ -47,20 +47,22 @@
     return jnp.sum(jnp.where(row == col, block, 0.0), axis=0, keepdims=True)
 
 
-def gram_kernel(grad_ref, momentum_ref, keep_ref, send_ref, square_ref, grad_in, momentum_in, sems):
-    core = lax.rem(lax.axis_index("fsdp"), CORES)
+def square_kernel(grad_ref, square_ref):
+    full = grad_ref[0].astype(jnp.float32)
+    squares = jnp.sum(full * full, axis=0, keepdims=True)
+    square_ref[...] = jnp.broadcast_to(jnp.sum(squares, axis=1, keepdims=True), square_ref.shape)
+
+
+def gram_kernel(grad_ref, momentum_ref, parts_ref, grad_in, momentum_in, sems):
     copies = [
         pltpu.make_async_copy(grad_ref.at[0], grad_in, sems.at[0]),
         pltpu.make_async_copy(momentum_ref.at[0], momentum_in, sems.at[1]),
     ]
     for copy in copies:
         copy.start()
-    copies[0].wait()
+    for copy in copies:
+        copy.wait()
     grad = grad_in[...]
-    full = grad.astype(jnp.float32)
-    squares = jnp.sum(full * full, axis=0, keepdims=True)
-    square_ref[...] = jnp.broadcast_to(jnp.sum(squares, axis=1, keepdims=True), square_ref.shape)
-    copies[1].wait()
     high, low = split(momentum_in[...])
     grad_t, high_t, low_t = grad.T, high.T, low.T
     grams = (
@@ -76,25 +78,18 @@
     packed += [block_of(gram, i, j) for gram in grams for i, j in pairs_of(side)]
     last = [diagonal_of(block) for block in gm + [mm[1]]]
     last = jnp.concatenate(last + [jnp.zeros((SUB - len(last), LANE), jnp.float32)], axis=0)
-    chips, rows, _ = keep_ref.shape
+    devices, rows, _ = parts_ref.shape
     pieces = rows // SUB - 1
-
-    def piece(q):
-        top = q % (LANE // SUB) * SUB
-        return packed[q // (LANE // SUB)][top : top + SUB]
-
-    for chip in range(chips):
+    for device in range(devices):
         for p in range(pieces):
-            first = piece((chip * CORES) * pieces + p)
-            second = piece((chip * CORES + 1) * pieces + p)
-            keep_ref[chip, p * SUB : (p + 1) * SUB, :] = jnp.where(core == 0, first, second)
-            send_ref[chip, p * SUB : (p + 1) * SUB, :] = jnp.where(core == 0, second, first)
-        keep_ref[chip, pieces * SUB :, :] = last
-        send_ref[chip, pieces * SUB :, :] = last
+            q = device * pieces + p
+            top = q % (LANE // SUB) * SUB
+            parts_ref[device, p * SUB : (p + 1) * SUB, :] = packed[q // (LANE // SUB)][top : top + SUB]
+        parts_ref[device, pieces * SUB :, :] = last
 
 
 def middle_kernel(parts_ref, squares_ref, spread_ref):
-    chips, rows, _ = parts_ref.shape
+    chips, rows, _ = spread_ref.shape
     total = jnp.sum(parts_ref[...], axis=0)
     squares = jnp.sum(squares_ref[...], axis=0, keepdims=True)
     row, _ = places((SUB, LANE))
@@ -217,14 +212,22 @@
     share = packed // fsdp_count + SUB
     f32 = jnp.float32
     half = jax.ShapeDtypeStruct((chips, share, LANE), f32)
+    pairs = [(i, i ^ 1) for i in range(fsdp_count)]
     groups = [[CORES * i + c for i in range(chips)] for c in range(CORES)]
 
-    def exchange(x):
-        return lax.all_to_all(x, "fsdp", split_axis=0, concat_axis=0, tiled=True, axis_index_groups=groups)
-
-    keep, send, square = pl.pallas_call(
+    def exchange(x, members=None):
+        return lax.all_to_all(x, "fsdp", split_axis=0, concat_axis=0, tiled=True, axis_index_groups=members)
+
+    turns = [
+        (f * group_count + z, f * group_count + (z + f // CORES) % group_count)
+        for f in range(fsdp_count)
+        for z in range(group_count)
+    ]
+    square = call(square_kernel, jax.ShapeDtypeStruct((chips, LANE), f32))(grad)
+    planes = lax.ppermute(exchange(square, members=groups), ("fsdp", "expert"), turns)
+    parts = pl.pallas_call(
         gram_kernel,
-        out_shape=(half, half, jax.ShapeDtypeStruct((chips, LANE), f32)),
+        out_shape=jax.ShapeDtypeStruct((fsdp_count, share, LANE), f32),
         compiler_params=pltpu.CompilerParams(vmem_limit_bytes=60 * 2**20),
         in_specs=[HBM, HBM],
         scratch_shapes=[
@@ -233,19 +236,11 @@
             pltpu.SemaphoreType.DMA((2,)),
         ],
     )(grad, momentum)
-    plane = exchange(square)
-    turns = [
-        (f * group_count + z, f * group_count + (z + f // CORES) % group_count)
-        for f in range(fsdp_count)
-        for z in range(group_count)
-    ]
-    planes = lax.ppermute(plane, ("fsdp", "expert"), turns)
-    pairs = [(i, i ^ 1) for i in range(fsdp_count)]
-    both = keep + lax.ppermute(send, "fsdp", pairs)
+    parts = exchange(parts)
     spread = call(
         middle_kernel, half
-    )(exchange(both), planes)
-    mine = exchange(spread)
+    )(parts, planes)
+    mine = exchange(spread, members=groups)
     other = lax.ppermute(mine, "fsdp", pairs)
     return call(
         functools.partial(final_kernel, step_scale, count),

time: 68.6 us -> 66.5 us (0.969)
  waiting for transfers between devices: 15.6 us -> 21.4 us
  blocking collectives: 18.4 us -> 13.4 us
  starting transfers between devices: 22.4 us -> 19.8 us
  other arithmetic: 1.9 us -> 0 us
  local copies, waits for them, and re-layouts: 0.01 us -> 0.93 us
  Pallas kernels: 9.16 us -> 9.91 us
    ppermute x2 -> x1, starting transfers between devices: 9.45 us -> 0.66 us  [per_device(): lax.ppermute(exchange(square, members=groups), ('fsdp', 'expert'), turns)]
    all_to_all x2, starting transfers between devices: 7.05 us -> 15 us  [exchange(): lax.all_to_all(x, 'fsdp', split_axis=0, concat_axis=0, tiled=True, axis_i...]
    all_to_all x2, waiting for transfers between devices: 14.1 us -> 19.9 us  [exchange(): lax.all_to_all(x, 'fsdp', split_axis=0, concat_axis=0, tiled=True, axis_i...]
    all_to_all x1, blocking collectives: 18.4 us -> 13.4 us  [exchange(): lax.all_to_all(x, 'fsdp', split_axis=0, concat_axis=0, tiled=True, axis_i...]
    add x1 -> x0, other arithmetic: 1.9 us -> none  [per_device(): both = keep + lax.ppermute(send, 'fsdp', pairs)]
    ppermute x1, starting transfers between devices: 5.9 us -> 4.16 us  [per_device(): other = lax.ppermute(mine, 'fsdp', pairs)]
    unnamed x4 -> x6, local copies, waits for them, and re-layouts: 0.01 us -> 0.93 us
    pallas_call x2 -> x3, Pallas kernels: 3.13 us -> 3.88 us  [the longest x1 3.07 us: per_device(): pl.pallas_call(gram_kernel, out_shape=jax.ShapeDtypeStruct((fsdp_count, s...]
  transfers between devices with their start and end apart: 5 -> 4, of which waited for: 3 -> 3; matrix products, arithmetic and copies ran while one was open for 3% -> 0% of each run, Pallas kernels for 0% -> 5%
where the time goes in v7:
time: 66.5 us; the launch traced here: 66.1 us
  waiting for transfers between devices  21.4 us (32%)
  starting transfers between devices  19.8 us (30%)
  blocking collectives  13.4 us (20%)
  Pallas kernels  9.91 us (15%)
  local copies, waits for them, and re-layouts  0.93 us (1%)
  between operations  0.71 us (1%)
    all_to_all x2, waiting for transfers between devices, exchange(): lax.all_to_all(x, 'fsdp', split_axis=0, concat_axis=0, tiled=True, axis_i...  19.9 us
    all_to_all x2, starting transfers between devices, exchange(): lax.all_to_all(x, 'fsdp', split_axis=0, concat_axis=0, tiled=True, axis_i...  15 us
    all_to_all x1, blocking collectives, exchange(): lax.all_to_all(x, 'fsdp', split_axis=0, concat_axis=0, tiled=True, axis_i...  13.4 us
    pallas_call x1, Pallas kernels, per_device(): call(functools.partial(final_kernel, step_scale, count), (jax.ShapeDtypeS...  6.03 us
    ppermute x1, starting transfers between devices, per_device(): other = lax.ppermute(mine, 'fsdp', pairs)  4.16 us
    pallas_call x1, Pallas kernels, per_device(): pl.pallas_call(gram_kernel, out_shape=jax.ShapeDtypeStruct((fsdp_count, s...  3.07 us
    ppermute x1, waiting for transfers between devices, per_device(): other = lax.ppermute(mine, 'fsdp', pairs)  1.51 us
  transfers between devices with their start and end apart: 4, of which 3 were waited for; matrix products, arithmetic and copies ran while one was open for 0% of the time, Pallas kernels for 5%

profile of v7, /device:TPU:1, one launch (start us, length us, event | category | flops | bytes accessed | tf_op | source)
XLA Modules:
  0.0 66.1 jit_solution(1140826826039726790)
XLA Ops:
  0.6 0.0 copy-start
  0.6 0.9 %copy-done = bf16[1,224,384]{2,1,0:T(8,128)(2,1)S(1)} copy-done((bf16[1,224,384]{2,1,0:T(8,128)(2,1)S(1)}, bf16[1,224,384]{2,1,0:T(8,128)(2,1)}, u32[]{:S(2)}) %copy-start) | copy-done | bytes 172056
  1.6 0.7 %shard_map.42 = f32[16,128]{1,0:T(8,128)} custom-call(bf16[1,224,384]{2,1,0:T(8,128)(2,1)S(1)} %copy-done), custom_call_target="tpu_custom_call" | custom-call | tf_op jit(solution)/shard_map/pallas_call | solution.py:226
  2.3 7.6 %all-to-all-start.1 = ((f32[16,1,128]{2,1,0:T(1,128)}), f32[16,1,128]{2,1,0:T(1,128)S(1)}, u32[]{:S(2)}, u32[]{:S(2)}) async-start(f32[16,1,128]{2,1,0:T(1,128)} %bitcast.1), calls=%async_computation.1 | async-start | bytes 16384 | tf_op jit(solution)/shard_map/all_to_all | solution.py:219
  9.9 3.1 %shard_map.41 = f32[32,64,128]{2,1,0:T(8,128)} custom-call(bf16[1,224,384]{2,1,0:T(8,128)(2,1)} %grad_ref.5, f32[1,224,384]{2,1,0:T(8,128)} %momentum_ref.3), custom_call_target="tpu_custom_call" | custom-call | tf_op jit(solution)/shard_map/pallas_call | solution.py:228
  12.9 3.3 %all-to-all-done.1 = f32[16,1,128]{2,1,0:T(1,128)S(1)} async-done(((f32[16,1,128]{2,1,0:T(1,128)}), f32[16,1,128]{2,1,0:T(1,128)S(1)}, u32[]{:S(2)}, u32[]{:S(2)}) %all-to-all-start.1) | async-done | bytes 8224 | tf_op jit(solution)/shard_map/all_to_all | solution.py:219
  16.2 7.4 %all-to-all-start = ((f32[32,64,128]{2,1,0:T(8,128)}), f32[32,64,128]{2,1,0:T(8,128)S(1)}, u32[]{:S(2)}, u32[]{:S(2)}) async-start(f32[32,64,128]{2,1,0:T(8,128)} %shard_map.41), calls=%async_computation | async-start | bytes 2097152 | tf_op jit(solution)/shard_map/all_to_all | solution.py:219
  23.6 0.7 %collective-permute-start = (f32[16,128]{1,0:T(8,128)S(1)}, f32[16,128]{1,0:T(8,128)S(1)}, u32[]{:S(2)}, u32[]{:S(2)}) collective-permute-start(f32[16,128]{1,0:T(8,128)S(1)} %bitcast.4), channel_id=1, source_target_pairs={{0,0},{1,1},{2,2},{3,3},{4,4},{5,5},{6,6},{7,7},{8,8},{9,9},{10,10... | collective-permute-start | bytes 24584 | tf_op jit(solution)/shard_map/ppermute | solution.py:227
  24.3 0.0 collective-permute-done.squares_ref
  24.3 16.6 %all-to-all-done.parts_ref = f32[32,64,128]{2,1,0:T(8,128)S(1)} async-done(((f32[32,64,128]{2,1,0:T(8,128)}), f32[32,64,128]{2,1,0:T(8,128)S(1)}, u32[]{:S(2)}, u32[]{:S(2)}) %all-to-all-start) | async-done | bytes 1048608 | tf_op jit(solution)/shard_map/all_to_all | solution.py:219
  40.9 0.1 shard_map.43
  41.0 0.0 copy-start.1
  41.0 0.0 copy-start.2
  41.0 13.4 %all_to_all.22.mine_ref = f32[16,64,128]{2,1,0:T(8,128)S(1)} all-to-all(f32[16,64,128]{2,1,0:T(8,128)S(1)} %shard_map.43), channel_id=1, replica_groups={{0,32,64,96,128,160,192,224,256,288,320,352,384,416,448,480},{16,48,80,..., dimensions={0} | all-to-all | bytes 1048576 | tf_op jit(solution)/shard_map/all_to_all | solution.py:219
  54.4 4.2 %collective-permute-start.1 = (f32[16,64,128]{2,1,0:T(8,128)S(1)}, f32[16,64,128]{2,1,0:T(8,128)S(1)}, u32[]{:S(2)}, u32[]{:S(2)}) collective-permute-start(f32[16,64,128]{2,1,0:T(8,128)S(1)} %all_to_all.22.mine_ref), channel_id=1, source_target_pairs={{0,16},{16,0},{32,48},{48,32},{64,80},{80,64},{96,112},{112,96},{1... | collective-permute-start | bytes 1572872 | tf_op jit(solution)/shard_map/ppermute | solution.py:244
  58.6 1.5 %collective-permute-done.1.other_ref = f32[16,64,128]{2,1,0:T(8,128)S(1)} collective-permute-done((f32[16,64,128]{2,1,0:T(8,128)S(1)}, f32[16,64,128]{2,1,0:T(8,128)S(1)}, u32[]{:S(2)}, u32[]{:S(2)}) %collective-permute-start.1) | collective-permute-done | bytes 524320 | tf_op jit(solution)/shard_map/ppermute | solution.py:244
  60.1 0.0 copy-done.1
  60.1 0.0 copy-done.2
  60.1 6.0 %shard_map.44 = (f32[1,224,384]{2,1,0:T(8,128)}, bf16[1,224,384]{2,1,0:T(8,128)(2,1)}) custom-call(f32[16,64,128]{2,1,0:T(8,128)S(1)} %all_to_all.22.mine_ref, f32[16,64,128]{2,1,0:T(8,128)S(1)} %collective-permute-done.1.other_ref, bf16[1,224,384]{2,1,0:T(8,128)(2,1)S(1)} %copy-done.1, f32[1,224,384]{2,1,0:T(8,128)S(1)} %copy-done.2), custom_call_target="tpu_custom_call" | custom-call | tf_op jit(solution)/shard_map/pallas_call | solution.py:245
Async XLA Ops:
  0.6 0.9 %copy-start = (bf16[1,224,384]{2,1,0:T(8,128)(2,1)S(1)}, bf16[1,224,384]{2,1,0:T(8,128)(2,1)}, u32[]{:S(2)}) copy-start(bf16[1,224,384]{2,1,0:T(8,128)(2,1)} %grad_ref.5) | copy-start | bytes 516100
  2.3 13.9 %all-to-all-start.1 = ((f32[16,1,128]{2,1,0:T(1,128)}), f32[16,1,128]{2,1,0:T(1,128)S(1)}, u32[]{:S(2)}, u32[]{:S(2)}) async-start(f32[16,1,128]{2,1,0:T(1,128)} %bitcast.1), calls=%async_computation.1 | async-start | bytes 16384 | tf_op jit(solution)/shard_map/all_to_all | solution.py:219
  16.2 24.7 %all-to-all-start = ((f32[32,64,128]{2,1,0:T(8,128)}), f32[32,64,128]{2,1,0:T(8,128)S(1)}, u32[]{:S(2)}, u32[]{:S(2)}) async-start(f32[32,64,128]{2,1,0:T(8,128)} %shard_map.41), calls=%async_computation | async-start | bytes 2097152 | tf_op jit(solution)/shard_map/all_to_all | solution.py:219
  23.6 0.7 %collective-permute-start = (f32[16,128]{1,0:T(8,128)S(1)}, f32[16,128]{1,0:T(8,128)S(1)}, u32[]{:S(2)}, u32[]{:S(2)}) collective-permute-start(f32[16,128]{1,0:T(8,128)S(1)} %bitcast.4), channel_id=1, source_target_pairs={{0,0},{1,1},{2,2},{3,3},{4,4},{5,5},{6,6},{7,7},{8,8},{9,9},{10,10... | collective-permute-start | bytes 24584 | tf_op jit(solution)/shard_map/ppermute | solution.py:227
  41.0 19.1 %copy-start.1 = (bf16[1,224,384]{2,1,0:T(8,128)(2,1)S(1)}, bf16[1,224,384]{2,1,0:T(8,128)(2,1)}, u32[]{:S(2)}) copy-start(bf16[1,224,384]{2,1,0:T(8,128)(2,1)} %grad_ref.5) | copy-start | bytes 516100
  41.0 19.1 %copy-start.2 = (f32[1,224,384]{2,1,0:T(8,128)S(1)}, f32[1,224,384]{2,1,0:T(8,128)}, u32[]{:S(2)}) copy-start(f32[1,224,384]{2,1,0:T(8,128)} %momentum_ref.3) | copy-start | bytes 1032196
  54.4 5.7 %collective-permute-start.1 = (f32[16,64,128]{2,1,0:T(8,128)S(1)}, f32[16,64,128]{2,1,0:T(8,128)S(1)}, u32[]{:S(2)}, u32[]{:S(2)}) collective-permute-start(f32[16,64,128]{2,1,0:T(8,128)S(1)} %all_to_all.22.mine_ref), channel_id=1, source_target_pairs={{0,16},{16,0},{32,48},{48,32},{64,80},{80,64},{96,112},{112,96},{1... | collective-permute-start | bytes 1572872 | tf_op jit(solution)/shard_map/ppermute | solution.py:244

commit v8 on v7

v8 whole, which is shorter than its diff:
```python
import functools
import math

import jax
import jax.numpy as jnp
from jax import lax
from jax.experimental import pallas as pl
from jax.experimental.pallas import tpu as pltpu
from jax.sharding import PartitionSpec as P

ITERS = 3

BETA = 0.95
COEF_A = 3.4445
COEF_B = -4.775
COEF_C = 2.0315

LANE = 128
SUB = 8
CORES = 2
HALF = 64
SECOND = 96


def dot(a, b):
    return jnp.dot(a, b, preferred_element_type=jnp.float32)


def split(x):
    high = x.astype(jnp.bfloat16)
    return high, (x - high.astype(jnp.float32)).astype(jnp.bfloat16)


def pairs_of(side):
    return [(i, j) for i in range(side) for j in range(i + 1, side)]


def block_order(side):
    pairs = len(pairs_of(side))
    sizes = (pairs, side + 2, pairs, pairs)
    return [(sum(sizes[:n]), size) for n, size in enumerate(sizes)]


def places(shape):
    return lax.broadcasted_iota(jnp.int32, shape, 0), lax.broadcasted_iota(jnp.int32, shape, 1)


def block_of(gram, i, j):
    return gram[i * LANE : (i + 1) * LANE, j * LANE : (j + 1) * LANE]


def diagonal_of(block):
    row, col = places(block.shape)
    return jnp.sum(jnp.where(row == col, block, 0.0), axis=0, keepdims=True)


def with_diagonals(block, tile):
    row, col = places(tile.shape)
    free = col < HALF
    return jnp.concatenate(
        [
            block[:HALF],
            jnp.where(free, tile, block[HALF : HALF + SUB]),
            block[HALF + SUB : SECOND],
            jnp.where(free, pltpu.roll(tile, HALF, 1), block[SECOND : SECOND + SUB]),
            block[SECOND + SUB :],
        ],
        axis=0,
    )


def diagonals_in(block):
    row, col = places((SUB, LANE))
    second = pltpu.roll(block[SECOND : SECOND + SUB], HALF, 1)
    return jnp.where(col < HALF, block[HALF : HALF + SUB], second)


def square_kernel(grad_ref, square_ref):
    full = grad_ref[0].astype(jnp.float32)
    squares = jnp.sum(full * full, axis=0, keepdims=True)
    square_ref[...] = jnp.broadcast_to(jnp.sum(squares, axis=1, keepdims=True), square_ref.shape)


def gram_kernel(grad_ref, momentum_ref, parts_ref, grad_in, momentum_in, parts_out, sems):
    copies = [
        pltpu.make_async_copy(grad_ref.at[0], grad_in, sems.at[0]),
        pltpu.make_async_copy(momentum_ref.at[0], momentum_in, sems.at[1]),
    ]
    for copy in copies:
        copy.start()
    copies[0].wait()
    width, order = grad_in.shape
    side = order // LANE
    pairs = pairs_of(side)
    row, col = places((LANE, LANE))
    devices, rows, _ = parts_ref.shape
    pieces = rows // SUB
    per_block = LANE // SUB
    blocks, sent = [], [0]

    def deal(more):
        known = len(blocks) * per_block
        blocks.extend(more)
        for q in range(known, len(blocks) * per_block):
            device, p = divmod(q, pieces)
            top = q % per_block * SUB
            parts_out[device, p * SUB : (p + 1) * SUB, :] = blocks[q // per_block][top : top + SUB]
        done = len(blocks) * per_block // pieces
        at = pl.ds(sent[0], done - sent[0])
        copy = pltpu.make_async_copy(parts_out.at[at], parts_ref.at[at], sems.at[len(copies)])
        copy.start()
        copies.append(copy)
        sent[0] = done

    def tall(x):
        pad = -width % 256
        return jnp.concatenate([x, jnp.zeros((pad, order), x.dtype)], axis=0)

    def summed(*terms):
        return dot(
            jnp.concatenate([a for a, _ in terms], axis=1), jnp.concatenate([b for _, b in terms], axis=0)
        )

    grad = tall(grad_in[...])
    grad_t = grad.T
    gg = summed((grad_t, grad))
    deal([block_of(gg, i, j) for i, j in pairs])
    copies[1].wait()
    high, low = [tall(x) for x in split(momentum_in[...])]
    high_t, low_t = high.T, low.T
    mm = summed((high_t, high), (high_t, low), (low_t, high))
    gm = summed((grad_t, high), (high_t, grad), (grad_t, low), (low_t, grad))
    gg, gm_on, mm_on = [[block_of(gram, k, k) for k in range(side)] for gram in (gg, gm, mm)]
    last = [diagonal_of(block) for block in gm_on + [mm_on[1]]]
    last = jnp.concatenate(last + [jnp.zeros((SUB - len(last), LANE), jnp.float32)], axis=0)
    shared = [jnp.where(row <= col, gg[k], gm_on[k]) for k in range(side)]
    shared += [jnp.where(row <= col, mm_on[0], mm_on[1]), with_diagonals(mm_on[2], last)]
    deal(shared + [block_of(gm, i, j) for i, j in pairs])
    deal([block_of(mm, i, j) for i, j in pairs])
    for copy in copies[2:]:
        copy.wait()


def middle_kernel(parts_ref, squares_ref, spread_ref):
    chips, rows, _ = spread_ref.shape
    total = jnp.sum(parts_ref[...], axis=0)
    squares = jnp.sum(squares_ref[...], axis=0, keepdims=True)
    for chip in range(chips):
        spread_ref[chip, : rows - SUB, :] = total
        spread_ref[chip, rows - SUB :, :] = jnp.broadcast_to(squares, (SUB, LANE))


def product(a, b):
    order = b[0].shape[1]
    cut = order - order % 256
    left = jnp.concatenate([a[0], a[1][:, cut:]], axis=1)
    rest = jnp.concatenate([b[0][cut:], jnp.zeros((order - cut, order), jnp.bfloat16)], axis=1)
    wide = dot(left, jnp.concatenate([jnp.concatenate(b, axis=1), rest], axis=0))
    return wide[:, :order] + (wide[:, order:] + dot(a[1][:, :cut], b[0][:cut]))


def final_kernel(step_scale, count, mine_ref, other_ref, grad_ref, momentum_ref, new_ref, update_ref, gram_ref, new_out, sem):
    core = lax.rem(lax.axis_index("fsdp"), CORES)
    order = grad_ref.shape[2]
    side = order // LANE
    chips, rows, _ = mine_ref.shape
    pieces = rows // SUB - 1
    squares = jnp.zeros((1, LANE), jnp.float32)
    for ref in (mine_ref, other_ref):
        squares = squares + jnp.sum(ref[:, rows - SUB :, :], axis=0)[:1]
    clip = 1.0 / jnp.sqrt(squares / count + 1e-06)
    alpha = (1.0 + BETA) * clip
    some = alpha > 0.0
    gain_gg, gain_gm, gain_mm = alpha * alpha, alpha * (BETA * BETA), BETA**4

    def grown(gain, block):
        return jnp.where(some, gain * block, 0.0)


    def piece(q):
        chip, rest = divmod(q, CORES * pieces)
        c, p = divmod(rest, pieces)
        at = slice(p * SUB, (p + 1) * SUB)
        first, second = (mine_ref, other_ref) if c == 0 else (other_ref, mine_ref)
        return jnp.where(core == 0, first[chip, at, :], second[chip, at, :])

    per_block = LANE // SUB
    blocks = [
        jnp.concatenate([piece(k * per_block + n) for n in range(per_block)], axis=0)
        for k in range(chips * CORES * pieces // per_block)
    ]
    pairs = pairs_of(side)
    gg_pairs, packed, gm_pairs, mm_pairs = [
        blocks[at : at + size] for at, size in block_order(side)
    ]
    last = diagonals_in(packed[side + 1])
    row, col = places((LANE, LANE))
    upper = jnp.where(row == col, 0.5, jnp.where(row < col, 1.0, 0.0))
    lower = jnp.where(row > col, 1.0, 0.0)
    half = jnp.where(row == col, 0.5, 0.0)
    trace = jnp.zeros((1, LANE), jnp.float32)
    for k in range(side):
        both = jnp.where(row > col, grown(gain_gm, packed[k]), grown(gain_gg, packed[k]) * jnp.where(row == col, 0.5, 1.0))
        both = both + half * grown(gain_gm, last[k : k + 1])
        if k == 0:
            both = both + gain_mm * (upper * packed[side])
        elif k == 1:
            both = both + gain_mm * (lower * packed[side] + half * last[side : side + 1])
        else:
            both = both + gain_mm * jnp.where(row > col, 0.0, upper * packed[side + 1])
        trace = trace + 2.0 * diagonal_of(both)
        both = both + both.T
        gram_ref[k * LANE : (k + 1) * LANE, k * LANE : (k + 1) * LANE] = both
    for (i, j), gg, gm, mm in zip(pairs, gg_pairs, gm_pairs, mm_pairs):
        block = grown(gain_gg, gg) + grown(gain_gm, gm) + gain_mm * mm
        gram_ref[i * LANE : (i + 1) * LANE, j * LANE : (j + 1) * LANE] = block
        gram_ref[j * LANE : (j + 1) * LANE, i * LANE : (i + 1) * LANE] = block.T

    clip = clip[:1, :1]
    grad_full = grad_ref[0].astype(jnp.float32)
    new_momentum = BETA * momentum_ref[0] + clip * grad_full
    new_out[...] = new_momentum
    copy = pltpu.make_async_copy(new_out, new_ref.at[0], sem)
    copy.start()
    direction = (clip * grad_full + BETA * new_momentum).astype(jnp.bfloat16)

    trace = jnp.sum(trace, axis=1, keepdims=True)
    norm_inv = 1.0 / (jnp.sqrt(trace) + 1e-07)
    moment = gram_ref[...] * (norm_inv * norm_inv)
    row = lax.broadcasted_iota(jnp.int32, (order, order), 0)
    col = lax.broadcasted_iota(jnp.int32, (order, order), 1)
    diagonal = jnp.where(row == col, COEF_A, 0.0)
    factor = None
    for iteration in range(ITERS):
        moment_parts = split(moment)
        poly = diagonal + COEF_B * moment + COEF_C * product(moment_parts, moment_parts)
        poly_parts = split(poly)
        if factor is None:
            factor = poly * norm_inv
        else:
            factor = product(poly_parts, split(factor))
        if iteration + 1 < ITERS:
            moment = product(split(product(poly_parts, moment_parts)), poly_parts)
    update = dot(direction, factor.astype(jnp.bfloat16))
    update_ref[0] = (step_scale * update).astype(jnp.bfloat16)
    copy.wait()


HBM = pl.BlockSpec(memory_space=pltpu.HBM)


def call(kernel, shapes, **specs):
    return pl.pallas_call(
        kernel,
        out_shape=shapes,
        compiler_params=pltpu.CompilerParams(vmem_limit_bytes=24 * 2**20),
        **specs,
    )


def per_device(grad, momentum):
    fsdp_count = lax.axis_size("fsdp")
    group_count = lax.axis_size("expert")
    _, width, order = grad.shape
    step_scale = 0.2 * math.sqrt(max(order, width * fsdp_count))
    count = grad.size * fsdp_count * group_count
    chips = fsdp_count // CORES
    side = order // LANE
    packed = (side + 2 + 3 * len(pairs_of(side))) * LANE
    share = packed // fsdp_count
    f32 = jnp.float32
    spread = jax.ShapeDtypeStruct((chips, share + SUB, LANE), f32)
    pairs = [(i, i ^ 1) for i in range(fsdp_count)]
    groups = [[CORES * i + c for i in range(chips)] for c in range(CORES)]

    def exchange(x, members=None):
        return lax.all_to_all(x, "fsdp", split_axis=0, concat_axis=0, tiled=True, axis_index_groups=members)

    turns = [
        (f * group_count + z, f * group_count + (z + f) % group_count)
        for f in range(fsdp_count)
        for z in range(group_count)
    ]
    halves = [list(range(at, at + group_count)) for at in range(0, fsdp_count, group_count)]
    square = call(square_kernel, jax.ShapeDtypeStruct((group_count, LANE), f32))(grad)
    planes = lax.ppermute(exchange(square, halves), ("fsdp", "expert"), turns)
    parts = jax.ShapeDtypeStruct((fsdp_count, share, LANE), f32)
    parts = pl.pallas_call(
        gram_kernel,
        out_shape=parts,
        in_specs=[HBM, HBM],
        out_specs=HBM,
        scratch_shapes=[
            pltpu.VMEM((width, order), grad.dtype),
            pltpu.VMEM((width, order), f32),
            pltpu.VMEM(parts.shape, f32),
            pltpu.SemaphoreType.DMA((5,)),
        ],
        compiler_params=pltpu.CompilerParams(vmem_limit_bytes=60 * 2**20),
    )(grad, momentum)
    parts = exchange(parts)
    spread = call(middle_kernel, spread)(parts, planes)
    mine = exchange(spread, members=groups)
    other = lax.ppermute(mine, "fsdp", pairs)
    return call(
        functools.partial(final_kernel, step_scale, count),
        (
            jax.ShapeDtypeStruct(grad.shape, f32),
            jax.ShapeDtypeStruct(grad.shape, jnp.bfloat16),
        ),
        out_specs=(HBM, pl.BlockSpec(memory_space=pltpu.VMEM)),
        scratch_shapes=[
            pltpu.VMEM((order, order), f32),
            pltpu.VMEM((width, order), f32),
            pltpu.SemaphoreType.DMA,
        ],
    )(mine, other, grad, momentum)


def solution(mesh):
    placed = P("expert", "fsdp", None)
    return jax.shard_map(
        per_device,
        mesh=mesh,
        in_specs=(placed, placed),
        out_specs=(placed, placed),
        check_vma=False,
    )
```

time: 66.5 us -> 64.9 us (0.976)
  waiting for transfers between devices: 21.4 us -> 17.8 us
  blocking collectives: 13.4 us -> 15 us
    all_to_all x2, waiting for transfers between devices: 19.9 us -> 7.77 us  [exchange(): lax.all_to_all(x, 'fsdp', split_axis=0, concat_axis=0, tiled=True, axis_i...]
    ppermute x1, waiting for transfers between devices: 0.01 us -> 8.52 us  [per_device(): planes = lax.ppermute(exchange(square, halves), ('fsdp', 'expert'), turns)]
    all_to_all x1, blocking collectives: 13.4 us -> 15 us  [exchange(): lax.all_to_all(x, 'fsdp', split_axis=0, concat_axis=0, tiled=True, axis_i...]
    ppermute x1, starting transfers between devices: 0.66 us -> 1.92 us  [per_device(): planes = lax.ppermute(exchange(square, halves), ('fsdp', 'expert'), turns)]
  transfers between devices with their start and end apart: 4 -> 4, of which waited for: 3 -> 4; matrix products, arithmetic and copies ran while one was open for 0% -> 0% of each run, Pallas kernels for 5% -> 5%
where the time goes in v8:
time: 64.9 us; the launch traced here: 64.5 us
  starting transfers between devices  20.1 us (31%)
  waiting for transfers between devices  17.8 us (27%)
  blocking collectives  15 us (23%)
  Pallas kernels  9.93 us (15%)
  local copies, waits for them, and re-layouts  0.93 us (1%)
  between operations  0.7 us (1%)
    all_to_all x1, blocking collectives, exchange(): lax.all_to_all(x, 'fsdp', split_axis=0, concat_axis=0, tiled=True, axis_i...  15 us
    all_to_all x2, starting transfers between devices, exchange(): lax.all_to_all(x, 'fsdp', split_axis=0, concat_axis=0, tiled=True, axis_i...  14.4 us
    ppermute x1, waiting for transfers between devices, per_device(): planes = lax.ppermute(exchange(square, halves), ('fsdp', 'expert'), turns)  8.52 us
    all_to_all x2, waiting for transfers between devices, exchange(): lax.all_to_all(x, 'fsdp', split_axis=0, concat_axis=0, tiled=True, axis_i...  7.77 us
    pallas_call x1, Pallas kernels, per_device(): call(functools.partial(final_kernel, step_scale, count), (jax.ShapeDtypeS...  6 us
    ppermute x1, starting transfers between devices, per_device(): other = lax.ppermute(mine, 'fsdp', pairs)  3.84 us
    pallas_call x1, Pallas kernels, per_device(): pl.pallas_call(gram_kernel, out_shape=parts, in_specs=[HBM, HBM], out_spe...  3.12 us
    ppermute x1, starting transfers between devices, per_device(): planes = lax.ppermute(exchange(square, halves), ('fsdp', 'expert'), turns)  1.92 us
  transfers between devices with their start and end apart: 4, of which 4 were waited for; matrix products, arithmetic and copies ran while one was open for 0% of the time, Pallas kernels for 5%

profile of v8, /device:TPU:1, one launch (start us, length us, event | category | flops | bytes accessed | tf_op | source)
XLA Modules:
  0.0 64.5 jit_solution(8509193747463090898)
XLA Ops:
  0.6 0.0 copy-start
  0.6 0.9 %copy-done = bf16[1,224,384]{2,1,0:T(8,128)(2,1)S(1)} copy-done((bf16[1,224,384]{2,1,0:T(8,128)(2,1)S(1)}, bf16[1,224,384]{2,1,0:T(8,128)(2,1)}, u32[]{:S(2)}) %copy-start) | copy-done | bytes 172056
  1.6 0.7 %shard_map.42 = f32[16,128]{1,0:T(8,128)} custom-call(bf16[1,224,384]{2,1,0:T(8,128)(2,1)S(1)} %copy-done), custom_call_target="tpu_custom_call" | custom-call | tf_op jit(solution)/shard_map/pallas_call | solution.py:285
  2.3 10.1 %all-to-all-start.1 = ((f32[16,1,128]{2,1,0:T(1,128)}), f32[16,1,128]{2,1,0:T(1,128)S(1)}, u32[]{:S(2)}, u32[]{:S(2)}) async-start(f32[16,1,128]{2,1,0:T(1,128)} %bitcast.1), calls=%async_computation.1 | async-start | bytes 16384 | tf_op jit(solution)/shard_map/all_to_all | solution.py:277
  12.4 3.1 %shard_map.41 = f32[32,56,128]{2,1,0:T(8,128)} custom-call(bf16[1,224,384]{2,1,0:T(8,128)(2,1)} %grad_ref.5, f32[1,224,384]{2,1,0:T(8,128)} %momentum_ref.3), custom_call_target="tpu_custom_call" | custom-call | tf_op jit(solution)/shard_map/pallas_call | solution.py:288
  15.5 2.3 %all-to-all-done.1 = f32[16,1,128]{2,1,0:T(1,128)S(1)} async-done(((f32[16,1,128]{2,1,0:T(1,128)}), f32[16,1,128]{2,1,0:T(1,128)S(1)}, u32[]{:S(2)}, u32[]{:S(2)}) %all-to-all-start.1) | async-done | bytes 8224 | tf_op jit(solution)/shard_map/all_to_all | solution.py:277
  17.9 4.2 %all-to-all-start = ((f32[32,56,128]{2,1,0:T(8,128)}), f32[32,56,128]{2,1,0:T(8,128)S(1)}, u32[]{:S(2)}, u32[]{:S(2)}) async-start(f32[32,56,128]{2,1,0:T(8,128)} %shard_map.41), calls=%async_computation | async-start | bytes 1835008 | tf_op jit(solution)/shard_map/all_to_all | solution.py:277
  22.1 1.9 %collective-permute-start = (f32[16,128]{1,0:T(8,128)S(1)}, f32[16,128]{1,0:T(8,128)S(1)}, u32[]{:S(2)}, u32[]{:S(2)}) collective-permute-start(f32[16,128]{1,0:T(8,128)S(1)} %bitcast.4), channel_id=1, source_target_pairs={{0,0},{1,1},{2,2},{3,3},{4,4},{5,5},{6,6},{7,7},{8,8},{9,9},{10,10... | collective-permute-start | bytes 24584 | tf_op jit(solution)/shard_map/ppermute | solution.py:286
  24.1 8.5 %collective-permute-done.squares_ref = f32[16,128]{1,0:T(8,128)S(1)} collective-permute-done((f32[16,128]{1,0:T(8,128)S(1)}, f32[16,128]{1,0:T(8,128)S(1)}, u32[]{:S(2)}, u32[]{:S(2)}) %collective-permute-start) | collective-permute-done | bytes 8224 | tf_op jit(solution)/shard_map/ppermute | solution.py:286
  32.6 5.4 %all-to-all-done.parts_ref = f32[32,56,128]{2,1,0:T(8,128)S(1)} async-done(((f32[32,56,128]{2,1,0:T(8,128)}), f32[32,56,128]{2,1,0:T(8,128)S(1)}, u32[]{:S(2)}, u32[]{:S(2)}) %all-to-all-start) | async-done | bytes 917536 | tf_op jit(solution)/shard_map/all_to_all | solution.py:277
  38.0 0.1 shard_map.43
  38.1 0.0 copy-start.1
  38.1 0.0 copy-start.2
  38.1 15.0 %all_to_all.22.mine_ref = f32[16,64,128]{2,1,0:T(8,128)S(1)} all-to-all(f32[16,64,128]{2,1,0:T(8,128)S(1)} %shard_map.43), channel_id=1, replica_groups={{0,32,64,96,128,160,192,224,256,288,320,352,384,416,448,480},{16,48,80,..., dimensions={0} | all-to-all | bytes 1048576 | tf_op jit(solution)/shard_map/all_to_all | solution.py:277
  53.2 3.8 %collective-permute-start.1 = (f32[16,64,128]{2,1,0:T(8,128)S(1)}, f32[16,64,128]{2,1,0:T(8,128)S(1)}, u32[]{:S(2)}, u32[]{:S(2)}) collective-permute-start(f32[16,64,128]{2,1,0:T(8,128)S(1)} %all_to_all.22.mine_ref), channel_id=1, source_target_pairs={{0,16},{16,0},{32,48},{48,32},{64,80},{80,64},{96,112},{112,96},{1... | collective-permute-start | bytes 1572872 | tf_op jit(solution)/shard_map/ppermute | solution.py:304
  57.0 1.5 %collective-permute-done.1.other_ref = f32[16,64,128]{2,1,0:T(8,128)S(1)} collective-permute-done((f32[16,64,128]{2,1,0:T(8,128)S(1)}, f32[16,64,128]{2,1,0:T(8,128)S(1)}, u32[]{:S(2)}, u32[]{:S(2)}) %collective-permute-start.1) | collective-permute-done | bytes 524320 | tf_op jit(solution)/shard_map/ppermute | solution.py:304
  58.5 0.0 copy-done.1
  58.5 0.0 copy-done.2
  58.5 6.0 %shard_map.44 = (f32[1,224,384]{2,1,0:T(8,128)}, bf16[1,224,384]{2,1,0:T(8,128)(2,1)}) custom-call(f32[16,64,128]{2,1,0:T(8,128)S(1)} %all_to_all.22.mine_ref, f32[16,64,128]{2,1,0:T(8,128)S(1)} %collective-permute-done.1.other_ref, bf16[1,224,384]{2,1,0:T(8,128)(2,1)S(1)} %copy-done.1, f32[1,224,384]{2,1,0:T(8,128)S(1)} %copy-done.2), custom_call_target="tpu_custom_call" | custom-call | tf_op jit(solution)/shard_map/pallas_call | solution.py:305
Async XLA Ops:
  0.6 0.9 %copy-start = (bf16[1,224,384]{2,1,0:T(8,128)(2,1)S(1)}, bf16[1,224,384]{2,1,0:T(8,128)(2,1)}, u32[]{:S(2)}) copy-start(bf16[1,224,384]{2,1,0:T(8,128)(2,1)} %grad_ref.5) | copy-start | bytes 516100
  2.3 15.6 %all-to-all-start.1 = ((f32[16,1,128]{2,1,0:T(1,128)}), f32[16,1,128]{2,1,0:T(1,128)S(1)}, u32[]{:S(2)}, u32[]{:S(2)}) async-start(f32[16,1,128]{2,1,0:T(1,128)} %bitcast.1), calls=%async_computation.1 | async-start | bytes 16384 | tf_op jit(solution)/shard_map/all_to_all | solution.py:277
  17.9 20.1 %all-to-all-start = ((f32[32,56,128]{2,1,0:T(8,128)}), f32[32,56,128]{2,1,0:T(8,128)S(1)}, u32[]{:S(2)}, u32[]{:S(2)}) async-start(f32[32,56,128]{2,1,0:T(8,128)} %shard_map.41), calls=%async_computation | async-start | bytes 1835008 | tf_op jit(solution)/shard_map/all_to_all | solution.py:277
  22.1 10.4 %collective-permute-start = (f32[16,128]{1,0:T(8,128)S(1)}, f32[16,128]{1,0:T(8,128)S(1)}, u32[]{:S(2)}, u32[]{:S(2)}) collective-permute-start(f32[16,128]{1,0:T(8,128)S(1)} %bitcast.4), channel_id=1, source_target_pairs={{0,0},{1,1},{2,2},{3,3},{4,4},{5,5},{6,6},{7,7},{8,8},{9,9},{10,10... | collective-permute-start | bytes 24584 | tf_op jit(solution)/shard_map/ppermute | solution.py:286
  38.1 20.4 %copy-start.1 = (bf16[1,224,384]{2,1,0:T(8,128)(2,1)S(1)}, bf16[1,224,384]{2,1,0:T(8,128)(2,1)}, u32[]{:S(2)}) copy-start(bf16[1,224,384]{2,1,0:T(8,128)(2,1)} %grad_ref.5) | copy-start | bytes 516100
  38.1 20.4 %copy-start.2 = (f32[1,224,384]{2,1,0:T(8,128)S(1)}, f32[1,224,384]{2,1,0:T(8,128)}, u32[]{:S(2)}) copy-start(f32[1,224,384]{2,1,0:T(8,128)} %momentum_ref.3) | copy-start | bytes 1032196
  53.2 5.4 %collective-permute-start.1 = (f32[16,64,128]{2,1,0:T(8,128)S(1)}, f32[16,64,128]{2,1,0:T(8,128)S(1)}, u32[]{:S(2)}, u32[]{:S(2)}) collective-permute-start(f32[16,64,128]{2,1,0:T(8,128)S(1)} %all_to_all.22.mine_ref), channel_id=1, source_target_pairs={{0,16},{16,0},{32,48},{48,32},{64,80},{80,64},{96,112},{112,96},{1... | collective-permute-start | bytes 1572872 | tf_op jit(solution)/shard_map/ppermute | solution.py:304

commit v9 on v8

--- a/solution.py
+++ b/solution.py
@@ -18,6 +18,7 @@
 LANE = 128
 SUB = 8
 CORES = 2
+ROW = 4
 HALF = 64
 SECOND = 96
 
@@ -276,8 +277,16 @@
     def exchange(x, members=None):
         return lax.all_to_all(x, "fsdp", split_axis=0, concat_axis=0, tiled=True, axis_index_groups=members)
 
+    def hops(f):
+        y, x = divmod(f // CORES, ROW)
+        return min(y, fsdp_count // (CORES * ROW) - y) + min(x, ROW - x)
+
+    ways = sorted(range(group_count), key=lambda k: -min(k, group_count - k))
+    shift = {}
+    for at in range(0, fsdp_count, group_count):
+        shift.update(zip(sorted(range(at, at + group_count), key=hops), ways))
     turns = [
-        (f * group_count + z, f * group_count + (z + f) % group_count)
+        (f * group_count + z, f * group_count + (z + shift[f]) % group_count)
         for f in range(fsdp_count)
         for z in range(group_count)
     ]

time: 64.9 us -> 63.6 us (0.980)
  starting transfers between devices: 20.1 us -> 29.5 us
  waiting for transfers between devices: 17.8 us -> 8.85 us
  blocking collectives: 15 us -> 13.3 us
    ppermute x1, starting transfers between devices: 1.92 us -> 10.9 us  [per_device(): planes = lax.ppermute(exchange(square, halves), ('fsdp', 'expert'), turns)]
    ppermute x1, waiting for transfers between devices: 8.52 us -> 3.21 us  [per_device(): planes = lax.ppermute(exchange(square, halves), ('fsdp', 'expert'), turns)]
    all_to_all x2, waiting for transfers between devices: 7.77 us -> 4.13 us  [exchange(): lax.all_to_all(x, 'fsdp', split_axis=0, concat_axis=0, tiled=True, axis_i...]
    all_to_all x1, blocking collectives: 15 us -> 13.3 us  [exchange(): lax.all_to_all(x, 'fsdp', split_axis=0, concat_axis=0, tiled=True, axis_i...]
where the time goes in v9:
time: 63.6 us; the launch traced here: 63.2 us
  starting transfers between devices  29.5 us (46%)
  blocking collectives  13.3 us (21%)
  Pallas kernels  9.91 us (16%)
  waiting for transfers between devices  8.85 us (14%)
  local copies, waits for them, and re-layouts  0.93 us (1%)
  between operations  0.7 us (1%)
    all_to_all x2, starting transfers between devices, exchange(): lax.all_to_all(x, 'fsdp', split_axis=0, concat_axis=0, tiled=True, axis_i...  14.4 us
    all_to_all x1, blocking collectives, exchange(): lax.all_to_all(x, 'fsdp', split_axis=0, concat_axis=0, tiled=True, axis_i...  13.3 us
    ppermute x1, starting transfers between devices, per_device(): planes = lax.ppermute(exchange(square, halves), ('fsdp', 'expert'), turns)  10.9 us
    pallas_call x1, Pallas kernels, per_device(): call(functools.partial(final_kernel, step_scale, count), (jax.ShapeDtypeS...  5.99 us
    ppermute x1, starting transfers between devices, per_device(): other = lax.ppermute(mine, 'fsdp', pairs)  4.23 us
    all_to_all x2, waiting for transfers between devices, exchange(): lax.all_to_all(x, 'fsdp', split_axis=0, concat_axis=0, tiled=True, axis_i...  4.13 us
    ppermute x1, waiting for transfers between devices, per_device(): planes = lax.ppermute(exchange(square, halves), ('fsdp', 'expert'), turns)  3.21 us
    pallas_call x1, Pallas kernels, per_device(): pl.pallas_call(gram_kernel, out_shape=parts, in_specs=[HBM, HBM], out_spe...  3.12 us
  transfers between devices with their start and end apart: 4, of which 4 were waited for; matrix products, arithmetic and copies ran while one was open for 0% of the time, Pallas kernels for 5%

profile of v9, /device:TPU:1, one launch (start us, length us, event | category | flops | bytes accessed | tf_op | source)
XLA Modules:
  0.0 63.2 jit_solution(11553402053626182270)
XLA Ops:
  0.6 0.0 copy-start
  0.6 0.9 %copy-done = bf16[1,224,384]{2,1,0:T(8,128)(2,1)S(1)} copy-done((bf16[1,224,384]{2,1,0:T(8,128)(2,1)S(1)}, bf16[1,224,384]{2,1,0:T(8,128)(2,1)}, u32[]{:S(2)}) %copy-start) | copy-done | bytes 172056
  1.6 0.7 %shard_map.42 = f32[16,128]{1,0:T(8,128)} custom-call(bf16[1,224,384]{2,1,0:T(8,128)(2,1)S(1)} %copy-done), custom_call_target="tpu_custom_call" | custom-call | tf_op jit(solution)/shard_map/pallas_call | solution.py:294
  2.3 10.1 %all-to-all-start.1 = ((f32[16,1,128]{2,1,0:T(1,128)}), f32[16,1,128]{2,1,0:T(1,128)S(1)}, u32[]{:S(2)}, u32[]{:S(2)}) async-start(f32[16,1,128]{2,1,0:T(1,128)} %bitcast.1), calls=%async_computation.1 | async-start | bytes 16384 | tf_op jit(solution)/shard_map/all_to_all | solution.py:278
  12.4 3.1 %shard_map.41 = f32[32,56,128]{2,1,0:T(8,128)} custom-call(bf16[1,224,384]{2,1,0:T(8,128)(2,1)} %grad_ref.5, f32[1,224,384]{2,1,0:T(8,128)} %momentum_ref.3), custom_call_target="tpu_custom_call" | custom-call | tf_op jit(solution)/shard_map/pallas_call | solution.py:297
  15.5 2.3 %all-to-all-done.1 = f32[16,1,128]{2,1,0:T(1,128)S(1)} async-done(((f32[16,1,128]{2,1,0:T(1,128)}), f32[16,1,128]{2,1,0:T(1,128)S(1)}, u32[]{:S(2)}, u32[]{:S(2)}) %all-to-all-start.1) | async-done | bytes 8224 | tf_op jit(solution)/shard_map/all_to_all | solution.py:278
  17.9 4.2 %all-to-all-start = ((f32[32,56,128]{2,1,0:T(8,128)}), f32[32,56,128]{2,1,0:T(8,128)S(1)}, u32[]{:S(2)}, u32[]{:S(2)}) async-start(f32[32,56,128]{2,1,0:T(8,128)} %shard_map.41), calls=%async_computation | async-start | bytes 1835008 | tf_op jit(solution)/shard_map/all_to_all | solution.py:278
  22.1 10.9 %collective-permute-start = (f32[16,128]{1,0:T(8,128)S(1)}, f32[16,128]{1,0:T(8,128)S(1)}, u32[]{:S(2)}, u32[]{:S(2)}) collective-permute-start(f32[16,128]{1,0:T(8,128)S(1)} %bitcast.4), channel_id=1, source_target_pairs={{0,8},{1,9},{2,10},{3,11},{4,12},{5,13},{6,14},{7,15},{8,0},{9,1},... | collective-permute-start | bytes 24584 | tf_op jit(solution)/shard_map/ppermute | solution.py:295
  33.0 3.2 %collective-permute-done.squares_ref = f32[16,128]{1,0:T(8,128)S(1)} collective-permute-done((f32[16,128]{1,0:T(8,128)S(1)}, f32[16,128]{1,0:T(8,128)S(1)}, u32[]{:S(2)}, u32[]{:S(2)}) %collective-permute-start) | collective-permute-done | bytes 8224 | tf_op jit(solution)/shard_map/ppermute | solution.py:295
  36.2 1.8 %all-to-all-done.parts_ref = f32[32,56,128]{2,1,0:T(8,128)S(1)} async-done(((f32[32,56,128]{2,1,0:T(8,128)}), f32[32,56,128]{2,1,0:T(8,128)S(1)}, u32[]{:S(2)}, u32[]{:S(2)}) %all-to-all-start) | async-done | bytes 917536 | tf_op jit(solution)/shard_map/all_to_all | solution.py:278
  38.0 0.1 shard_map.43
  38.1 0.0 copy-start.1
  38.1 0.0 copy-start.2
  38.1 13.3 %all_to_all.22.mine_ref = f32[16,64,128]{2,1,0:T(8,128)S(1)} all-to-all(f32[16,64,128]{2,1,0:T(8,128)S(1)} %shard_map.43), channel_id=1, replica_groups={{0,32,64,96,128,160,192,224,256,288,320,352,384,416,448,480},{16,48,80,..., dimensions={0} | all-to-all | bytes 1048576 | tf_op jit(solution)/shard_map/all_to_all | solution.py:278
  51.4 4.2 %collective-permute-start.1 = (f32[16,64,128]{2,1,0:T(8,128)S(1)}, f32[16,64,128]{2,1,0:T(8,128)S(1)}, u32[]{:S(2)}, u32[]{:S(2)}) collective-permute-start(f32[16,64,128]{2,1,0:T(8,128)S(1)} %all_to_all.22.mine_ref), channel_id=1, source_target_pairs={{0,16},{16,0},{32,48},{48,32},{64,80},{80,64},{96,112},{112,96},{1... | collective-permute-start | bytes 1572872 | tf_op jit(solution)/shard_map/ppermute | solution.py:313
  55.7 1.5 %collective-permute-done.1.other_ref = f32[16,64,128]{2,1,0:T(8,128)S(1)} collective-permute-done((f32[16,64,128]{2,1,0:T(8,128)S(1)}, f32[16,64,128]{2,1,0:T(8,128)S(1)}, u32[]{:S(2)}, u32[]{:S(2)}) %collective-permute-start.1) | collective-permute-done | bytes 524320 | tf_op jit(solution)/shard_map/ppermute | solution.py:313
  57.2 0.0 copy-done.1
  57.2 0.0 copy-done.2
  57.2 6.0 %shard_map.44 = (f32[1,224,384]{2,1,0:T(8,128)}, bf16[1,224,384]{2,1,0:T(8,128)(2,1)}) custom-call(f32[16,64,128]{2,1,0:T(8,128)S(1)} %all_to_all.22.mine_ref, f32[16,64,128]{2,1,0:T(8,128)S(1)} %collective-permute-done.1.other_ref, bf16[1,224,384]{2,1,0:T(8,128)(2,1)S(1)} %copy-done.1, f32[1,224,384]{2,1,0:T(8,128)S(1)} %copy-done.2), custom_call_target="tpu_custom_call" | custom-call | tf_op jit(solution)/shard_map/pallas_call | solution.py:314
Async XLA Ops:
  0.6 0.9 %copy-start = (bf16[1,224,384]{2,1,0:T(8,128)(2,1)S(1)}, bf16[1,224,384]{2,1,0:T(8,128)(2,1)}, u32[]{:S(2)}) copy-start(bf16[1,224,384]{2,1,0:T(8,128)(2,1)} %grad_ref.5) | copy-start | bytes 516100
  2.3 15.6 %all-to-all-start.1 = ((f32[16,1,128]{2,1,0:T(1,128)}), f32[16,1,128]{2,1,0:T(1,128)S(1)}, u32[]{:S(2)}, u32[]{:S(2)}) async-start(f32[16,1,128]{2,1,0:T(1,128)} %bitcast.1), calls=%async_computation.1 | async-start | bytes 16384 | tf_op jit(solution)/shard_map/all_to_all | solution.py:278
  17.9 20.1 %all-to-all-start = ((f32[32,56,128]{2,1,0:T(8,128)}), f32[32,56,128]{2,1,0:T(8,128)S(1)}, u32[]{:S(2)}, u32[]{:S(2)}) async-start(f32[32,56,128]{2,1,0:T(8,128)} %shard_map.41), calls=%async_computation | async-start | bytes 1835008 | tf_op jit(solution)/shard_map/all_to_all | solution.py:278
  22.1 14.1 %collective-permute-start = (f32[16,128]{1,0:T(8,128)S(1)}, f32[16,128]{1,0:T(8,128)S(1)}, u32[]{:S(2)}, u32[]{:S(2)}) collective-permute-start(f32[16,128]{1,0:T(8,128)S(1)} %bitcast.4), channel_id=1, source_target_pairs={{0,8},{1,9},{2,10},{3,11},{4,12},{5,13},{6,14},{7,15},{8,0},{9,1},... | collective-permute-start | bytes 24584 | tf_op jit(solution)/shard_map/ppermute | solution.py:295
  38.1 19.1 %copy-start.1 = (bf16[1,224,384]{2,1,0:T(8,128)(2,1)S(1)}, bf16[1,224,384]{2,1,0:T(8,128)(2,1)}, u32[]{:S(2)}) copy-start(bf16[1,224,384]{2,1,0:T(8,128)(2,1)} %grad_ref.5) | copy-start | bytes 516100
  38.1 19.1 %copy-start.2 = (f32[1,224,384]{2,1,0:T(8,128)S(1)}, f32[1,224,384]{2,1,0:T(8,128)}, u32[]{:S(2)}) copy-start(f32[1,224,384]{2,1,0:T(8,128)} %momentum_ref.3) | copy-start | bytes 1032196
  51.4 5.8 %collective-permute-start.1 = (f32[16,64,128]{2,1,0:T(8,128)S(1)}, f32[16,64,128]{2,1,0:T(8,128)S(1)}, u32[]{:S(2)}, u32[]{:S(2)}) collective-permute-start(f32[16,64,128]{2,1,0:T(8,128)S(1)} %all_to_all.22.mine_ref), channel_id=1, source_target_pairs={{0,16},{16,0},{32,48},{48,32},{64,80},{80,64},{96,112},{112,96},{1... | collective-permute-start | bytes 1572872 | tf_op jit(solution)/shard_map/ppermute | solution.py:313

commit v10 on v9

--- a/solution.py
+++ b/solution.py
@@ -290,7 +290,9 @@
         for f in range(fsdp_count)
         for z in range(group_count)
     ]
-    halves = [list(range(at, at + group_count)) for at in range(0, fsdp_count, group_count)]
+    halves = [
+        sorted(range(at, at + group_count), key=lambda f: abs(f // CORES % ROW - 1)) for at in range(0, fsdp_count, group_count)
+    ]
     square = call(square_kernel, jax.ShapeDtypeStruct((group_count, LANE), f32))(grad)
     planes = lax.ppermute(exchange(square, halves), ("fsdp", "expert"), turns)
     parts = jax.ShapeDtypeStruct((fsdp_count, share, LANE), f32)

time: 63.6 us -> 62.7 us (0.986)
  starting transfers between devices: 29.5 us -> 30.9 us
  waiting for transfers between devices: 8.85 us -> 7.58 us
  blocking collectives: 13.3 us -> 12.3 us
    all_to_all x2, waiting for transfers between devices: 4.13 us -> 2.86 us  [exchange(): lax.all_to_all(x, 'fsdp', split_axis=0, concat_axis=0, tiled=True, axis_i...]
    all_to_all x1, blocking collectives: 13.3 us -> 12.3 us  [exchange(): lax.all_to_all(x, 'fsdp', split_axis=0, concat_axis=0, tiled=True, axis_i...]
    ppermute x1, starting transfers between devices: 10.9 us -> 11.8 us  [per_device(): planes = lax.ppermute(exchange(square, halves), ('fsdp', 'expert'), turns)]
    ppermute x1, starting transfers between devices: 4.23 us -> 5.06 us  [per_device(): other = lax.ppermute(mine, 'fsdp', pairs)]
where the time goes in v10:
time: 62.7 us; the launch traced here: 62.3 us
  starting transfers between devices  30.9 us (49%)
  blocking collectives  12.3 us (20%)
  Pallas kernels  9.91 us (16%)
  waiting for transfers between devices  7.58 us (12%)
  local copies, waits for them, and re-layouts  0.93 us (1%)
  between operations  0.7 us (1%)
    all_to_all x2, starting transfers between devices, exchange(): lax.all_to_all(x, 'fsdp', split_axis=0, concat_axis=0, tiled=True, axis_i...  14.1 us
    all_to_all x1, blocking collectives, exchange(): lax.all_to_all(x, 'fsdp', split_axis=0, concat_axis=0, tiled=True, axis_i...  12.3 us
    ppermute x1, starting transfers between devices, per_device(): planes = lax.ppermute(exchange(square, halves), ('fsdp', 'expert'), turns)  11.8 us
    pallas_call x1, Pallas kernels, per_device(): call(functools.partial(final_kernel, step_scale, count), (jax.ShapeDtypeS...  5.99 us
    ppermute x1, starting transfers between devices, per_device(): other = lax.ppermute(mine, 'fsdp', pairs)  5.06 us
    ppermute x1, waiting for transfers between devices, per_device(): planes = lax.ppermute(exchange(square, halves), ('fsdp', 'expert'), turns)  3.21 us
    pallas_call x1, Pallas kernels, per_device(): pl.pallas_call(gram_kernel, out_shape=parts, in_specs=[HBM, HBM], out_spe...  3.13 us
    all_to_all x2, waiting for transfers between devices, exchange(): lax.all_to_all(x, 'fsdp', split_axis=0, concat_axis=0, tiled=True, axis_i...  2.86 us
  transfers between devices with their start and end apart: 4, of which 4 were waited for; matrix products, arithmetic and copies ran while one was open for 0% of the time, Pallas kernels for 5%

profile of v10, /device:TPU:1, one launch (start us, length us, event | category | flops | bytes accessed | tf_op | source)
XLA Modules:
  0.0 62.3 jit_solution(16229650615628195710)
XLA Ops:
  0.6 0.0 copy-start
  0.6 0.9 %copy-done = bf16[1,224,384]{2,1,0:T(8,128)(2,1)S(1)} copy-done((bf16[1,224,384]{2,1,0:T(8,128)(2,1)S(1)}, bf16[1,224,384]{2,1,0:T(8,128)(2,1)}, u32[]{:S(2)}) %copy-start) | copy-done | bytes 172056
  1.6 0.7 %shard_map.42 = f32[16,128]{1,0:T(8,128)} custom-call(bf16[1,224,384]{2,1,0:T(8,128)(2,1)S(1)} %copy-done), custom_call_target="tpu_custom_call" | custom-call | tf_op jit(solution)/shard_map/pallas_call | solution.py:296
  2.3 9.8 %all-to-all-start.1 = ((f32[16,1,128]{2,1,0:T(1,128)}), f32[16,1,128]{2,1,0:T(1,128)S(1)}, u32[]{:S(2)}, u32[]{:S(2)}) async-start(f32[16,1,128]{2,1,0:T(1,128)} %bitcast.1), calls=%async_computation.1 | async-start | bytes 16384 | tf_op jit(solution)/shard_map/all_to_all | solution.py:278
  12.1 3.1 %shard_map.41 = f32[32,56,128]{2,1,0:T(8,128)} custom-call(bf16[1,224,384]{2,1,0:T(8,128)(2,1)} %grad_ref.5, f32[1,224,384]{2,1,0:T(8,128)} %momentum_ref.3), custom_call_target="tpu_custom_call" | custom-call | tf_op jit(solution)/shard_map/pallas_call | solution.py:299
  15.2 1.8 %all-to-all-done.1 = f32[16,1,128]{2,1,0:T(1,128)S(1)} async-done(((f32[16,1,128]{2,1,0:T(1,128)}), f32[16,1,128]{2,1,0:T(1,128)S(1)}, u32[]{:S(2)}, u32[]{:S(2)}) %all-to-all-start.1) | async-done | bytes 8224 | tf_op jit(solution)/shard_map/all_to_all | solution.py:278
  17.0 4.3 %all-to-all-start = ((f32[32,56,128]{2,1,0:T(8,128)}), f32[32,56,128]{2,1,0:T(8,128)S(1)}, u32[]{:S(2)}, u32[]{:S(2)}) async-start(f32[32,56,128]{2,1,0:T(8,128)} %shard_map.41), calls=%async_computation | async-start | bytes 1835008 | tf_op jit(solution)/shard_map/all_to_all | solution.py:278
  21.3 11.8 %collective-permute-start = (f32[16,128]{1,0:T(8,128)S(1)}, f32[16,128]{1,0:T(8,128)S(1)}, u32[]{:S(2)}, u32[]{:S(2)}) collective-permute-start(f32[16,128]{1,0:T(8,128)S(1)} %bitcast.4), channel_id=1, source_target_pairs={{0,8},{1,9},{2,10},{3,11},{4,12},{5,13},{6,14},{7,15},{8,0},{9,1},... | collective-permute-start | bytes 24584 | tf_op jit(solution)/shard_map/ppermute | solution.py:297
  33.0 3.2 %collective-permute-done.squares_ref = f32[16,128]{1,0:T(8,128)S(1)} collective-permute-done((f32[16,128]{1,0:T(8,128)S(1)}, f32[16,128]{1,0:T(8,128)S(1)}, u32[]{:S(2)}, u32[]{:S(2)}) %collective-permute-start) | collective-permute-done | bytes 8224 | tf_op jit(solution)/shard_map/ppermute | solution.py:297
  36.2 1.1 %all-to-all-done.parts_ref = f32[32,56,128]{2,1,0:T(8,128)S(1)} async-done(((f32[32,56,128]{2,1,0:T(8,128)}), f32[32,56,128]{2,1,0:T(8,128)S(1)}, u32[]{:S(2)}, u32[]{:S(2)}) %all-to-all-start) | async-done | bytes 917536 | tf_op jit(solution)/shard_map/all_to_all | solution.py:278
  37.3 0.1 shard_map.43
  37.4 0.0 copy-start.1
  37.4 0.0 copy-start.2
  37.5 12.3 %all_to_all.22.mine_ref = f32[16,64,128]{2,1,0:T(8,128)S(1)} all-to-all(f32[16,64,128]{2,1,0:T(8,128)S(1)} %shard_map.43), channel_id=1, replica_groups={{0,32,64,96,128,160,192,224,256,288,320,352,384,416,448,480},{16,48,80,..., dimensions={0} | all-to-all | bytes 1048576 | tf_op jit(solution)/shard_map/all_to_all | solution.py:278
  49.7 5.1 %collective-permute-start.1 = (f32[16,64,128]{2,1,0:T(8,128)S(1)}, f32[16,64,128]{2,1,0:T(8,128)S(1)}, u32[]{:S(2)}, u32[]{:S(2)}) collective-permute-start(f32[16,64,128]{2,1,0:T(8,128)S(1)} %all_to_all.22.mine_ref), channel_id=1, source_target_pairs={{0,16},{16,0},{32,48},{48,32},{64,80},{80,64},{96,112},{112,96},{1... | collective-permute-start | bytes 1572872 | tf_op jit(solution)/shard_map/ppermute | solution.py:315
  54.8 1.5 %collective-permute-done.1.other_ref = f32[16,64,128]{2,1,0:T(8,128)S(1)} collective-permute-done((f32[16,64,128]{2,1,0:T(8,128)S(1)}, f32[16,64,128]{2,1,0:T(8,128)S(1)}, u32[]{:S(2)}, u32[]{:S(2)}) %collective-permute-start.1) | collective-permute-done | bytes 524320 | tf_op jit(solution)/shard_map/ppermute | solution.py:315
  56.3 0.0 copy-done.1
  56.3 0.0 copy-done.2
  56.3 6.0 %shard_map.44 = (f32[1,224,384]{2,1,0:T(8,128)}, bf16[1,224,384]{2,1,0:T(8,128)(2,1)}) custom-call(f32[16,64,128]{2,1,0:T(8,128)S(1)} %all_to_all.22.mine_ref, f32[16,64,128]{2,1,0:T(8,128)S(1)} %collective-permute-done.1.other_ref, bf16[1,224,384]{2,1,0:T(8,128)(2,1)S(1)} %copy-done.1, f32[1,224,384]{2,1,0:T(8,128)S(1)} %copy-done.2), custom_call_target="tpu_custom_call" | custom-call | tf_op jit(solution)/shard_map/pallas_call | solution.py:316
Async XLA Ops:
  0.6 0.9 %copy-start = (bf16[1,224,384]{2,1,0:T(8,128)(2,1)S(1)}, bf16[1,224,384]{2,1,0:T(8,128)(2,1)}, u32[]{:S(2)}) copy-start(bf16[1,224,384]{2,1,0:T(8,128)(2,1)} %grad_ref.5) | copy-start | bytes 516100
  2.3 14.7 %all-to-all-start.1 = ((f32[16,1,128]{2,1,0:T(1,128)}), f32[16,1,128]{2,1,0:T(1,128)S(1)}, u32[]{:S(2)}, u32[]{:S(2)}) async-start(f32[16,1,128]{2,1,0:T(1,128)} %bitcast.1), calls=%async_computation.1 | async-start | bytes 16384 | tf_op jit(solution)/shard_map/all_to_all | solution.py:278
  17.0 20.3 %all-to-all-start = ((f32[32,56,128]{2,1,0:T(8,128)}), f32[32,56,128]{2,1,0:T(8,128)S(1)}, u32[]{:S(2)}, u32[]{:S(2)}) async-start(f32[32,56,128]{2,1,0:T(8,128)} %shard_map.41), calls=%async_computation | async-start | bytes 1835008 | tf_op jit(solution)/shard_map/all_to_all | solution.py:278
  21.3 15.0 %collective-permute-start = (f32[16,128]{1,0:T(8,128)S(1)}, f32[16,128]{1,0:T(8,128)S(1)}, u32[]{:S(2)}, u32[]{:S(2)}) collective-permute-start(f32[16,128]{1,0:T(8,128)S(1)} %bitcast.4), channel_id=1, source_target_pairs={{0,8},{1,9},{2,10},{3,11},{4,12},{5,13},{6,14},{7,15},{8,0},{9,1},... | collective-permute-start | bytes 24584 | tf_op jit(solution)/shard_map/ppermute | solution.py:297
  37.4 18.9 %copy-start.1 = (bf16[1,224,384]{2,1,0:T(8,128)(2,1)S(1)}, bf16[1,224,384]{2,1,0:T(8,128)(2,1)}, u32[]{:S(2)}) copy-start(bf16[1,224,384]{2,1,0:T(8,128)(2,1)} %grad_ref.5) | copy-start | bytes 516100
  37.4 18.9 %copy-start.2 = (f32[1,224,384]{2,1,0:T(8,128)S(1)}, f32[1,224,384]{2,1,0:T(8,128)}, u32[]{:S(2)}) copy-start(f32[1,224,384]{2,1,0:T(8,128)} %momentum_ref.3) | copy-start | bytes 1032196
  49.7 6.6 %collective-permute-start.1 = (f32[16,64,128]{2,1,0:T(8,128)S(1)}, f32[16,64,128]{2,1,0:T(8,128)S(1)}, u32[]{:S(2)}, u32[]{:S(2)}) collective-permute-start(f32[16,64,128]{2,1,0:T(8,128)S(1)} %all_to_all.22.mine_ref), channel_id=1, source_target_pairs={{0,16},{16,0},{32,48},{48,32},{64,80},{80,64},{96,112},{112,96},{1... | collective-permute-start | bytes 1572872 | tf_op jit(solution)/shard_map/ppermute | solution.py:315

commit v11 on v10

--- a/solution.py
+++ b/solution.py
@@ -183,8 +183,9 @@
         c, p = divmod(rest, pieces)
         at = slice(p * SUB, (p + 1) * SUB)
         first, second = (mine_ref, other_ref) if c == 0 else (other_ref, mine_ref)
-        return jnp.where(core == 0, first[chip, at, :], second[chip, at, :])
-
+        return jnp.where(core == 0, first[seat[chip], at, :], second[seat[chip], at, :])
+
+    seat = {chip: n for n, chip in enumerate(middle_first(chips))}
     per_block = LANE // SUB
     blocks = [
         jnp.concatenate([piece(k * per_block + n) for n in range(per_block)], axis=0)
@@ -250,6 +251,10 @@
 HBM = pl.BlockSpec(memory_space=pltpu.HBM)
 
 
+def middle_first(chips):
+    return sorted(range(chips), key=lambda i: abs(i // ROW - 1) + abs(i % ROW - 1))
+
+
 def call(kernel, shapes, **specs):
     return pl.pallas_call(
         kernel,
@@ -272,7 +277,7 @@
     f32 = jnp.float32
     spread = jax.ShapeDtypeStruct((chips, share + SUB, LANE), f32)
     pairs = [(i, i ^ 1) for i in range(fsdp_count)]
-    groups = [[CORES * i + c for i in range(chips)] for c in range(CORES)]
+    groups = [[CORES * i + c for i in middle_first(chips)] for c in range(CORES)]
 
     def exchange(x, members=None):
         return lax.all_to_all(x, "fsdp", split_axis=0, concat_axis=0, tiled=True, axis_index_groups=members)

time: 62.7 us -> 62.4 us (level)
  starting transfers between devices: 30.9 us -> 29.8 us
  blocking collectives: 12.3 us -> 13.1 us
    ppermute x1, starting transfers between devices: 5.06 us -> 3.94 us  [per_device(): other = lax.ppermute(mine, 'fsdp', pairs)]
    all_to_all x1, blocking collectives: 12.3 us -> 13.1 us  [exchange(): lax.all_to_all(x, 'fsdp', split_axis=0, concat_axis=0, tiled=True, axis_i...]
where the time goes in v11:
time: 62.4 us; the launch traced here: 62 us
  starting transfers between devices  29.8 us (48%)
  blocking collectives  13.1 us (21%)
  Pallas kernels  9.9 us (16%)
  waiting for transfers between devices  7.58 us (12%)
  local copies, waits for them, and re-layouts  0.93 us (1%)
  between operations  0.7 us (1%)
    all_to_all x2, starting transfers between devices, exchange(): lax.all_to_all(x, 'fsdp', split_axis=0, concat_axis=0, tiled=True, axis_i...  14.1 us
    all_to_all x1, blocking collectives, exchange(): lax.all_to_all(x, 'fsdp', split_axis=0, concat_axis=0, tiled=True, axis_i...  13.1 us
    ppermute x1, starting transfers between devices, per_device(): planes = lax.ppermute(exchange(square, halves), ('fsdp', 'expert'), turns)  11.8 us
    pallas_call x1, Pallas kernels, per_device(): call(functools.partial(final_kernel, step_scale, count), (jax.ShapeDtypeS...  5.97 us
    ppermute x1, starting transfers between devices, per_device(): other = lax.ppermute(mine, 'fsdp', pairs)  3.94 us
    ppermute x1, waiting for transfers between devices, per_device(): planes = lax.ppermute(exchange(square, halves), ('fsdp', 'expert'), turns)  3.21 us
    pallas_call x1, Pallas kernels, per_device(): pl.pallas_call(gram_kernel, out_shape=parts, in_specs=[HBM, HBM], out_spe...  3.13 us
    all_to_all x2, waiting for transfers between devices, exchange(): lax.all_to_all(x, 'fsdp', split_axis=0, concat_axis=0, tiled=True, axis_i...  2.86 us
  transfers between devices with their start and end apart: 4, of which 4 were waited for; matrix products, arithmetic and copies ran while one was open for 0% of the time, Pallas kernels for 5%

profile of v11, /device:TPU:1, one launch (start us, length us, event | category | flops | bytes accessed | tf_op | source)
XLA Modules:
  0.0 62.0 jit_solution(10483661514846779258)
XLA Ops:
  0.6 0.0 copy-start
  0.6 0.9 %copy-done = bf16[1,224,384]{2,1,0:T(8,128)(2,1)S(1)} copy-done((bf16[1,224,384]{2,1,0:T(8,128)(2,1)S(1)}, bf16[1,224,384]{2,1,0:T(8,128)(2,1)}, u32[]{:S(2)}) %copy-start) | copy-done | bytes 172056
  1.6 0.7 %shard_map.42 = f32[16,128]{1,0:T(8,128)} custom-call(bf16[1,224,384]{2,1,0:T(8,128)(2,1)S(1)} %copy-done), custom_call_target="tpu_custom_call" | custom-call | tf_op jit(solution)/shard_map/pallas_call | solution.py:301
  2.3 9.8 %all-to-all-start.1 = ((f32[16,1,128]{2,1,0:T(1,128)}), f32[16,1,128]{2,1,0:T(1,128)S(1)}, u32[]{:S(2)}, u32[]{:S(2)}) async-start(f32[16,1,128]{2,1,0:T(1,128)} %bitcast.1), calls=%async_computation.1 | async-start | bytes 16384 | tf_op jit(solution)/shard_map/all_to_all | solution.py:283
  12.1 3.1 %shard_map.41 = f32[32,56,128]{2,1,0:T(8,128)} custom-call(bf16[1,224,384]{2,1,0:T(8,128)(2,1)} %grad_ref.5, f32[1,224,384]{2,1,0:T(8,128)} %momentum_ref.3), custom_call_target="tpu_custom_call" | custom-call | tf_op jit(solution)/shard_map/pallas_call | solution.py:304
  15.2 1.8 %all-to-all-done.1 = f32[16,1,128]{2,1,0:T(1,128)S(1)} async-done(((f32[16,1,128]{2,1,0:T(1,128)}), f32[16,1,128]{2,1,0:T(1,128)S(1)}, u32[]{:S(2)}, u32[]{:S(2)}) %all-to-all-start.1) | async-done | bytes 8224 | tf_op jit(solution)/shard_map/all_to_all | solution.py:283
  17.0 4.3 %all-to-all-start = ((f32[32,56,128]{2,1,0:T(8,128)}), f32[32,56,128]{2,1,0:T(8,128)S(1)}, u32[]{:S(2)}, u32[]{:S(2)}) async-start(f32[32,56,128]{2,1,0:T(8,128)} %shard_map.41), calls=%async_computation | async-start | bytes 1835008 | tf_op jit(solution)/shard_map/all_to_all | solution.py:283
  21.3 11.8 %collective-permute-start = (f32[16,128]{1,0:T(8,128)S(1)}, f32[16,128]{1,0:T(8,128)S(1)}, u32[]{:S(2)}, u32[]{:S(2)}) collective-permute-start(f32[16,128]{1,0:T(8,128)S(1)} %bitcast.4), channel_id=1, source_target_pairs={{0,8},{1,9},{2,10},{3,11},{4,12},{5,13},{6,14},{7,15},{8,0},{9,1},... | collective-permute-start | bytes 24584 | tf_op jit(solution)/shard_map/ppermute | solution.py:302
  33.0 3.2 %collective-permute-done.squares_ref = f32[16,128]{1,0:T(8,128)S(1)} collective-permute-done((f32[16,128]{1,0:T(8,128)S(1)}, f32[16,128]{1,0:T(8,128)S(1)}, u32[]{:S(2)}, u32[]{:S(2)}) %collective-permute-start) | collective-permute-done | bytes 8224 | tf_op jit(solution)/shard_map/ppermute | solution.py:302
  36.2 1.1 %all-to-all-done.parts_ref = f32[32,56,128]{2,1,0:T(8,128)S(1)} async-done(((f32[32,56,128]{2,1,0:T(8,128)}), f32[32,56,128]{2,1,0:T(8,128)S(1)}, u32[]{:S(2)}, u32[]{:S(2)}) %all-to-all-start) | async-done | bytes 917536 | tf_op jit(solution)/shard_map/all_to_all | solution.py:283
  37.3 0.1 shard_map.43
  37.4 0.0 copy-start.1
  37.4 0.0 copy-start.2
  37.5 13.1 %all_to_all.22.mine_ref = f32[16,64,128]{2,1,0:T(8,128)S(1)} all-to-all(f32[16,64,128]{2,1,0:T(8,128)S(1)} %shard_map.43), channel_id=1, replica_groups={{160,32,128,192,288,0,64,224,256,320,416,96,352,384,448,480},{176,48,14..., dimensions={0} | all-to-all | bytes 1048576 | tf_op jit(solution)/shard_map/all_to_all | solution.py:283
  50.6 3.9 %collective-permute-start.1 = (f32[16,64,128]{2,1,0:T(8,128)S(1)}, f32[16,64,128]{2,1,0:T(8,128)S(1)}, u32[]{:S(2)}, u32[]{:S(2)}) collective-permute-start(f32[16,64,128]{2,1,0:T(8,128)S(1)} %all_to_all.22.mine_ref), channel_id=1, source_target_pairs={{0,16},{16,0},{32,48},{48,32},{64,80},{80,64},{96,112},{112,96},{1... | collective-permute-start | bytes 1572872 | tf_op jit(solution)/shard_map/ppermute | solution.py:320
  54.5 1.5 %collective-permute-done.1.other_ref = f32[16,64,128]{2,1,0:T(8,128)S(1)} collective-permute-done((f32[16,64,128]{2,1,0:T(8,128)S(1)}, f32[16,64,128]{2,1,0:T(8,128)S(1)}, u32[]{:S(2)}, u32[]{:S(2)}) %collective-permute-start.1) | collective-permute-done | bytes 524320 | tf_op jit(solution)/shard_map/ppermute | solution.py:320
  56.1 0.0 copy-done.1
  56.1 0.0 copy-done.2
  56.1 6.0 %shard_map.44 = (f32[1,224,384]{2,1,0:T(8,128)}, bf16[1,224,384]{2,1,0:T(8,128)(2,1)}) custom-call(f32[16,64,128]{2,1,0:T(8,128)S(1)} %all_to_all.22.mine_ref, f32[16,64,128]{2,1,0:T(8,128)S(1)} %collective-permute-done.1.other_ref, bf16[1,224,384]{2,1,0:T(8,128)(2,1)S(1)} %copy-done.1, f32[1,224,384]{2,1,0:T(8,128)S(1)} %copy-done.2), custom_call_target="tpu_custom_call" | custom-call | tf_op jit(solution)/shard_map/pallas_call | solution.py:321
Async XLA Ops:
  0.6 0.9 %copy-start = (bf16[1,224,384]{2,1,0:T(8,128)(2,1)S(1)}, bf16[1,224,384]{2,1,0:T(8,128)(2,1)}, u32[]{:S(2)}) copy-start(bf16[1,224,384]{2,1,0:T(8,128)(2,1)} %grad_ref.5) | copy-start | bytes 516100
  2.3 14.7 %all-to-all-start.1 = ((f32[16,1,128]{2,1,0:T(1,128)}), f32[16,1,128]{2,1,0:T(1,128)S(1)}, u32[]{:S(2)}, u32[]{:S(2)}) async-start(f32[16,1,128]{2,1,0:T(1,128)} %bitcast.1), calls=%async_computation.1 | async-start | bytes 16384 | tf_op jit(solution)/shard_map/all_to_all | solution.py:283
  17.0 20.3 %all-to-all-start = ((f32[32,56,128]{2,1,0:T(8,128)}), f32[32,56,128]{2,1,0:T(8,128)S(1)}, u32[]{:S(2)}, u32[]{:S(2)}) async-start(f32[32,56,128]{2,1,0:T(8,128)} %shard_map.41), calls=%async_computation | async-start | bytes 1835008 | tf_op jit(solution)/shard_map/all_to_all | solution.py:283
  21.3 15.0 %collective-permute-start = (f32[16,128]{1,0:T(8,128)S(1)}, f32[16,128]{1,0:T(8,128)S(1)}, u32[]{:S(2)}, u32[]{:S(2)}) collective-permute-start(f32[16,128]{1,0:T(8,128)S(1)} %bitcast.4), channel_id=1, source_target_pairs={{0,8},{1,9},{2,10},{3,11},{4,12},{5,13},{6,14},{7,15},{8,0},{9,1},... | collective-permute-start | bytes 24584 | tf_op jit(solution)/shard_map/ppermute | solution.py:302
  37.4 18.6 %copy-start.1 = (bf16[1,224,384]{2,1,0:T(8,128)(2,1)S(1)}, bf16[1,224,384]{2,1,0:T(8,128)(2,1)}, u32[]{:S(2)}) copy-start(bf16[1,224,384]{2,1,0:T(8,128)(2,1)} %grad_ref.5) | copy-start | bytes 516100
  37.4 18.6 %copy-start.2 = (f32[1,224,384]{2,1,0:T(8,128)S(1)}, f32[1,224,384]{2,1,0:T(8,128)}, u32[]{:S(2)}) copy-start(f32[1,224,384]{2,1,0:T(8,128)} %momentum_ref.3) | copy-start | bytes 1032196
  50.6 5.5 %collective-permute-start.1 = (f32[16,64,128]{2,1,0:T(8,128)S(1)}, f32[16,64,128]{2,1,0:T(8,128)S(1)}, u32[]{:S(2)}, u32[]{:S(2)}) collective-permute-start(f32[16,64,128]{2,1,0:T(8,128)S(1)} %all_to_all.22.mine_ref), channel_id=1, source_target_pairs={{0,16},{16,0},{32,48},{48,32},{64,80},{80,64},{96,112},{112,96},{1... | collective-permute-start | bytes 1572872 | tf_op jit(solution)/shard_map/ppermute | solution.py:320
